TPU v7x, 512 devices: a whole 4x8x8 slice. The times are simulated.
512 devices in a mesh: band: 4 (over x), dx: 8 (over y), dyz: 16 (over z, core).
Axes of the slice: x: 4, y: 8, z: 8, core: 2. Of those that a mesh axis runs over, the one named last changes fastest.
Arguments:
- density: float32 [256, 384, 512], P('dx', 'dyz', 'band'), may hold values from 0.1 to 3
- hartree: float32 [256, 384, 512], P('dx', 'dyz', 'band'), may hold values from -6 to 6
- box_root: int32 [3, 8192], P(None, ('dx', 'dyz')), may hold values from 0 to 511, as said below
- species: int32 [8192], P(('dx', 'dyz')), may hold values from 0 to 1
- atom_count: int32 [128], P(('dx', 'dyz')), may hold values from 1 to 64, 4096 in all
- shape_functions: float32 [2, 25, 4096], replicated, may hold values from -28 to 28
- coupling: float32 [2, 25, 256], replicated, may hold values from -1.25 to 1.25
- coulomb: float32 [2, 256, 256], replicated, may hold values from -0.375 to 0.375
- rho_ij: float32 [8192, 256], P(('dx', 'dyz')), may hold values from -6 to 6
- projections: float32 [8192, 16, 512], P(('dx', 'dyz'), None, 'band'), may hold values from -6 to 6
Outputs:
- potential: float32 [256, 384, 512], P('dx', 'dyz', 'band')
- atom_hamiltonian: float32 [8192, 256], P(('dx', 'dyz'))
- applied: float32 [8192, 16, 512], P(('dx', 'dyz'), None, 'band')
Inputs may be any that keep to these rules, and one draw needn't show every extreme that they name: Atom a's first two box_root entries lie within the first- and second-dimension cells held by the devices that hold atom a; the third is any cell of the third dimension. Domain column c holds its atoms in slots c * 64 to c * 64 + atom_count[c] - 1; its other slots are empty.
All inputs are finite; a program needn't handle non-finite values. No bound on the sum of `atom_count` on one device may be relied on, other than what follows from the above.
Results may differ from a plain program's by a relative error of at most 0.0003.
Values sent between devices are 32-bit elements; how exact they have to be, the bound alone decides.
No kernel may reach another device: no remote copies, remote signals or barrier semaphores. Data moves between devices by JAX's collectives and lax.ppermute only.
A program may use at most 64 MiB of HBM per device.

v0:
```python
import jax
import jax.numpy as jnp
from jax import lax
from jax.sharding import PartitionSpec as P

BOX = 16
NI = 16


GRID_H = 0.15
KAPPA = 0.804
MU_COEF = 0.2195149727645171
PRECISE = lax.Precision.HIGHEST


def padded_2(array, sides, width):
    for axis, dim in sides:
        devices, length = (lax.axis_size(axis), array.shape[dim])
        up = [(i, (i + 1) % devices) for i in range(devices)]
        down = [(j, i) for i, j in up]
        last = lax.slice_in_dim(array, length - width, length, axis=dim)
        leading = lax.slice_in_dim(array, 0, width, axis=dim)
        before = lax.ppermute(last, axis, up)
        after = lax.ppermute(leading, axis, down)
        array = jnp.concatenate([before, array, after], axis=dim)
    return array


def passed_along(block, axis, distance):
    devices = range(lax.axis_size(axis))
    route = [((i - distance) % len(devices), i) for i in devices]
    return lax.ppermute(block, axis, route)


def exchange_energy(dens, sigma):
    prefactor = -0.75 * (3.0 / jnp.pi) ** (1.0 / 3.0)
    reduced = sigma / (4.0 * (3.0 * jnp.pi**2) ** (2.0 / 3.0) * dens ** (8.0 / 3.0))
    enhance = 1.0 + KAPPA - KAPPA / (1.0 + MU_COEF * reduced / KAPPA)
    return prefactor * dens ** (4.0 / 3.0) * enhance


def energy_slopes(dens, sigma):

    def summed(dens_in, sigma_in):
        return jnp.sum(exchange_energy(dens_in, sigma_in))

    return jax.grad(summed, argnums=(0, 1))(dens, sigma)


def gradients(padded):
    half_step = 0.5 / GRID_H
    inner = padded[1:-1, 1:-1, 1:-1]
    grad_x = (padded[2:, 1:-1, 1:-1] - padded[:-2, 1:-1, 1:-1]) * half_step
    grad_y = (padded[1:-1, 2:, 1:-1] - padded[1:-1, :-2, 1:-1]) * half_step
    grad_z = (padded[1:-1, 1:-1, 2:] - padded[1:-1, 1:-1, :-2]) * half_step
    return (inner, grad_x, grad_y, grad_z)


def divergence(flux_x, flux_y, flux_z):
    half_step = 0.5 / GRID_H
    part_x = (flux_x[2:, 1:-1, 1:-1] - flux_x[:-2, 1:-1, 1:-1]) * half_step
    part_y = (flux_y[1:-1, 2:, 1:-1] - flux_y[1:-1, :-2, 1:-1]) * half_step
    part_z = (flux_z[1:-1, 1:-1, 2:] - flux_z[1:-1, 1:-1, :-2]) * half_step
    return part_x + part_y + part_z


def hamiltonian_blocks(moments, rho_rows, picks, live, coupling, coulomb):
    summed = jnp.zeros((moments.shape[0], coulomb.shape[2]), jnp.float32)
    for spec_id in range(coupling.shape[0]):
        term = jnp.dot(moments, coupling[spec_id], precision=PRECISE) + 2.0 * jnp.dot(
            rho_rows, coulomb[spec_id], precision=PRECISE
        )
        summed = summed + picks[:, spec_id : spec_id + 1] * term
    return jnp.where(live[:, None], summed, 0.0)


def fold_moments(source, plan, shape_functions, z_cells, depth_all):
    width_x, width_y, depth = source.shape
    box_steps = jnp.arange(BOX, dtype=jnp.int32)
    spec_count = shape_functions.shape[0]
    comp_count = shape_functions.shape[1]
    shaped = shape_functions.reshape(spec_count * comp_count, BOX, BOX, BOX)
    flat_source = source.reshape(width_x * width_y, depth)
    cells_x = jnp.arange(width_x, dtype=jnp.int32)
    cells_y = jnp.arange(width_y, dtype=jnp.int32)
    slots = plan.shape[1]
    group = 16
    turns = slots // group

    def block_moments(block_plan):
        offset = (z_cells[None, :] - block_plan[2][:, None]) % depth_all
        select_z = (offset[:, None, :] == box_steps[None, :, None]).astype(jnp.float32)
        select_z = select_z.reshape(group * BOX, depth)
        along_z = lax.dot_general(
            flat_source, select_z, (((1,), (1,)), ((), ())), precision=PRECISE
        )
        along_z = along_z.reshape(width_x, width_y, group, BOX)
        select_y = (
            cells_y[None, None, :] - block_plan[1][:, None, None] == box_steps[None, :, None]
        ).astype(jnp.float32)
        along_y = jnp.einsum("xyak,ajy->xjak", along_z, select_y, precision=PRECISE)
        select_x = (
            cells_x[None, None, :] - block_plan[0][:, None, None] == box_steps[None, :, None]
        ).astype(jnp.float32)
        select_x = select_x * block_plan[3][:, None, None].astype(jnp.float32)
        along_x = jnp.einsum("xjak,aix->ijak", along_y, select_x, precision=PRECISE)
        return jnp.einsum("sijk,ijak->as", shaped, along_x, precision=PRECISE)

    blocks_in = plan.reshape(5, turns, group).transpose(1, 0, 2)
    every = lax.map(block_moments, blocks_in)
    every = every.reshape(slots, spec_count, comp_count)
    picks = (plan[4][:, None] == jnp.arange(spec_count, dtype=jnp.int32)[None, :]).astype(
        jnp.float32
    )
    return jnp.sum(every * picks[:, :, None], axis=1) * GRID_H**3


def local(
    density,
    hartree,
    box_root,
    species,
    atom_count,
    shape_functions,
    coupling,
    coulomb,
    rho_ij,
    projections,
):
    padded = padded_2(density, (("dx", 0), ("dyz", 1), ("band", 2)), 1)
    inner, grad_x, grad_y, grad_z = gradients(padded)
    sigma = grad_x * grad_x + grad_y * grad_y + grad_z * grad_z
    slope_n, slope_s = energy_slopes(inner, sigma)
    fluxes = jnp.stack([slope_s * grad_x, slope_s * grad_y, slope_s * grad_z])
    flux_pad = padded_2(fluxes, (("dx", 1), ("dyz", 2), ("band", 3)), 1)
    spread = divergence(flux_pad[0], flux_pad[1], flux_pad[2])
    potential = hartree + slope_n - 2.0 * spread
    width_x, width_y, depth = potential.shape
    first_x = lax.axis_index("dx") * width_x
    first_y = lax.axis_index("dyz") * width_y
    depth_all = depth * lax.axis_size("band")
    z_cells = lax.axis_index("band") * depth + jnp.arange(depth, dtype=jnp.int32)
    atom_slots = box_root.shape[1]
    rim_first = passed_along(potential[:BOX], "dx", -1)
    widened = jnp.concatenate([potential, rim_first], 0)
    rim_second = passed_along(widened[:, :BOX], "dyz", -1)
    widened = jnp.concatenate([widened, rim_second], 1)
    ones = jnp.ones((atom_slots,), jnp.int32)
    plan = jnp.stack([box_root[0] - first_x, box_root[1] - first_y, box_root[2], ones, species])
    partial_value = fold_moments(widened, plan, shape_functions, z_cells, depth_all)
    spec_count = shape_functions.shape[0]
    picks = (species[:, None] == jnp.arange(spec_count, dtype=jnp.int32)[None, :]).astype(
        jnp.float32
    )
    live = jnp.arange(atom_slots, dtype=jnp.int32) < atom_count[0]
    moments = lax.psum(partial_value, "band")
    atom_hamiltonian = hamiltonian_blocks(moments, rho_ij, picks, live, coupling, coulomb)
    blocks = atom_hamiltonian.reshape(atom_slots, NI, NI)
    applied = jnp.einsum("aij,ajn->ain", blocks, projections, precision=PRECISE)
    return (potential, atom_hamiltonian, applied)


def solution(mesh):
    in_specs = (
        P("dx", "dyz", "band"),
        P("dx", "dyz", "band"),
        P(None, ("dx", "dyz")),
        P(("dx", "dyz")),
        P(("dx", "dyz")),
        P(),
        P(),
        P(),
        P(("dx", "dyz"), None),
        P(("dx", "dyz"), None, "band"),
    )
    out_specs = (P("dx", "dyz", "band"), P(("dx", "dyz"), None), P(("dx", "dyz"), None, "band"))
    return jax.shard_map(local, mesh=mesh, in_specs=in_specs, out_specs=out_specs, check_vma=False)
```

profile of v0, /device:TPU:56, one launch (start us, length us, event | category | flops | bytes accessed | tf_op | source)
XLA Modules:
  0.0 280.3 jit_solution(11129144492574158440)
XLA Ops:
  1.4 7.0 %collective-permute-start.1 = (f32[1,24,128]{2,1,0:T(8,128)S(1)}, f32[1,24,128]{2,1,0:T(8,128)S(1)}, u32[]{:S(2)}, u32[]{:S(2)}) collective-permute-start(f32[1,24,128]{2,1,0:T(8,128)S(1)} %get-tuple-element.230), channel_id=1, source_target_pairs={{0,16},{16,32},{32,48},{48,64},{64,80},{80,96},{96,112},{112,0},{1... | collective-permute-start | bytes 36872 | tf_op jit(solution)/shard_map/ppermute | solution.py:23
  8.5 1.9 collective-permute-start
  15.3 3.8 %collective-permute-start.2 = (f32[34,1,128]{2,1,0:T(1,128)S(1)}, f32[34,1,128]{2,1,0:T(1,128)S(1)}, u32[]{:S(2)}, u32[]{:S(2)}) collective-permute-start(f32[34,1,128]{2,1,0:T(1,128)S(1)} %get-tuple-element.225), channel_id=1, source_target_pairs={{1,0},{2,1},{3,2},{4,3},{5,4},{6,5},{7,6},{8,7},{9,8},{10,9},{11,1... | collective-permute-start | bytes 52232 | tf_op jit(solution)/shard_map/ppermute | solution.py:24
  20.6 2.9 %collective-permute-done.3 = f32[34,1,128]{2,1,0:T(1,128)S(1)} collective-permute-done((f32[34,1,128]{2,1,0:T(1,128)S(1)}, f32[34,1,128]{2,1,0:T(1,128)S(1)}, u32[]{:S(2)}, u32[]{:S(2)}) %collective-permute-start.3) | collective-permute-done | bytes 17440 | tf_op jit(solution)/shard_map/ppermute | solution.py:23
  24.2 4.7 %collective-permute-start.4 = (f32[34,26,1]{0,2,1:T(1,128)S(1)}, f32[34,26,1]{0,2,1:T(1,128)S(1)}, u32[]{:S(2)}, u32[]{:S(2)}) collective-permute-start(f32[34,26,1]{0,2,1:T(1,128)S(1)} %copy.47), channel_id=1, source_target_pairs={{128,0},{256,128},{384,256},{0,384},{129,1},{257,129},{385,257},{1... | collective-permute-start | bytes 10616 | tf_op jit(solution)/shard_map/ppermute | solution.py:24
  29.2 1.9 collective-permute-start.5
  31.9 4.2 %collective-permute-done.5 = f32[34,26,1]{0,2,1:T(1,128)S(1)} collective-permute-done((f32[34,26,1]{0,2,1:T(1,128)S(1)}, f32[34,26,1]{0,2,1:T(1,128)S(1)}, u32[]{:S(2)}, u32[]{:S(2)}) %collective-permute-start.5) | collective-permute-done | bytes 3568 | tf_op jit(solution)/shard_map/ppermute | solution.py:23
  37.4 2.2 multiply_bitcast_fusion.2
  39.8 3.4 %collective-permute-start.6 = (f32[3,1,24,128]{3,2,1,0:T(8,128)S(1)}, f32[3,1,24,128]{3,2,1,0:T(8,128)S(1)}, u32[]{:S(2)}, u32[]{:S(2)}) collective-permute-start(f32[3,1,24,128]{3,2,1,0:T(8,128)S(1)} %get-tuple-element.221), channel_id=1, source_target_pairs={{0,16},{16,32},{32,48},{48,64},{64,80},{80,96},{96,112},{112,0},{1... | collective-permute-start | bytes 110600 | tf_op jit(solution)/shard_map/ppermute | solution.py:23
  43.2 2.4 collective-permute-start.7
  45.8 4.5 %collective-permute-done.7 = f32[3,1,24,128]{3,2,1,0:T(8,128)S(1)} collective-permute-done((f32[3,1,24,128]{3,2,1,0:T(8,128)S(1)}, f32[3,1,24,128]{3,2,1,0:T(8,128)S(1)}, u32[]{:S(2)}, u32[]{:S(2)}) %collective-permute-start.7) | collective-permute-done | bytes 36896 | tf_op jit(solution)/shard_map/ppermute | solution.py:24
  50.4 2.9 %collective-permute-start.9 = (f32[3,34,1,128]{3,2,1,0:T(1,128)S(1)}, f32[3,34,1,128]{3,2,1,0:T(1,128)S(1)}, u32[]{:S(2)}, u32[]{:S(2)}) collective-permute-start(f32[3,34,1,128]{3,2,1,0:T(1,128)S(1)} %get-tuple-element.220), channel_id=1, source_target_pairs={{1,0},{2,1},{3,2},{4,3},{5,4},{6,5},{7,6},{8,7},{9,8},{10,9},{11,1... | collective-permute-start | bytes 156680 | tf_op jit(solution)/shard_map/ppermute | solution.py:24
  53.4 1.8 collective-permute-done.8
  55.4 2.3 fusion.58
  57.7 2.2 copy.51
  60.0 1.9 collective-permute-start.10
  61.9 2.2 copy.52
  64.1 5.3 %collective-permute-start.11 = (f32[3,34,26,1]{1,3,2,0:T(1,128)S(1)}, f32[3,34,26,1]{1,3,2,0:T(1,128)S(1)}, u32[]{:S(2)}, u32[]{:S(2)}) collective-permute-start(f32[3,34,26,1]{1,3,2,0:T(1,128)S(1)} %copy.52), channel_id=1, source_target_pairs={{128,0},{256,128},{384,256},{0,384},{129,1},{257,129},{385,257},{1... | collective-permute-start | bytes 31832 | tf_op jit(solution)/shard_map/ppermute | solution.py:24
  70.1 2.6 copy.53
  72.7 2.6 copy.54
  75.3 5.4 %pad_maximum_fusion = f32[3,34,26,130]{3,2,1,0:T(8,128)S(1)} fusion(f32[3,34,26,1]{3,2,1,0:T(8,128)} %copy.54, f32[3,34,1,128]{3,2,1,0:T(1,128)S(1)} %collective-permute-done.9, f32[3,1,24,128]{3,2,1,0:T(8,128)S(1)} %collective-permute-done.7, f32[1,32,24,128]{3,2,1,0:T(8,128)S(1)} %get-tuple-element.228, f32[1,32,24,128]{3,2,1,0:T(8,128)S(1)} %get-tuple-element.227, ...), kind=kLoop, calls=%fused_computation.43 | loop fusion | flops 2758080 | bytes 2758080 | tf_op jit(solution)/shard_map/concatenate | solution.py:25
  81.9 1.6 fusion.43
  83.5 1.9 collective-permute-start.12
  85.5 6.8 %collective-permute-done.12 = f32[16,24,128]{2,1,0:T(8,128)S(1)} collective-permute-done((f32[16,24,128]{2,1,0:T(8,128)S(1)}, f32[16,24,128]{2,1,0:T(8,128)S(1)}, u32[]{:S(2)}, u32[]{:S(2)}) %collective-permute-start.12) | collective-permute-done | bytes 196640 | tf_op jit(solution)/shard_map/ppermute | solution.py:32
  93.8 5.8 %copy.55 = f32[2,25,4096]{1,0,2:T(2,128)} copy(f32[2,25,4096]{2,0,1:T(2,128)} %param.17) | data formatting | bytes 1638400 | tf_op args[5]
  99.6 5.5 %reshape.189 = f32[50,16,16,16]{0,3,2,1:T(8,128)} reshape(f32[2,25,4096]{1,0,2:T(2,128)} %copy.55) | data formatting | bytes 1638400 | tf_op jit(solution)/shard_map/reshape | solution.py:82
  106.5 155.5 %while.14 = (s32[]{:T(128)}, f32[4,16,50]{2,1,0:T(8,128)S(1)}, s32[4,5,16]{2,0,1:T(4,128)S(1)}, f32[1920,128]{1,0:T(8,128)}, f32[50,16,16,16]{0,3,2,1:T(8,128)},...) while((s32[]{:T(128)}, f32[4,16,50]{2,1,0:T(8,128)S(1)}, ...), condition=%wide.region_1.2_spmd.clone.clone, body=%wide.region_0.1_spmd.clone.clone.sunk | while | flops 926510592 | bytes 18260932 | solution.py:110
  106.8 2.2 convolution_bitcast_fusion.4
  109.0 6.0 %reshape.215 = f32[48,40,16,16]{1,0,3,2:T(8,128)} reshape(f32[1920,256]{0,1:T(8,128)S(1)} %convolution_bitcast_fusion.4) | data formatting | bytes 3932160 | tf_op jit(solution)/shard_map/while/body/eval_jaxpr/reshape | solution.py:97
  115.1 11.1 %convolution_bitcast_fusion.5 = f32[48,16,16,16]{0,1,3,2:T(8,128)S(1)} fusion(f32[48,40,16,16]{1,0,3,2:T(8,128)} %reshape.215, s32[16,40]{1,0:T(8,128)S(1)} %iota_subtract_fusion.4), kind=kOutput, calls=%fused_computation.10.clone.1 | convolution fusion | flops 94382080 | bytes 2755072 | tf_op jit(solution)/shard_map/while/body/eval_jaxpr/xyak,ajy->xjak/dot_general | solution.py:101
  126.2 14.7 %fusion.94 = f32[16,16,16,16]{3,0,1,2:T(8,128)S(1)} fusion(f32[48,16,16,16]{0,1,3,2:T(8,128)S(1)} %convolution_bitcast_fusion.5, f32[16]{0:T(128)S(1)} %get-tuple-element.278, s32[16,48]{1,0:T(8,128)S(1)} %iota_subtract_fusion.5), kind=kOutput, calls=%fused_computation.9.clone.1 | convolution fusion | flops 37773312 | bytes 1051712 | tf_op jit(solution)/shard_map/while/body/eval_jaxpr/xjak,aix->ijak/dot_general | solution.py:106
  141.0 4.4 %fusion.95 = f32[4,16,50]{2,1,0:T(8,128)S(1)} fusion(f32[4,16,50]{2,1,0:T(8,128)S(1)} %get-tuple-element.292, s32[]{:T(128)} %get-tuple-element.291, f32[50,16,16,16]{0,3,2,1:T(8,128)S(1)} %copy-done.1, f32[16,16,16,16]{3,0,1,2:T(8,128)S(1)} %fusion.94), kind=kOutput, calls=%fused_computation.12.clone.1 | convolution fusion | flops 39321600 | bytes 4202500 | tf_op jit(solution)/shard_map/while/body/eval_jaxpr/sijk,ijak->as/dot_general | solution.py:107
  145.7 2.2 convolution_bitcast_fusion.4
  147.9 6.0 %reshape.215 = f32[48,40,16,16]{1,0,3,2:T(8,128)} reshape(f32[1920,256]{0,1:T(8,128)S(1)} %convolution_bitcast_fusion.4) | data formatting | bytes 3932160 | tf_op jit(solution)/shard_map/while/body/eval_jaxpr/reshape | solution.py:97
  154.0 11.1 %convolution_bitcast_fusion.5 = f32[48,16,16,16]{0,1,3,2:T(8,128)S(1)} fusion(f32[48,40,16,16]{1,0,3,2:T(8,128)} %reshape.215, s32[16,40]{1,0:T(8,128)S(1)} %iota_subtract_fusion.4), kind=kOutput, calls=%fused_computation.10.clone.1 | convolution fusion | flops 94382080 | bytes 2755072 | tf_op jit(solution)/shard_map/while/body/eval_jaxpr/xyak,ajy->xjak/dot_general | solution.py:101
  165.1 14.7 %fusion.94 = f32[16,16,16,16]{3,0,1,2:T(8,128)S(1)} fusion(f32[48,16,16,16]{0,1,3,2:T(8,128)S(1)} %convolution_bitcast_fusion.5, f32[16]{0:T(128)S(1)} %get-tuple-element.278, s32[16,48]{1,0:T(8,128)S(1)} %iota_subtract_fusion.5), kind=kOutput, calls=%fused_computation.9.clone.1 | convolution fusion | flops 37773312 | bytes 1051712 | tf_op jit(solution)/shard_map/while/body/eval_jaxpr/xjak,aix->ijak/dot_general | solution.py:106
  179.8 4.4 %fusion.95 = f32[4,16,50]{2,1,0:T(8,128)S(1)} fusion(f32[4,16,50]{2,1,0:T(8,128)S(1)} %get-tuple-element.292, s32[]{:T(128)} %get-tuple-element.291, f32[50,16,16,16]{0,3,2,1:T(8,128)S(1)} %copy-done.1, f32[16,16,16,16]{3,0,1,2:T(8,128)S(1)} %fusion.94), kind=kOutput, calls=%fused_computation.12.clone.1 | convolution fusion | flops 39321600 | bytes 4202500 | tf_op jit(solution)/shard_map/while/body/eval_jaxpr/sijk,ijak->as/dot_general | solution.py:107
  184.6 2.2 convolution_bitcast_fusion.4
  186.8 6.0 %reshape.215 = f32[48,40,16,16]{1,0,3,2:T(8,128)} reshape(f32[1920,256]{0,1:T(8,128)S(1)} %convolution_bitcast_fusion.4) | data formatting | bytes 3932160 | tf_op jit(solution)/shard_map/while/body/eval_jaxpr/reshape | solution.py:97
  192.9 11.1 %convolution_bitcast_fusion.5 = f32[48,16,16,16]{0,1,3,2:T(8,128)S(1)} fusion(f32[48,40,16,16]{1,0,3,2:T(8,128)} %reshape.215, s32[16,40]{1,0:T(8,128)S(1)} %iota_subtract_fusion.4), kind=kOutput, calls=%fused_computation.10.clone.1 | convolution fusion | flops 94382080 | bytes 2755072 | tf_op jit(solution)/shard_map/while/body/eval_jaxpr/xyak,ajy->xjak/dot_general | solution.py:101
  204.0 14.7 %fusion.94 = f32[16,16,16,16]{3,0,1,2:T(8,128)S(1)} fusion(f32[48,16,16,16]{0,1,3,2:T(8,128)S(1)} %convolution_bitcast_fusion.5, f32[16]{0:T(128)S(1)} %get-tuple-element.278, s32[16,48]{1,0:T(8,128)S(1)} %iota_subtract_fusion.5), kind=kOutput, calls=%fused_computation.9.clone.1 | convolution fusion | flops 37773312 | bytes 1051712 | tf_op jit(solution)/shard_map/while/body/eval_jaxpr/xjak,aix->ijak/dot_general | solution.py:106
  218.7 4.4 %fusion.95 = f32[4,16,50]{2,1,0:T(8,128)S(1)} fusion(f32[4,16,50]{2,1,0:T(8,128)S(1)} %get-tuple-element.292, s32[]{:T(128)} %get-tuple-element.291, f32[50,16,16,16]{0,3,2,1:T(8,128)S(1)} %copy-done.1, f32[16,16,16,16]{3,0,1,2:T(8,128)S(1)} %fusion.94), kind=kOutput, calls=%fused_computation.12.clone.1 | convolution fusion | flops 39321600 | bytes 4202500 | tf_op jit(solution)/shard_map/while/body/eval_jaxpr/sijk,ijak->as/dot_general | solution.py:107
  223.5 2.2 convolution_bitcast_fusion.4
  225.6 6.0 %reshape.215 = f32[48,40,16,16]{1,0,3,2:T(8,128)} reshape(f32[1920,256]{0,1:T(8,128)S(1)} %convolution_bitcast_fusion.4) | data formatting | bytes 3932160 | tf_op jit(solution)/shard_map/while/body/eval_jaxpr/reshape | solution.py:97
  231.8 11.1 %convolution_bitcast_fusion.5 = f32[48,16,16,16]{0,1,3,2:T(8,128)S(1)} fusion(f32[48,40,16,16]{1,0,3,2:T(8,128)} %reshape.215, s32[16,40]{1,0:T(8,128)S(1)} %iota_subtract_fusion.4), kind=kOutput, calls=%fused_computation.10.clone.1 | convolution fusion | flops 94382080 | bytes 2755072 | tf_op jit(solution)/shard_map/while/body/eval_jaxpr/xyak,ajy->xjak/dot_general | solution.py:101
  242.9 14.7 %fusion.94 = f32[16,16,16,16]{3,0,1,2:T(8,128)S(1)} fusion(f32[48,16,16,16]{0,1,3,2:T(8,128)S(1)} %convolution_bitcast_fusion.5, f32[16]{0:T(128)S(1)} %get-tuple-element.278, s32[16,48]{1,0:T(8,128)S(1)} %iota_subtract_fusion.5), kind=kOutput, calls=%fused_computation.9.clone.1 | convolution fusion | flops 37773312 | bytes 1051712 | tf_op jit(solution)/shard_map/while/body/eval_jaxpr/xjak,aix->ijak/dot_general | solution.py:106
  257.6 4.4 %fusion.95 = f32[4,16,50]{2,1,0:T(8,128)S(1)} fusion(f32[4,16,50]{2,1,0:T(8,128)S(1)} %get-tuple-element.292, s32[]{:T(128)} %get-tuple-element.291, f32[50,16,16,16]{0,3,2,1:T(8,128)S(1)} %copy-done.1, f32[16,16,16,16]{3,0,1,2:T(8,128)S(1)} %fusion.94), kind=kOutput, calls=%fused_computation.12.clone.1 | convolution fusion | flops 39321600 | bytes 4202500 | tf_op jit(solution)/shard_map/while/body/eval_jaxpr/sijk,ijak->as/dot_general | solution.py:107
  262.4 15.7 %psum.7 = f32[64,25]{1,0:T(8,128)S(1)} all-reduce(f32[64,25]{1,0:T(8,128)S(1)} %broadcast_multiply_fusion), channel_id=1, replica_groups=mesh['band'=4,'dx'=8,'dyz'=16] {'band'}, use_global_device_ids=true, to_apply=%region_3.4 | all-reduce | flops 1600 | bytes 12800 | tf_op jit(solution)/shard_map/psum | solution.py:156
  (117 shorter events, 19.1 us)
Async XLA Ops:
  0.6 278.2 %copy-start = (f32[64,16,128]{2,1,0:T(8,128)S(1)}, f32[64,16,128]{2,1,0:T(8,128)}, u32[]{:S(2)}) copy-start(f32[64,16,128]{2,1,0:T(8,128)} %param.21) | copy-start | bytes 1572868
  1.4 11.8 %collective-permute-start.1 = (f32[1,24,128]{2,1,0:T(8,128)S(1)}, f32[1,24,128]{2,1,0:T(8,128)S(1)}, u32[]{:S(2)}, u32[]{:S(2)}) collective-permute-start(f32[1,24,128]{2,1,0:T(8,128)S(1)} %get-tuple-element.230), channel_id=1, source_target_pairs={{0,16},{16,32},{32,48},{48,64},{64,80},{80,96},{96,112},{112,0},{1... | collective-permute-start | bytes 36872 | tf_op jit(solution)/shard_map/ppermute | solution.py:23
  8.5 6.8 %collective-permute-start = (f32[1,24,128]{2,1,0:T(8,128)S(1)}, f32[1,24,128]{2,1,0:T(8,128)S(1)}, u32[]{:S(2)}, u32[]{:S(2)}) collective-permute-start(f32[1,24,128]{2,1,0:T(8,128)S(1)} %get-tuple-element.229), channel_id=1, source_target_pairs={{16,0},{32,16},{48,32},{64,48},{80,64},{96,80},{112,96},{0,112},{1... | collective-permute-start | bytes 36872 | tf_op jit(solution)/shard_map/ppermute | solution.py:24
  15.3 5.3 %collective-permute-start.2 = (f32[34,1,128]{2,1,0:T(1,128)S(1)}, f32[34,1,128]{2,1,0:T(1,128)S(1)}, u32[]{:S(2)}, u32[]{:S(2)}) collective-permute-start(f32[34,1,128]{2,1,0:T(1,128)S(1)} %get-tuple-element.225), channel_id=1, source_target_pairs={{1,0},{2,1},{3,2},{4,3},{5,4},{6,5},{7,6},{8,7},{9,8},{10,9},{11,1... | collective-permute-start | bytes 52232 | tf_op jit(solution)/shard_map/ppermute | solution.py:24
  19.1 4.4 %collective-permute-start.3 = (f32[34,1,128]{2,1,0:T(1,128)S(1)}, f32[34,1,128]{2,1,0:T(1,128)S(1)}, u32[]{:S(2)}, u32[]{:S(2)}) collective-permute-start(f32[34,1,128]{2,1,0:T(1,128)S(1)} %get-tuple-element.226), channel_id=1, source_target_pairs={{0,1},{1,2},{2,3},{3,4},{4,5},{5,6},{6,7},{7,8},{8,9},{9,10},{10,1... | collective-permute-start | bytes 52232 | tf_op jit(solution)/shard_map/ppermute | solution.py:23
  23.6 13.8 %copy-start.3 = (f32[32,24,128]{2,1,0:T(8,128)S(1)}, f32[32,24,128]{2,1,0:T(8,128)}, u32[]{:S(2)}) copy-start(f32[32,24,128]{2,1,0:T(8,128)} %param.12) | copy-start | bytes 1179652
  24.2 7.1 %collective-permute-start.4 = (f32[34,26,1]{0,2,1:T(1,128)S(1)}, f32[34,26,1]{0,2,1:T(1,128)S(1)}, u32[]{:S(2)}, u32[]{:S(2)}) collective-permute-start(f32[34,26,1]{0,2,1:T(1,128)S(1)} %copy.47), channel_id=1, source_target_pairs={{128,0},{256,128},{384,256},{0,384},{129,1},{257,129},{385,257},{1... | collective-permute-start | bytes 10616 | tf_op jit(solution)/shard_map/ppermute | solution.py:24
  29.2 6.8 %collective-permute-start.5 = (f32[34,26,1]{0,2,1:T(1,128)S(1)}, f32[34,26,1]{0,2,1:T(1,128)S(1)}, u32[]{:S(2)}, u32[]{:S(2)}) collective-permute-start(f32[34,26,1]{0,2,1:T(1,128)S(1)} %copy.49), channel_id=1, source_target_pairs={{0,128},{128,256},{256,384},{384,0},{1,129},{129,257},{257,385},{3... | collective-permute-start | bytes 10616 | tf_op jit(solution)/shard_map/ppermute | solution.py:23
  39.6 10.8 %copy-start.4 = (f32[32,24,128]{2,1,0:T(8,128)}, f32[32,24,128]{2,1,0:T(8,128)S(1)}, u32[]{:S(2)}) copy-start(f32[32,24,128]{2,1,0:T(8,128)S(1)} %get-tuple-element.209) | copy-start | bytes 1179652
  39.8 6.0 %collective-permute-start.6 = (f32[3,1,24,128]{3,2,1,0:T(8,128)S(1)}, f32[3,1,24,128]{3,2,1,0:T(8,128)S(1)}, u32[]{:S(2)}, u32[]{:S(2)}) collective-permute-start(f32[3,1,24,128]{3,2,1,0:T(8,128)S(1)} %get-tuple-element.221), channel_id=1, source_target_pairs={{0,16},{16,32},{32,48},{48,64},{64,80},{80,96},{96,112},{112,0},{1... | collective-permute-start | bytes 110600 | tf_op jit(solution)/shard_map/ppermute | solution.py:23
  43.2 7.1 %collective-permute-start.7 = (f32[3,1,24,128]{3,2,1,0:T(8,128)S(1)}, f32[3,1,24,128]{3,2,1,0:T(8,128)S(1)}, u32[]{:S(2)}, u32[]{:S(2)}) collective-permute-start(f32[3,1,24,128]{3,2,1,0:T(8,128)S(1)} %get-tuple-element.222), channel_id=1, source_target_pairs={{16,0},{32,16},{48,32},{64,48},{80,64},{96,80},{112,96},{0,112},{1... | collective-permute-start | bytes 110600 | tf_op jit(solution)/shard_map/ppermute | solution.py:24
  50.4 4.8 %collective-permute-start.8 = (f32[3,34,1,128]{3,2,1,0:T(1,128)S(1)}, f32[3,34,1,128]{3,2,1,0:T(1,128)S(1)}, u32[]{:S(2)}, u32[]{:S(2)}) collective-permute-start(f32[3,34,1,128]{3,2,1,0:T(1,128)S(1)} %get-tuple-element.219), channel_id=1, source_target_pairs={{0,1},{1,2},{2,3},{3,4},{4,5},{5,6},{6,7},{7,8},{8,9},{9,10},{10,1... | collective-permute-start | bytes 156680 | tf_op jit(solution)/shard_map/ppermute | solution.py:23
  50.4 4.7 %collective-permute-start.9 = (f32[3,34,1,128]{3,2,1,0:T(1,128)S(1)}, f32[3,34,1,128]{3,2,1,0:T(1,128)S(1)}, u32[]{:S(2)}, u32[]{:S(2)}) collective-permute-start(f32[3,34,1,128]{3,2,1,0:T(1,128)S(1)} %get-tuple-element.220), channel_id=1, source_target_pairs={{1,0},{2,1},{3,2},{4,3},{5,4},{6,5},{7,6},{8,7},{9,8},{10,9},{11,1... | collective-permute-start | bytes 156680 | tf_op jit(solution)/shard_map/ppermute | solution.py:24
  60.0 10.1 %collective-permute-start.10 = (f32[3,34,26,1]{1,3,2,0:T(1,128)S(1)}, f32[3,34,26,1]{1,3,2,0:T(1,128)S(1)}, u32[]{:S(2)}, u32[]{:S(2)}) collective-permute-start(f32[3,34,26,1]{1,3,2,0:T(1,128)S(1)} %copy.51), channel_id=1, source_target_pairs={{0,128},{128,256},{256,384},{384,0},{1,129},{129,257},{257,385},{3... | collective-permute-start | bytes 31832 | tf_op jit(solution)/shard_map/ppermute | solution.py:23
  64.1 8.6 %collective-permute-start.11 = (f32[3,34,26,1]{1,3,2,0:T(1,128)S(1)}, f32[3,34,26,1]{1,3,2,0:T(1,128)S(1)}, u32[]{:S(2)}, u32[]{:S(2)}) collective-permute-start(f32[3,34,26,1]{1,3,2,0:T(1,128)S(1)} %copy.52), channel_id=1, source_target_pairs={{128,0},{256,128},{384,256},{0,384},{129,1},{257,129},{385,257},{1... | collective-permute-start | bytes 31832 | tf_op jit(solution)/shard_map/ppermute | solution.py:24
  80.8 1.0 copy-start.5
  80.8 1.1 copy-start.7
  81.9 11.7 %copy-start.10 = (s32[64]{0:T(128)S(1)}, s32[64]{0:T(128)}, u32[]{:S(2)}) copy-start(s32[64]{0:T(128)} %param.15) | copy-start | bytes 772
  83.5 21.9 %copy-start.2 = (f32[32,24,128]{2,1,0:T(8,128)}, f32[32,24,128]{2,1,0:T(8,128)S(1)}, u32[]{:S(2)}) copy-start(f32[32,24,128]{2,1,0:T(8,128)S(1)} %fusion.43) | copy-start | bytes 1179652
  83.5 8.8 %collective-permute-start.12 = (f32[16,24,128]{2,1,0:T(8,128)S(1)}, f32[16,24,128]{2,1,0:T(8,128)S(1)}, u32[]{:S(2)}, u32[]{:S(2)}) collective-permute-start(f32[16,24,128]{2,1,0:T(8,128)S(1)} %slice.209), channel_id=1, source_target_pairs={{16,0},{32,16},{48,32},{64,48},{80,64},{96,80},{112,96},{0,112},{1... | collective-permute-start | bytes 589832 | tf_op jit(solution)/shard_map/ppermute | solution.py:32
  92.3 13.1 %collective-permute-start.13 = (f32[48,16,128]{2,1,0:T(8,128)S(1)}, f32[48,16,128]{2,1,0:T(8,128)S(1)}, u32[]{:S(2)}, u32[]{:S(2)}) collective-permute-start(f32[48,16,128]{2,1,0:T(8,128)S(1)} %pad_maximum_fusion.4), channel_id=1, source_target_pairs={{1,0},{2,1},{3,2},{4,3},{5,4},{6,5},{7,6},{8,7},{9,8},{10,9},{11,1... | collective-permute-start | bytes 1179656 | tf_op jit(solution)/shard_map/ppermute | solution.py:32
  99.6 5.5 %copy-start.6 = (f32[2,256,256]{2,1,0:T(8,128)S(1)}, f32[2,256,256]{2,1,0:T(8,128)}, u32[]{:S(2)}) copy-start(f32[2,256,256]{2,1,0:T(8,128)} %param.19) | copy-start | bytes 1572868
  99.6 5.5 %copy-start.9 = (f32[64,256]{1,0:T(8,128)S(1)}, f32[64,256]{1,0:T(8,128)}, u32[]{:S(2)}) copy-start(f32[64,256]{1,0:T(8,128)} %param.20) | copy-start | bytes 196612
  126.2 14.8 %copy-start.1 = (f32[50,16,16,16]{0,3,2,1:T(8,128)S(1)}, f32[50,16,16,16]{0,3,2,1:T(8,128)}, u32[]{:S(2)}) copy-start(f32[50,16,16,16]{0,3,2,1:T(8,128)} %get-tuple-element.306) | copy-start | bytes 2457604 | tf_op jit(solution)/shard_map/while
  165.1 14.8 %copy-start.1 = (f32[50,16,16,16]{0,3,2,1:T(8,128)S(1)}, f32[50,16,16,16]{0,3,2,1:T(8,128)}, u32[]{:S(2)}) copy-start(f32[50,16,16,16]{0,3,2,1:T(8,128)} %get-tuple-element.306) | copy-start | bytes 2457604 | tf_op jit(solution)/shard_map/while
  204.0 14.8 %copy-start.1 = (f32[50,16,16,16]{0,3,2,1:T(8,128)S(1)}, f32[50,16,16,16]{0,3,2,1:T(8,128)}, u32[]{:S(2)}) copy-start(f32[50,16,16,16]{0,3,2,1:T(8,128)} %get-tuple-element.306) | copy-start | bytes 2457604 | tf_op jit(solution)/shard_map/while
  242.9 14.8 %copy-start.1 = (f32[50,16,16,16]{0,3,2,1:T(8,128)S(1)}, f32[50,16,16,16]{0,3,2,1:T(8,128)}, u32[]{:S(2)}) copy-start(f32[50,16,16,16]{0,3,2,1:T(8,128)} %get-tuple-element.306) | copy-start | bytes 2457604 | tf_op jit(solution)/shard_map/while
  278.4 1.8 copy-start.8
where the time goes:
time: 284 us; the launch traced here: 280 us
  matrix products  133 us (47%)
  local copies, waits for them, and re-layouts  55.6 us (20%)
  starting transfers between devices  38.6 us (14%)
  waiting for transfers between devices  21.9 us (8%)
  blocking collectives  15.7 us (6%)
  other arithmetic  14 us (5%)
    dot_general x4, matrix products, block_moments(): along_x = jnp.einsum('xjak,aix->ijak', along_y, select_x, precision=PRECISE)  59 us
    dot_general x4, matrix products, block_moments(): along_y = jnp.einsum('xyak,ajy->xjak', along_z, select_y, precision=PRECISE)  44.2 us
    reshape x4, local copies, waits for them, and re-layouts, block_moments(): along_z = along_z.reshape(width_x, width_y, group, BOX)  24.1 us
    ppermute x6, starting transfers between devices, padded_2(): after = lax.ppermute(leading, axis, down)  21.1 us
    dot_general x4, matrix products, block_moments(): return jnp.einsum('sijk,ijak->as', shaped, along_x, precision=PRECISE)  17.7 us
    psum x1, blocking collectives, local(): moments = lax.psum(partial_value, 'band')  15.7 us
    ppermute x6, starting transfers between devices, padded_2(): before = lax.ppermute(last, axis, up)  14.3 us
    ppermute x6, waiting for transfers between devices, padded_2(): before = lax.ppermute(last, axis, up)  8.93 us
  transfers between devices with their start and end apart: 14, of which 7 were waited for; matrix products, arithmetic and copies ran while one was open for 8% of the time, Pallas kernels for 0%

commit v1 on v0

v1 whole, which is shorter than its diff:
```python
import math

import jax
import jax.numpy as jnp
from jax import lax
from jax.experimental import pallas as pl
from jax.experimental.pallas import tpu as pltpu
from jax.sharding import PartitionSpec as P

BOX = 16
NI = 16
NL = 25
GRID_H = 0.15
HALF = 0.5 / GRID_H
KAPPA = 0.804
MU = 0.2195149727645171
A0 = -0.75 * (3.0 / math.pi) ** (1.0 / 3.0)
C0 = 4.0 * (3.0 * math.pi**2) ** (2.0 / 3.0)

CX, CY, CZ = 32, 24, 128
LOW = 2
DUP = 17
HUP = 15
XD = 56
XH = 48
YD = CY + LOW + DUP
YH = CY + HUP
F32, BF16 = jnp.float32, jnp.bfloat16
PARAMS = pltpu.CompilerParams(vmem_limit_bytes=48 * 1024 * 1024)


def shifted(block, axis, distance):
    n = lax.axis_size(axis)
    return lax.ppermute(block, axis, [(i, (i + distance) % n) for i in range(n)])


def split(value):
    high = value.astype(BF16)
    low = (value - high.astype(F32)).astype(BF16)
    return high, low


def dot(left, right):
    return jnp.dot(left, right, preferred_element_type=F32)


def dot3(left, right):
    lh, ll = split(left)
    rh, rl = split(right)
    return dot(lh, rh) + (dot(ll, rh) + dot(lh, rl))


def prep_kernel(shape_ref, rho_ref, coulomb_ref, pick_ref, shaped_ref, base_ref):
    pad = jnp.zeros((7, 128), F32)
    rest = jnp.zeros((64, 128), F32)
    for c in range(32):
        cols = pl.ds(c * 128, 128)
        rows = jnp.concatenate([shape_ref[0, :, cols], pad, shape_ref[1, :, cols], pad, rest], axis=0)
        turned = rows.T
        high = turned.astype(BF16).astype(F32)
        low = (turned - high).astype(BF16).astype(F32)
        shaped_ref[cols, :] = (high + pltpu.roll(low, 64, 1)).astype(BF16)
    rho = rho_ref[...]
    total = jnp.zeros((64, 256), F32)
    for s in range(2):
        total = total + dot3(rho * pick_ref[:, s : s + 1], coulomb_ref[s])
    base_ref[...] = 2.0 * total


def widen_kernel(dens_ref, hart_ref, above_ref, below_ref, ed_ref, eh_ref, down_ref, up_ref):
    ones = jnp.ones((CY, CZ), F32)
    for s in range(XD):
        x = s - LOW
        if x < 0:
            plane = below_ref[s]
        elif x < CX:
            plane = dens_ref[x]
        elif x < CX + DUP:
            plane = above_ref[x - CX]
        else:
            plane = ones
        ed_ref[pl.ds(s, CY, stride=XD), :] = plane
    for x in range(XH):
        if x < CX:
            plane = hart_ref[x]
        elif x < CX + HUP:
            plane = above_ref[DUP + x - CX]
        else:
            plane = ones
        eh_ref[pl.ds(x, CY, stride=XH), :] = plane
    down_ref[: DUP * XD] = ed_ref[: DUP * XD]
    down_ref[DUP * XD :] = eh_ref[: HUP * XH]
    up_ref[...] = ed_ref[(CY - LOW) * XD :]


def gather_density(ed_ref, down_ref, up_ref, dens, sems):
    copies = [
        pltpu.make_async_copy(up_ref, dens.at[pl.ds(0, LOW * XD)], sems.at[0]),
        pltpu.make_async_copy(ed_ref, dens.at[pl.ds(LOW * XD, CY * XD)], sems.at[1]),
        pltpu.make_async_copy(
            down_ref.at[pl.ds(0, DUP * XD)], dens.at[pl.ds((LOW + CY) * XD, DUP * XD)], sems.at[2]
        ),
    ]
    return copies


def ends_kernel(ed_ref, down_ref, up_ref, low_ref, high_ref, dens, sems):
    copies = gather_density(ed_ref, down_ref, up_ref, dens, sems)
    for copy in copies:
        copy.start()
    for copy in copies:
        copy.wait()
    lane = lax.broadcasted_iota(jnp.int32, (XD, 128), 1)

    def step(line, planes):
        rows = dens[pl.ds(pl.multiple_of(line * XD, 8), XD), :]
        here = lane == line
        return tuple(
            jnp.where(here, pltpu.roll(rows, lax.rem(line - z + 128, 128), 1), plane)
            for z, plane in zip((0, 1, 126, 127), planes)
        )

    start = jnp.ones((XD, 128), F32)
    planes = lax.fori_loop(0, YD, step, (start,) * 4)
    low_ref[:XD], low_ref[XD:] = planes[0], planes[1]
    high_ref[:XD], high_ref[XD:] = planes[2], planes[3]


def slopes(dens, sigma):
    root = jnp.exp(jnp.log(dens) * (1.0 / 3.0))
    inv = 1.0 / (dens * root)
    scaled = sigma * inv * inv
    t = 1.0 / (1.0 + (MU / (KAPPA * C0)) * scaled)
    tt = t * t
    slope_s = (A0 * MU / C0) * inv * tt
    slope_n = root * (
        (A0 * 4.0 / 3.0 * (1.0 + KAPPA) - (A0 * 4.0 / 3.0 * KAPPA) * t)
        - (A0 * 8.0 / 3.0 * MU / C0) * scaled * tt
    )
    return slope_n, slope_s


def field_kernel(
    plan_ref,
    ed_ref, eh_ref, down_ref, up_ref,
    low_ref, high_ref, after_ref, before_ref,
    shaped_ref, mask_ref,
    out_ref, part_ref,
    dens, hart, ends, flux_x, flux_y, local_n, field, windows, sems,
):
    copies = gather_density(ed_ref, down_ref, up_ref, dens, sems)
    copies += [
        pltpu.make_async_copy(eh_ref, hart.at[pl.ds(0, CY * XH)], sems.at[3]),
        pltpu.make_async_copy(
            down_ref.at[pl.ds(DUP * XD, HUP * XH)], hart.at[pl.ds(CY * XH, HUP * XH)], sems.at[4]
        ),
    ]
    for copy in copies:
        copy.start()
    windows[...] = jnp.zeros_like(windows)

    def outside(center, toward_high, toward_low):
        gx = (pltpu.roll(center, XD - 1, 0) - pltpu.roll(center, 1, 0)) * HALF
        gy = (pltpu.roll(center, 127, 1) - pltpu.roll(center, 1, 1)) * HALF
        gz = (toward_high - toward_low) * HALF
        _, slope_s = slopes(center, gx * gx + gy * gy + gz * gz)
        return slope_s * gz

    below = before_ref[XD:]
    above = after_ref[:XD]
    ends[0] = below
    ends[1] = above
    ends[2] = outside(below, low_ref[:XD], before_ref[:XD])
    ends[3] = outside(above, after_ref[XD:], high_ref[XD:])
    for copy in copies:
        copy.wait()

    lane = lax.broadcasted_iota(jnp.int32, (XD, 128), 1)
    first, last = lane == 0, lane == 127

    def z_pair(rows, low_end, high_end, line):
        up = jnp.where(last, pltpu.roll(high_end, 127 - line, 1), pltpu.roll(rows, 127, 1))
        down = jnp.where(first, pltpu.roll(low_end, 128 - line, 1), pltpu.roll(rows, 1, 1))
        return up - down

    def flux_step(line, carry):
        base = pl.multiple_of(line * XD, 8)
        center = dens[pl.ds(base, XD), :]
        gx = (dens[pl.ds(base + 1, XD), :] - dens[pl.ds(base - 1, XD), :]) * HALF
        gy = (
            dens[pl.ds(pl.multiple_of(base + XD, 8), XD), :]
            - dens[pl.ds(pl.multiple_of(base - XD, 8), XD), :]
        ) * HALF
        gz = z_pair(center, ends[0], ends[1], line) * HALF
        slope_n, slope_s = slopes(center, gx * gx + gy * gy + gz * gz)
        flux_x[pl.ds(base, XD), :] = slope_s * gx
        flux_y[pl.ds(base, XD), :] = slope_s * gy
        spread = z_pair(slope_s * gz, ends[2], ends[3], line)
        local_n[pl.ds(base, XD), :] = slope_n - (2.0 * HALF) * spread
        return carry

    lax.fori_loop(1, YD - 1, flux_step, 0)

    def field_step(y, carry):
        base = (y + LOW) * XD + LOW
        spread = (flux_x[pl.ds(base + 1, XH), :] - flux_x[pl.ds(base - 1, XH), :]) + (
            flux_y[pl.ds(base + XD, XH), :] - flux_y[pl.ds(base - XD, XH), :]
        )
        here = pl.multiple_of(y * XH, 8)
        value = hart[pl.ds(here, XH), :] + local_n[pl.ds(base, XH), :] - (2.0 * HALF) * spread
        field[pl.ds(here, XH), :] = value

        @pl.when(y < CY)
        def _():
            out_ref[pl.ds(y, CX, stride=CY), :] = value[:CX]

        return carry

    lax.fori_loop(0, YH, field_step, 0)

    step_z = lax.broadcasted_iota(jnp.int32, (16, 128), 1)
    group = step_z // 16
    step_z = step_z % 16

    def atom_step(atom, carry):
        @pl.when(plan_ref[3, atom] != 0)
        def _():
            rx, ry, rz = plan_ref[0, atom], plan_ref[1, atom], plan_ref[2, atom]
            shift = 128 - lax.rem(rz, 128)
            inside = ((step_z + rz) & 511) < 128
            for jh in range(2):
                packed = jnp.zeros((16, 128), F32)
                for jl in range(8):
                    j = jh * 8 + jl
                    rows = field[pl.ds((ry + j) * XH + rx, 16), :]
                    turned = pltpu.roll(rows, lax.rem(shift + jl * 16, 128), 1)
                    packed = jnp.where(group == jl, turned, packed)
                packed = jnp.where(inside, packed, 0.0)
                windows[pl.ds(atom + jh * 1024, 16, stride=64), :] = packed

        return carry

    lax.fori_loop(0, 64, atom_step, 0)

    total = jnp.zeros((128, 128), F32)
    for i in range(16):
        rows = [windows[pl.ds(jh * 1024 + i * 64, 64), :] for jh in range(2)]
        high, low = split(jnp.concatenate(rows, axis=1))
        both = jnp.concatenate([high, low], axis=0)
        total = total + dot(both, shaped_ref[pl.ds(i * 256, 256), :])
    total = total[:64] + total[64:]
    total = (total + pltpu.roll(total, 64, 1)) * mask_ref[...]
    for b in range(4):
        part_ref[b] = total


def apply_kernel(parts_ref, coupling_ref, base_ref, live_ref, proj_ref, ham_ref, out_ref, spread_ref):
    moments = (parts_ref[0] + parts_ref[1]) + (parts_ref[2] + parts_ref[3])
    ham = (dot3(moments, coupling_ref[...]) + base_ref[...]) * live_ref[:, :1]
    ham_ref[...] = ham
    lane = lax.broadcasted_iota(jnp.int32, (64, 128), 1)
    row = lax.broadcasted_iota(jnp.int32, (64, 128), 0)
    mine = (lane // 16) == (row % 8)
    halves = [pltpu.roll(ham[:, s : s + 128], 0, 1, stride=16, stride_axis=0) for s in (0, 128)]
    for i in range(16):
        placed = halves[i // 8]
        if i % 8:
            placed = pltpu.roll(placed, 128 - (i % 8) * 16, 1)
        spread_ref[pl.ds(i, 64, stride=16), :] = jnp.where(mine, placed, 0.0)
    for g in range(8):
        rows = pl.ds(g * 128, 128)
        out_ref[rows, :] = dot3(spread_ref[rows, :], proj_ref[rows, :])


def vmem(count):
    return [pl.BlockSpec(memory_space=pltpu.VMEM)] * count


def anywhere(count):
    return [pl.BlockSpec(memory_space=pl.ANY)] * count


def shape(*dims, dtype=F32):
    return jax.ShapeDtypeStruct(dims, dtype)


def local(
    density, hartree, box_root, species, atom_count, shape_functions, coupling, coulomb, rho_ij, projections
):
    slots = box_root.shape[1]
    first_x = lax.axis_index("dx") * CX
    first_y = lax.axis_index("dyz") * CY
    first_z = lax.axis_index("band") * CZ
    depth = CZ * lax.axis_size("band")

    above = shifted(jnp.concatenate([density[:DUP], hartree[:HUP]], axis=0), "dx", -1)
    below = shifted(density[CX - LOW :], "dx", 1)

    live = jnp.arange(slots, dtype=jnp.int32) < atom_count[0]
    offset = (box_root[2] - first_z) % depth
    meets = live & ((offset < CZ) | (offset > depth - BOX))
    plan = jnp.stack([box_root[0] - first_x, box_root[1] - first_y, offset, meets.astype(jnp.int32)])
    spec_lane = jnp.arange(128, dtype=jnp.int32)[None, :] // 32
    mask = (spec_lane == species[:, None]).astype(F32) * GRID_H**3
    picks = (jnp.arange(128, dtype=jnp.int32)[None, :] == species[:, None]).astype(F32)
    live_rows = jnp.broadcast_to(live[:, None], (slots, 128)).astype(F32)
    tensors = jnp.pad(coupling, ((0, 2), (0, 32 - NL), (0, 0))).reshape(128, NI * NI)

    shaped, base = pl.pallas_call(
        prep_kernel,
        out_shape=(shape(4096, 128, dtype=BF16), shape(64, 256)),
        in_specs=vmem(4),
        out_specs=tuple(vmem(2)),
        compiler_params=PARAMS,
        name="prep",
    )(shape_functions, rho_ij, coulomb, picks)

    wide_d, wide_h, send_down, send_up = pl.pallas_call(
        widen_kernel,
        out_shape=(
            shape(CY * XD, CZ),
            shape(CY * XH, CZ),
            shape(DUP * XD + HUP * XH, CZ),
            shape(LOW * XD, CZ),
        ),
        in_specs=vmem(4),
        out_specs=tuple(vmem(4)),
        compiler_params=PARAMS,
        name="widen",
    )(density, hartree, above, below)

    from_up = shifted(send_down, "dyz", -1)
    from_down = shifted(send_up, "dyz", 1)

    low, high = pl.pallas_call(
        ends_kernel,
        out_shape=(shape(2 * XD, 128), shape(2 * XD, 128)),
        in_specs=anywhere(3),
        out_specs=tuple(vmem(2)),
        scratch_shapes=[pltpu.VMEM((YD * XD, CZ), F32), pltpu.SemaphoreType.DMA((3,))],
        compiler_params=PARAMS,
        name="ends",
    )(wide_d, from_up, from_down)

    after = shifted(low, "band", -1)
    before = shifted(high, "band", 1)

    potential, parts = pl.pallas_call(
        field_kernel,
        out_shape=(shape(CX * CY, CZ), shape(4, 64, 128)),
        in_specs=[pl.BlockSpec(memory_space=pltpu.SMEM)] + anywhere(4) + vmem(6),
        out_specs=tuple(vmem(2)),
        scratch_shapes=[
            pltpu.VMEM((YD * XD, CZ), F32),
            pltpu.VMEM((YH * XH, CZ), F32),
            pltpu.VMEM((4, XD, 128), F32),
            pltpu.VMEM((YD * XD, CZ), F32),
            pltpu.VMEM((YD * XD, CZ), F32),
            pltpu.VMEM((YD * XD, CZ), F32),
            pltpu.VMEM((YH * XH, CZ), F32),
            pltpu.VMEM((2 * 16 * 64, 128), F32),
            pltpu.SemaphoreType.DMA((5,)),
        ],
        compiler_params=PARAMS,
        name="field",
    )(plan, wide_d, wide_h, from_up, from_down, low, high, after, before, shaped, mask)

    parts = lax.all_to_all(parts, "band", 0, 0)

    atom_hamiltonian, applied = pl.pallas_call(
        apply_kernel,
        out_shape=(shape(64, 256), shape(64 * NI, 128)),
        in_specs=vmem(5),
        out_specs=tuple(vmem(2)),
        scratch_shapes=[pltpu.VMEM((64 * NI, 128), F32)],
        compiler_params=PARAMS,
        name="apply",
    )(parts, tensors, base, live_rows, projections.reshape(slots * NI, CZ))
    return (
        potential.reshape(CX, CY, CZ),
        atom_hamiltonian,
        applied.reshape(slots, NI, CZ),
    )


def solution(mesh):
    in_specs = (
        P("dx", "dyz", "band"),
        P("dx", "dyz", "band"),
        P(None, ("dx", "dyz")),
        P(("dx", "dyz")),
        P(("dx", "dyz")),
        P(),
        P(),
        P(),
        P(("dx", "dyz"), None),
        P(("dx", "dyz"), None, "band"),
    )
    out_specs = (P("dx", "dyz", "band"), P(("dx", "dyz"), None), P(("dx", "dyz"), None, "band"))
    return jax.shard_map(local, mesh=mesh, in_specs=in_specs, out_specs=out_specs, check_vma=False)
```

time: 284 us -> 77 us (0.27); the launches traced: 280 us -> 76.6 us
  matrix products: 133 us -> 0 us
  local copies, waits for them, and re-layouts: 55.6 us -> 2.48 us
  Pallas kernels: 0 us -> 22.6 us
  blocking collectives: 15.7 us -> 0 us
  other arithmetic: 14 us -> 0.21 us
  starting transfers between devices: 38.6 us -> 26.7 us
    dot_general x21 -> x0, matrix products: 133 us -> none  [the longest x4 59 us: block_moments(): along_x = jnp.einsum('xjak,aix->ijak', along_y, select_x, precision=PRECISE)]
    reshape x7 -> x0, local copies, waits for them, and re-layouts: 30.1 us -> none  [the longest x4 24.1 us: block_moments(): along_z = along_z.reshape(width_x, width_y, group, BOX)]
    pallas_call x0 -> x5, Pallas kernels: none -> 22.6 us  [the longest x1 14.7 us: local(): pl.pallas_call(field_kernel, out_shape=(shape(CX * CY, CZ), shape(4, 64,...]
    psum x1 -> x0, blocking collectives: 15.7 us -> none  [local(): moments = lax.psum(partial_value, 'band')]
    ppermute x14 -> x6, starting transfers between devices: 38.6 us -> 23.3 us  [shifted(): lax.ppermute(block, axis, [(i, (i + distance) % n) for i in range(n)])]
    slice x10 -> x5, local copies, waits for them, and re-layouts: 9.47 us -> 1.01 us  [the longest x2 0.91 us: local(): density[:DUP]]
    ppermute x4 -> x0, local copies, waits for them, and re-layouts: 7.15 us -> none  [the longest x2 3.93 us: padded_2(): before = lax.ppermute(last, axis, up)]
    concatenate x5 -> x1, other arithmetic: 6.92 us -> 0.03 us  [local(): jnp.concatenate([density[:DUP], hartree[:HUP]], axis=0)]
  transfers between devices with their start and end apart: 14 -> 7, of which waited for: 7 -> 6; matrix products, arithmetic and copies ran while one was open for 8% -> 1% of each run, Pallas kernels for 0% -> 1%
where the time goes in v1:
time: 77 us; the launch traced here: 76.6 us
  starting transfers between devices  26.7 us (35%)
  waiting for transfers between devices  23.1 us (30%)
  Pallas kernels  22.6 us (29%)
  local copies, waits for them, and re-layouts  2.48 us (3%)
  between operations  1.51 us (2%)
    ppermute x6, starting transfers between devices, shifted(): lax.ppermute(block, axis, [(i, (i + distance) % n) for i in range(n)])  23.3 us
    ppermute x6, waiting for transfers between devices, shifted(): lax.ppermute(block, axis, [(i, (i + distance) % n) for i in range(n)])  17.2 us
    pallas_call x1, Pallas kernels, local(): pl.pallas_call(field_kernel, out_shape=(shape(CX * CY, CZ), shape(4, 64,...  14.7 us
    all_to_all x1, waiting for transfers between devices, local(): parts = lax.all_to_all(parts, 'band', 0, 0)  5.93 us
    pallas_call x1, Pallas kernels, local(): pl.pallas_call(ends_kernel, out_shape=(shape(2 * XD, 128), shape(2 * XD,...  4.86 us
    all_to_all x1, starting transfers between devices, local(): parts = lax.all_to_all(parts, 'band', 0, 0)  3.34 us
    pallas_call x1, Pallas kernels, local(): pl.pallas_call(apply_kernel, out_shape=(shape(64, 256), shape(64 * NI, 12...  1.6 us
  transfers between devices with their start and end apart: 7, of which 6 were waited for; matrix products, arithmetic and copies ran while one was open for 1% of the time, Pallas kernels for 1%

profile of v1, /device:TPU:56, one launch (start us, length us, event | category | flops | bytes accessed | tf_op | source)
XLA Modules:
  0.0 76.6 jit_solution(14142084217608647371)
XLA Ops:
  0.6 0.0 slice-start
  0.6 0.0 slice-start.1
  0.7 0.9 %slice-done = f32[17,24,128]{2,1,0:T(8,128)S(1)} async-done(((f32[32,24,128]{2,1,0:T(8,128)}), f32[17,24,128]{2,1,0:T(8,128)S(1)}, s32[]{:S(2)}) %slice-start) | async-done | bytes 208920 | tf_op jit(solution)/shard_map/slice | solution.py:296
  1.6 0.1 slice-done.1
  1.7 0.0 copy-start
  1.7 0.0 copy-start.1
  1.7 0.0 copy-start.5
  1.7 3.4 %collective-permute-start = (f32[32,24,128]{2,1,0:T(8,128)S(1)}, f32[32,24,128]{2,1,0:T(8,128)S(1)}, u32[]{:S(2)}, u32[]{:S(2)}) collective-permute-start(f32[32,24,128]{2,1,0:T(8,128)S(1)} %pad_maximum_fusion), channel_id=1, source_target_pairs={{0,112},{16,0},{32,16},{48,32},{64,48},{80,64},{96,80},{112,96},{1... | collective-permute-start | bytes 1179656 | tf_op jit(solution)/shard_map/ppermute | solution.py:34
  5.1 0.0 copy-done
  5.1 5.7 %collective-permute-start.1 = (f32[2,24,128]{2,1,0:T(8,128)S(1)}, f32[2,24,128]{2,1,0:T(8,128)S(1)}, u32[]{:S(2)}, u32[]{:S(2)}) collective-permute-start(f32[2,24,128]{2,1,0:T(8,128)S(1)} %slice.23), channel_id=1, source_target_pairs={{0,16},{16,32},{32,48},{48,64},{64,80},{80,96},{96,112},{112,0},{1... | collective-permute-start | bytes 73736 | tf_op jit(solution)/shard_map/ppermute | solution.py:34
  11.5 0.8 %collective-permute-done.1.below_ref = f32[2,24,128]{2,1,0:T(8,128)S(1)} collective-permute-done((f32[2,24,128]{2,1,0:T(8,128)S(1)}, f32[2,24,128]{2,1,0:T(8,128)S(1)}, u32[]{:S(2)}, u32[]{:S(2)}) %collective-permute-start.1) | collective-permute-done | bytes 24608 | tf_op jit(solution)/shard_map/ppermute | solution.py:34
  12.3 3.5 %collective-permute-done.above_ref = f32[32,24,128]{2,1,0:T(8,128)S(1)} collective-permute-done((f32[32,24,128]{2,1,0:T(8,128)S(1)}, f32[32,24,128]{2,1,0:T(8,128)S(1)}, u32[]{:S(2)}, u32[]{:S(2)}) %collective-permute-start) | collective-permute-done | bytes 393248 | tf_op jit(solution)/shard_map/ppermute | solution.py:34
  15.8 0.0 copy-done.1
  15.8 0.0 copy-start.8
  15.8 0.0 copy-start.7
  15.8 0.4 widen.1
  16.2 0.0 copy-start.6
  16.2 7.6 %collective-permute-start.2 = (f32[1672,128]{1,0:T(8,128)S(1)}, f32[1672,128]{1,0:T(8,128)S(1)}, u32[]{:S(2)}, u32[]{:S(2)}) collective-permute-start(f32[1672,128]{1,0:T(8,128)S(1)} %get-tuple-element.17), channel_id=1, source_target_pairs={{0,15},{1,0},{2,1},{3,2},{4,3},{5,4},{6,5},{7,6},{8,7},{9,8},{10,9... | collective-permute-start | bytes 2568200 | tf_op jit(solution)/shard_map/ppermute | solution.py:34
  23.8 0.0 copy-done.8
  23.8 0.0 copy-done.7
  23.8 0.1 fusion.pick_ref
  23.9 0.1 compare_select_fusion.mask_ref
  24.0 0.0 collective-permute-start.3
  24.0 0.0 copy-done.6
  24.1 0.0 copy-done.5
  24.1 0.0 copy-start.2
  24.1 0.5 copy.13.shape_ref
  24.6 0.0 copy-start.4
  24.6 0.5 copy-done.2
  25.1 0.3 copy-done.4
  25.4 1.1 %prep.1 = (bf16[4096,128]{1,0:T(8,128)(2,1)S(1)}, f32[64,256]{1,0:T(8,128)S(1)}) custom-call(f32[2,25,4096]{2,1,0:T(8,128)S(1)} %copy.13.shape_ref, f32[64,256]{1,0:T(8,128)S(1)} %copy-done.4, f32[2,256,256]{2,1,0:T(8,128)S(1)} %copy-done.2, f32[64,128]{1,0:T(8,128)S(1)} %fusion.pick_ref), custom_call_target="tpu_custom_call" | custom-call | tf_op jit(solution)/shard_map/prep/pallas_call | solution.py:309
  26.5 2.3 %collective-permute-done.3.up_ref = f32[112,128]{1,0:T(8,128)S(1)} collective-permute-done((f32[112,128]{1,0:T(8,128)S(1)}, f32[112,128]{1,0:T(8,128)S(1)}, u32[]{:S(2)}, u32[]{:S(2)}) %collective-permute-start.3) | collective-permute-done | bytes 57376 | tf_op jit(solution)/shard_map/ppermute | solution.py:34
  28.8 5.3 %collective-permute-done.2.down_ref = f32[1672,128]{1,0:T(8,128)S(1)} collective-permute-done((f32[1672,128]{1,0:T(8,128)S(1)}, f32[1672,128]{1,0:T(8,128)S(1)}, u32[]{:S(2)}, u32[]{:S(2)}) %collective-permute-start.2) | collective-permute-done | bytes 856096 | tf_op jit(solution)/shard_map/ppermute | solution.py:34
  34.1 4.9 %ends.1 = (f32[112,128]{1,0:T(8,128)S(1)}, f32[112,128]{1,0:T(8,128)S(1)}) custom-call(f32[1344,128]{1,0:T(8,128)S(1)} %get-tuple-element.15.ed_ref, f32[1672,128]{1,0:T(8,128)S(1)} %collective-permute-done.2.down_ref, f32[112,128]{1,0:T(8,128)S(1)} %collective-permute-done.3.up_ref), custom_call_target="tpu_custom_call" | custom-call | tf_op jit(solution)/shard_map/ends/pallas_call | solution.py:335
  39.0 4.7 %collective-permute-start.4 = (f32[112,128]{1,0:T(8,128)S(1)}, f32[112,128]{1,0:T(8,128)S(1)}, u32[]{:S(2)}, u32[]{:S(2)}) collective-permute-start(f32[112,128]{1,0:T(8,128)S(1)} %get-tuple-element.19.low_ref), channel_id=1, source_target_pairs={{0,384},{128,0},{256,128},{384,256},{1,385},{129,1},{257,129},{385... | collective-permute-start | bytes 172040 | tf_op jit(solution)/shard_map/ppermute | solution.py:34
  43.6 1.9 %collective-permute-start.5 = (f32[112,128]{1,0:T(8,128)S(1)}, f32[112,128]{1,0:T(8,128)S(1)}, u32[]{:S(2)}, u32[]{:S(2)}) collective-permute-start(f32[112,128]{1,0:T(8,128)S(1)} %get-tuple-element.20.high_ref), channel_id=1, source_target_pairs={{0,128},{128,256},{256,384},{384,0},{1,129},{129,257},{257,385},{3... | collective-permute-start | bytes 172040 | tf_op jit(solution)/shard_map/ppermute | solution.py:34
  45.6 0.0 collective-permute-done.4.after_ref
  45.6 5.3 %collective-permute-done.5.before_ref = f32[112,128]{1,0:T(8,128)S(1)} collective-permute-done((f32[112,128]{1,0:T(8,128)S(1)}, f32[112,128]{1,0:T(8,128)S(1)}, u32[]{:S(2)}, u32[]{:S(2)}) %collective-permute-start.5) | collective-permute-done | bytes 57376 | tf_op jit(solution)/shard_map/ppermute | solution.py:34
  50.9 0.0 copy-start.3
  50.9 14.7 %field.1 = (f32[768,128]{1,0:T(8,128)}, f32[4,64,128]{2,1,0:T(8,128)}) custom-call(s32[4,64]{1,0:T(4,128)S(1)} %pad_add_fusion.plan_ref, f32[1344,128]{1,0:T(8,128)S(1)} %get-tuple-element.15.ed_ref, f32[1152,128]{1,0:T(8,128)S(1)} %get-tuple-element.16.eh_ref, f32[1672,128]{1,0:T(8,128)S(1)} %collective-permute-done.2.down_ref, ...), custom_call_target="tpu_custom_call" | custom-call | tf_op jit(solution)/shard_map/field/pallas_call | solution.py:348
  65.6 3.3 %all-to-all-start = ((f32[4,64,128]{2,1,0:T(8,128)}), f32[4,64,128]{2,1,0:T(8,128)S(1)}, u32[]{:S(2)}, u32[]{:S(2)}) async-start(f32[4,64,128]{2,1,0:T(8,128)} %get-tuple-element.23), calls=%async_computation | async-start | bytes 262144 | tf_op jit(solution)/shard_map/all_to_all | solution.py:368
  69.0 5.9 %all-to-all-done.parts_ref = f32[4,64,128]{2,1,0:T(8,128)S(1)} async-done(((f32[4,64,128]{2,1,0:T(8,128)}), f32[4,64,128]{2,1,0:T(8,128)S(1)}, u32[]{:S(2)}, u32[]{:S(2)}) %all-to-all-start) | async-done | bytes 131104 | tf_op jit(solution)/shard_map/all_to_all | solution.py:368
  74.9 0.1 broadcast_in_dim.2.live_ref
  75.0 0.0 copy-done.3
  75.0 1.6 %apply.1 = (f32[64,256]{1,0:T(8,128)}, f32[1024,128]{1,0:T(8,128)}) custom-call(f32[4,64,128]{2,1,0:T(8,128)S(1)} %all-to-all-done.parts_ref, f32[128,256]{1,0:T(8,128)S(1)} %bitcast.8, f32[64,256]{1,0:T(8,128)S(1)} %get-tuple-element.24.base_ref, f32[64,128]{1,0:T(8,128)S(1)} %broadcast_in_dim.2.live_ref, f32[1024,128]{1,0:T(8,128)S(1)} %bitcast.7), custom_call_target="tpu_custom_call" | custom-call | tf_op jit(solution)/shard_map/apply/pallas_call | solution.py:370
  (9 shorter events, 0.1 us)
Async XLA Ops:
  0.6 0.9 %slice-start = ((f32[32,24,128]{2,1,0:T(8,128)}), f32[17,24,128]{2,1,0:T(8,128)S(1)}, s32[]{:S(2)}) async-start(f32[32,24,128]{2,1,0:T(8,128)} %dens_ref.1), calls=%async_computation.1 | async-start | bytes 417792 | tf_op jit(solution)/shard_map/slice | solution.py:296
  0.6 1.0 %slice-start.1 = ((f32[32,24,128]{2,1,0:T(8,128)}), f32[15,24,128]{2,1,0:T(8,128)S(1)}, s32[]{:S(2)}) async-start(f32[32,24,128]{2,1,0:T(8,128)} %hart_ref.1), calls=%async_computation.2 | async-start | bytes 368640 | tf_op jit(solution)/shard_map/slice | solution.py:296
  1.7 3.4 %copy-start = (f32[32,24,128]{2,1,0:T(8,128)S(1)}, f32[32,24,128]{2,1,0:T(8,128)}, u32[]{:S(2)}) copy-start(f32[32,24,128]{2,1,0:T(8,128)} %dens_ref.1) | copy-start | bytes 1179652
  1.7 14.1 %copy-start.1 = (f32[32,24,128]{2,1,0:T(8,128)S(1)}, f32[32,24,128]{2,1,0:T(8,128)}, u32[]{:S(2)}) copy-start(f32[32,24,128]{2,1,0:T(8,128)} %hart_ref.1) | copy-start | bytes 1179652
  1.7 22.4 %copy-start.5 = (f32[2,25,4096]{2,0,1:T(2,128)S(1)}, f32[2,25,4096]{2,0,1:T(2,128)}, u32[]{:S(2)}) copy-start(f32[2,25,4096]{2,0,1:T(2,128)} %param.15) | copy-start | bytes 2457604
  1.7 14.1 %collective-permute-start = (f32[32,24,128]{2,1,0:T(8,128)S(1)}, f32[32,24,128]{2,1,0:T(8,128)S(1)}, u32[]{:S(2)}, u32[]{:S(2)}) collective-permute-start(f32[32,24,128]{2,1,0:T(8,128)S(1)} %pad_maximum_fusion), channel_id=1, source_target_pairs={{0,112},{16,0},{32,16},{48,32},{64,48},{80,64},{96,80},{112,96},{1... | collective-permute-start | bytes 1179656 | tf_op jit(solution)/shard_map/ppermute | solution.py:34
  5.1 7.2 %collective-permute-start.1 = (f32[2,24,128]{2,1,0:T(8,128)S(1)}, f32[2,24,128]{2,1,0:T(8,128)S(1)}, u32[]{:S(2)}, u32[]{:S(2)}) collective-permute-start(f32[2,24,128]{2,1,0:T(8,128)S(1)} %slice.23), channel_id=1, source_target_pairs={{0,16},{16,32},{32,48},{48,64},{64,80},{80,96},{96,112},{112,0},{1... | collective-permute-start | bytes 73736 | tf_op jit(solution)/shard_map/ppermute | solution.py:34
  15.8 8.0 %copy-start.8 = (s32[3,64]{1,0:T(4,128)S(1)}, s32[3,64]{1,0:T(4,128)}, u32[]{:S(2)}) copy-start(s32[3,64]{1,0:T(4,128)} %param.12) | copy-start | bytes 2308
  15.8 8.0 %copy-start.7 = (s32[64]{0:T(128)S(1)}, s32[64]{0:T(128)}, u32[]{:S(2)}) copy-start(s32[64]{0:T(128)} %param.13) | copy-start | bytes 772
  16.2 7.8 %copy-start.6 = (f32[2,25,256]{2,0,1:T(2,128)S(1)}, f32[2,25,256]{2,0,1:T(2,128)}, u32[]{:S(2)}) copy-start(f32[2,25,256]{2,0,1:T(2,128)} %param.16) | copy-start | bytes 153604
  16.2 17.9 %collective-permute-start.2 = (f32[1672,128]{1,0:T(8,128)S(1)}, f32[1672,128]{1,0:T(8,128)S(1)}, u32[]{:S(2)}, u32[]{:S(2)}) collective-permute-start(f32[1672,128]{1,0:T(8,128)S(1)} %get-tuple-element.17), channel_id=1, source_target_pairs={{0,15},{1,0},{2,1},{3,2},{4,3},{5,4},{6,5},{7,6},{8,7},{9,8},{10,9... | collective-permute-start | bytes 2568200 | tf_op jit(solution)/shard_map/ppermute | solution.py:34
  24.0 4.8 %collective-permute-start.3 = (f32[112,128]{1,0:T(8,128)S(1)}, f32[112,128]{1,0:T(8,128)S(1)}, u32[]{:S(2)}, u32[]{:S(2)}) collective-permute-start(f32[112,128]{1,0:T(8,128)S(1)} %get-tuple-element.18), channel_id=1, source_target_pairs={{0,1},{1,2},{2,3},{3,4},{4,5},{5,6},{6,7},{7,8},{8,9},{9,10},{10,1... | collective-permute-start | bytes 172040 | tf_op jit(solution)/shard_map/ppermute | solution.py:34
  24.1 1.0 %copy-start.2 = (f32[2,256,256]{2,1,0:T(8,128)S(1)}, f32[2,256,256]{2,1,0:T(8,128)}, u32[]{:S(2)}) copy-start(f32[2,256,256]{2,1,0:T(8,128)} %coulomb_ref.1) | copy-start | bytes 1572868
  24.6 0.9 %copy-start.4 = (f32[64,256]{1,0:T(8,128)S(1)}, f32[64,256]{1,0:T(8,128)}, u32[]{:S(2)}) copy-start(f32[64,256]{1,0:T(8,128)} %rho_ref.1) | copy-start | bytes 196612
  39.0 6.6 %collective-permute-start.4 = (f32[112,128]{1,0:T(8,128)S(1)}, f32[112,128]{1,0:T(8,128)S(1)}, u32[]{:S(2)}, u32[]{:S(2)}) collective-permute-start(f32[112,128]{1,0:T(8,128)S(1)} %get-tuple-element.19.low_ref), channel_id=1, source_target_pairs={{0,384},{128,0},{256,128},{384,256},{1,385},{129,1},{257,129},{385... | collective-permute-start | bytes 172040 | tf_op jit(solution)/shard_map/ppermute | solution.py:34
  43.6 7.3 %collective-permute-start.5 = (f32[112,128]{1,0:T(8,128)S(1)}, f32[112,128]{1,0:T(8,128)S(1)}, u32[]{:S(2)}, u32[]{:S(2)}) collective-permute-start(f32[112,128]{1,0:T(8,128)S(1)} %get-tuple-element.20.high_ref), channel_id=1, source_target_pairs={{0,128},{128,256},{256,384},{384,0},{1,129},{129,257},{257,385},{3... | collective-permute-start | bytes 172040 | tf_op jit(solution)/shard_map/ppermute | solution.py:34
  50.9 24.1 %copy-start.3 = (f32[64,16,128]{2,1,0:T(8,128)S(1)}, f32[64,16,128]{2,1,0:T(8,128)}, u32[]{:S(2)}) copy-start(f32[64,16,128]{2,1,0:T(8,128)} %param.19) | copy-start | bytes 1572868
  65.6 9.3 %all-to-all-start = ((f32[4,64,128]{2,1,0:T(8,128)}), f32[4,64,128]{2,1,0:T(8,128)S(1)}, u32[]{:S(2)}, u32[]{:S(2)}) async-start(f32[4,64,128]{2,1,0:T(8,128)} %get-tuple-element.23), calls=%async_computation | async-start | bytes 262144 | tf_op jit(solution)/shard_map/all_to_all | solution.py:368

commit v2 on v1

--- a/solution.py
+++ b/solution.py
@@ -26,7 +26,7 @@
 YD = CY + LOW + DUP
 YH = CY + HUP
 F32, BF16 = jnp.float32, jnp.bfloat16
-PARAMS = pltpu.CompilerParams(vmem_limit_bytes=48 * 1024 * 1024)
+PARAMS = pltpu.CompilerParams(vmem_limit_bytes=16 * 1024 * 1024)
 
 
 def shifted(block, axis, distance):
@@ -93,37 +93,25 @@
     up_ref[...] = ed_ref[(CY - LOW) * XD :]
 
 
-def gather_density(ed_ref, down_ref, up_ref, dens, sems):
-    copies = [
-        pltpu.make_async_copy(up_ref, dens.at[pl.ds(0, LOW * XD)], sems.at[0]),
-        pltpu.make_async_copy(ed_ref, dens.at[pl.ds(LOW * XD, CY * XD)], sems.at[1]),
-        pltpu.make_async_copy(
-            down_ref.at[pl.ds(0, DUP * XD)], dens.at[pl.ds((LOW + CY) * XD, DUP * XD)], sems.at[2]
-        ),
-    ]
-    return copies
-
-
-def ends_kernel(ed_ref, down_ref, up_ref, low_ref, high_ref, dens, sems):
-    copies = gather_density(ed_ref, down_ref, up_ref, dens, sems)
-    for copy in copies:
-        copy.start()
-    for copy in copies:
-        copy.wait()
-    lane = lax.broadcasted_iota(jnp.int32, (XD, 128), 1)
-
-    def step(line, planes):
-        rows = dens[pl.ds(pl.multiple_of(line * XD, 8), XD), :]
-        here = lane == line
-        return tuple(
-            jnp.where(here, pltpu.roll(rows, lax.rem(line - z + 128, 128), 1), plane)
-            for z, plane in zip((0, 1, 126, 127), planes)
-        )
-
-    start = jnp.ones((XD, 128), F32)
-    planes = lax.fori_loop(0, YD, step, (start,) * 4)
-    low_ref[:XD], low_ref[XD:] = planes[0], planes[1]
-    high_ref[:XD], high_ref[XD:] = planes[2], planes[3]
+def packed(own, tile, lines, group):
+    for line, rows in lines:
+        if line // 32 == tile:
+            turned = pltpu.roll(rows, (4 * (line % 32) + 2) % 128, 1)
+            own = jnp.where(group == line % 32, turned, own)
+    return own
+
+
+def line_group():
+    return lax.broadcasted_iota(jnp.int32, (XD, 128), 1) // 4
+
+
+def ends_kernel(own_ref, down_ref, up_ref, ends_ref):
+    group = line_group()
+    lines = [(0, up_ref[:XD]), (1, up_ref[XD:])]
+    lines += [(LOW + CY + i, down_ref[i * XD : (i + 1) * XD]) for i in range(DUP)]
+    for tile in range(2):
+        cols = pl.ds(tile * 128, 128)
+        ends_ref[:, cols] = packed(own_ref[:, cols], tile, lines, group)
 
 
 def slopes(dens, sigma):
@@ -140,83 +128,115 @@
     return slope_n, slope_s
 
 
+def line_flux(center, x_up, x_down, y_up, y_down):
+    gx = (x_up - x_down) * HALF
+    gy = (y_up - y_down) * HALF
+    gz = (pltpu.roll(center, 127, 1) - pltpu.roll(center, 1, 1)) * HALF
+    slope_n, slope_s = slopes(center, gx * gx + gy * gy + gz * gz)
+    fx, fy, fz = slope_s * gx, slope_s * gy, slope_s * gz
+    spread = (pltpu.roll(fx, XD - 1, 0) - pltpu.roll(fx, 1, 0)) + (
+        pltpu.roll(fz, 127, 1) - pltpu.roll(fz, 1, 1)
+    )
+    return slope_n - (2.0 * HALF) * spread, fy
+
+
+def flux_lines(source, first, count, local_ref, flux_ref, target):
+    def step(i, carry):
+        base = pl.multiple_of((first + i) * XD, 8)
+        goal = pl.ds(pl.multiple_of((target + i) * XD, 8), XD)
+        part, flux = line_flux(
+            source[pl.ds(base, XD), :],
+            source[pl.ds(base + 1, XD), :],
+            source[pl.ds(base - 1, XD), :],
+            source[pl.ds(pl.multiple_of(base + XD, 8), XD), :],
+            source[pl.ds(pl.multiple_of(base - XD, 8), XD), :],
+        )
+        local_ref[goal, :] = part
+        flux_ref[goal, :] = flux
+        return carry
+
+    lax.fori_loop(0, count, step, 0, unroll=2)
+
+
+def inner_kernel(ed_ref, local_ref, flux_ref, ends_ref):
+    group = line_group()
+    lines = [(LOW + i, ed_ref[i * XD : (i + 1) * XD]) for i in range(CY)]
+    for tile in range(2):
+        ends_ref[:, pl.ds(tile * 128, 128)] = packed(jnp.ones((XD, 128), F32), tile, lines, group)
+    flux_lines(ed_ref, 1, CY - 2, local_ref, flux_ref, 0)
+
+
+def packed_flux(dens):
+    gx = (pltpu.roll(dens, XD - 1, 0) - pltpu.roll(dens, 1, 0)) * HALF
+    gy = (pltpu.roll(dens, 252, 1) - pltpu.roll(dens, 4, 1)) * HALF
+    gz = (pltpu.roll(dens, 255, 1) - pltpu.roll(dens, 1, 1)) * HALF
+    slope_n, slope_s = slopes(dens, gx * gx + gy * gy + gz * gz)
+    return slope_n, slope_s * gx, slope_s * gy, slope_s * gz
+
+
+def outer_kernel(ed_ref, down_ref, up_ref, ends_ref, local1_ref, flux1_ref, bulk_ref, wrap_ref, near, far, part, flux):
+    near[: 2 * XD] = up_ref[...]
+    near[2 * XD :] = ed_ref[: 2 * XD]
+    far[: 2 * XD] = ed_ref[(CY - 2) * XD :]
+    far[2 * XD :] = down_ref[: DUP * XD]
+    mine = pl.ds(3 * XD, (CY - 2) * XD)
+    part[mine, :] = local1_ref[...]
+    flux[mine, :] = flux1_ref[...]
+    flux_lines(near, 1, 2, part, flux, 1)
+    flux_lines(far, 1, DUP, part, flux, CY + 1)
+
+    def step(y, carry):
+        base = (y + LOW) * XD + LOW
+        spread = flux[pl.ds(base + XD, XH), :] - flux[pl.ds(base - XD, XH), :]
+        bulk_ref[pl.ds(pl.multiple_of(y * XH, 8), XH), :] = part[pl.ds(base, XH), :] - (2.0 * HALF) * spread
+        return carry
+
+    lax.fori_loop(0, YH, step, 0, unroll=3)
+    for i, value in enumerate(packed_flux(ends_ref[...])):
+        wrap_ref[i] = value
+
+
 def field_kernel(
     plan_ref,
-    ed_ref, eh_ref, down_ref, up_ref,
-    low_ref, high_ref, after_ref, before_ref,
+    bulk_ref, eh_ref, down_ref, ends_ref, after_ref, before_ref, wrap_ref,
     shaped_ref, mask_ref,
     out_ref, part_ref,
-    dens, hart, ends, flux_x, flux_y, local_n, field, windows, sems,
+    field, windows, fixes,
 ):
-    copies = gather_density(ed_ref, down_ref, up_ref, dens, sems)
-    copies += [
-        pltpu.make_async_copy(eh_ref, hart.at[pl.ds(0, CY * XH)], sems.at[3]),
-        pltpu.make_async_copy(
-            down_ref.at[pl.ds(DUP * XD, HUP * XH)], hart.at[pl.ds(CY * XH, HUP * XH)], sems.at[4]
-        ),
-    ]
-    for copy in copies:
-        copy.start()
     windows[...] = jnp.zeros_like(windows)
-
-    def outside(center, toward_high, toward_low):
-        gx = (pltpu.roll(center, XD - 1, 0) - pltpu.roll(center, 1, 0)) * HALF
-        gy = (pltpu.roll(center, 127, 1) - pltpu.roll(center, 1, 1)) * HALF
-        gz = (toward_high - toward_low) * HALF
-        _, slope_s = slopes(center, gx * gx + gy * gy + gz * gz)
-        return slope_s * gz
-
-    below = before_ref[XD:]
-    above = after_ref[:XD]
-    ends[0] = below
-    ends[1] = above
-    ends[2] = outside(below, low_ref[:XD], before_ref[:XD])
-    ends[3] = outside(above, after_ref[XD:], high_ref[XD:])
-    for copy in copies:
-        copy.wait()
-
-    lane = lax.broadcasted_iota(jnp.int32, (XD, 128), 1)
-    first, last = lane == 0, lane == 127
-
-    def z_pair(rows, low_end, high_end, line):
-        up = jnp.where(last, pltpu.roll(high_end, 127 - line, 1), pltpu.roll(rows, 127, 1))
-        down = jnp.where(first, pltpu.roll(low_end, 128 - line, 1), pltpu.roll(rows, 1, 1))
-        return up - down
-
-    def flux_step(line, carry):
-        base = pl.multiple_of(line * XD, 8)
-        center = dens[pl.ds(base, XD), :]
-        gx = (dens[pl.ds(base + 1, XD), :] - dens[pl.ds(base - 1, XD), :]) * HALF
-        gy = (
-            dens[pl.ds(pl.multiple_of(base + XD, 8), XD), :]
-            - dens[pl.ds(pl.multiple_of(base - XD, 8), XD), :]
-        ) * HALF
-        gz = z_pair(center, ends[0], ends[1], line) * HALF
-        slope_n, slope_s = slopes(center, gx * gx + gy * gy + gz * gz)
-        flux_x[pl.ds(base, XD), :] = slope_s * gx
-        flux_y[pl.ds(base, XD), :] = slope_s * gy
-        spread = z_pair(slope_s * gz, ends[2], ends[3], line)
-        local_n[pl.ds(base, XD), :] = slope_n - (2.0 * HALF) * spread
-        return carry
-
-    lax.fori_loop(1, YD - 1, flux_step, 0)
-
-    def field_step(y, carry):
-        base = (y + LOW) * XD + LOW
-        spread = (flux_x[pl.ds(base + 1, XH), :] - flux_x[pl.ds(base - 1, XH), :]) + (
-            flux_y[pl.ds(base + XD, XH), :] - flux_y[pl.ds(base - XD, XH), :]
+    place = lax.broadcasted_iota(jnp.int32, (XD, 256), 1) % 4
+    middle = (place == 1) | (place == 2)
+    low = place < 2
+    own = ends_ref[...]
+
+    def fix(dens):
+        dn, dx, dy, dz = [
+            jnp.where(middle, value - wrap_ref[i], 0.0) for i, value in enumerate(packed_flux(dens))
+        ]
+        spread = (
+            (pltpu.roll(dx, XD - 1, 0) - pltpu.roll(dx, 1, 0))
+            + (pltpu.roll(dy, 252, 1) - pltpu.roll(dy, 4, 1))
+            + (pltpu.roll(dz, 255, 1) - pltpu.roll(dz, 1, 1))
         )
-        here = pl.multiple_of(y * XH, 8)
-        value = hart[pl.ds(here, XH), :] + local_n[pl.ds(base, XH), :] - (2.0 * HALF) * spread
-        field[pl.ds(here, XH), :] = value
-
-        @pl.when(y < CY)
-        def _():
+        return dn - (2.0 * HALF) * spread
+
+    top = fix(jnp.where(low, own, after_ref[...]))
+    bottom = fix(jnp.where(low, before_ref[...], own))
+    fixes[...] = jnp.where(low, top, bottom)
+
+    lane = lax.broadcasted_iota(jnp.int32, (XH, 128), 1)
+    edge = (lane < 2) | (lane >= 126)
+    tiles = [fixes[pl.ds(LOW, XH), pl.ds(t * 128, 128)] for t in range(2)]
+
+    for y in range(YH):
+        line = y + LOW
+        turned = pltpu.roll(tiles[line // 32], (254 - 4 * (line % 32)) % 128, 1)
+        rows = pl.ds(y * XH, XH)
+        hart = eh_ref[rows, :] if y < CY else down_ref[pl.ds(DUP * XD + (y - CY) * XH, XH), :]
+        value = (hart + bulk_ref[rows, :]) + jnp.where(edge, turned, 0.0)
+        field[rows, :] = value
+        if y < CY:
             out_ref[pl.ds(y, CX, stride=CY), :] = value[:CX]
-
-        return carry
-
-    lax.fori_loop(0, YH, field_step, 0)
 
     step_z = lax.broadcasted_iota(jnp.int32, (16, 128), 1)
     group = step_z // 16
@@ -276,10 +296,6 @@
     return [pl.BlockSpec(memory_space=pltpu.VMEM)] * count
 
 
-def anywhere(count):
-    return [pl.BlockSpec(memory_space=pl.ANY)] * count
-
-
 def shape(*dims, dtype=F32):
     return jax.ShapeDtypeStruct(dims, dtype)
 
@@ -332,38 +348,55 @@
     from_up = shifted(send_down, "dyz", -1)
     from_down = shifted(send_up, "dyz", 1)
 
-    low, high = pl.pallas_call(
+    local1, flux1, ends1 = pl.pallas_call(
+        inner_kernel,
+        out_shape=(shape((CY - 2) * XD, CZ), shape((CY - 2) * XD, CZ), shape(XD, 256)),
+        in_specs=vmem(1),
+        out_specs=tuple(vmem(3)),
+        compiler_params=PARAMS,
+        name="inner",
+    )(wide_d)
+
+    ends = pl.pallas_call(
         ends_kernel,
-        out_shape=(shape(2 * XD, 128), shape(2 * XD, 128)),
-        in_specs=anywhere(3),
+        out_shape=shape(XD, 256),
+        in_specs=vmem(3),
+        out_specs=vmem(1)[0],
+        compiler_params=PARAMS,
+        name="ends",
+    )(ends1, from_up, from_down)
+
+    after = shifted(ends, "band", -1)
+    before = shifted(ends, "band", 1)
+
+    bulk, wrap = pl.pallas_call(
+        outer_kernel,
+        out_shape=(shape(YH * XH, CZ), shape(4, XD, 256)),
+        in_specs=vmem(6),
         out_specs=tuple(vmem(2)),
-        scratch_shapes=[pltpu.VMEM((YD * XD, CZ), F32), pltpu.SemaphoreType.DMA((3,))],
-        compiler_params=PARAMS,
-        name="ends",
-    )(wide_d, from_up, from_down)
-
-    after = shifted(low, "band", -1)
-    before = shifted(high, "band", 1)
+        scratch_shapes=[
+            pltpu.VMEM((4 * XD, CZ), F32),
+            pltpu.VMEM((19 * XD, CZ), F32),
+            pltpu.VMEM((YD * XD, CZ), F32),
+            pltpu.VMEM((YD * XD, CZ), F32),
+        ],
+        compiler_params=PARAMS,
+        name="outer",
+    )(wide_d, from_up, from_down, ends, local1, flux1)
 
     potential, parts = pl.pallas_call(
         field_kernel,
         out_shape=(shape(CX * CY, CZ), shape(4, 64, 128)),
-        in_specs=[pl.BlockSpec(memory_space=pltpu.SMEM)] + anywhere(4) + vmem(6),
+        in_specs=[pl.BlockSpec(memory_space=pltpu.SMEM)] + vmem(9),
         out_specs=tuple(vmem(2)),
         scratch_shapes=[
-            pltpu.VMEM((YD * XD, CZ), F32),
-            pltpu.VMEM((YH * XH, CZ), F32),
-            pltpu.VMEM((4, XD, 128), F32),
-            pltpu.VMEM((YD * XD, CZ), F32),
-            pltpu.VMEM((YD * XD, CZ), F32),
-            pltpu.VMEM((YD * XD, CZ), F32),
             pltpu.VMEM((YH * XH, CZ), F32),
             pltpu.VMEM((2 * 16 * 64, 128), F32),
-            pltpu.SemaphoreType.DMA((5,)),
+            pltpu.VMEM((XD, 256), F32),
         ],
         compiler_params=PARAMS,
         name="field",
-    )(plan, wide_d, wide_h, from_up, from_down, low, high, after, before, shaped, mask)
+    )(plan, bulk, wide_h, from_up, ends, after, before, wrap, shaped, mask)
 
     parts = lax.all_to_all(parts, "band", 0, 0)
 

time: 77 us -> 63.3 us (0.82)
  Pallas kernels: 22.6 us -> 13.9 us
  waiting for transfers between devices: 23.1 us -> 17.9 us
    pallas_call x1, Pallas kernels: 14.7 us -> 5.66 us  [local(): pl.pallas_call(field_kernel, out_shape=(shape(CX * CY, CZ), shape(4, 64,...]
    ppermute x6, waiting for transfers between devices: 17.2 us -> 11.9 us  [shifted(): lax.ppermute(block, axis, [(i, (i + distance) % n) for i in range(n)])]
    slice x2, local copies, waits for them, and re-layouts: 0.91 us -> 0.1 us  [local(): density[:DUP]]
    slice x2, local copies, waits for them, and re-layouts: 0.1 us -> 0.91 us  [local(): hartree[:HUP]]
    pallas_call x1 -> x3, Pallas kernels: 4.86 us -> 5.15 us  [the longest x1 2.5 us: local(): pl.pallas_call(inner_kernel, out_shape=(shape((CY - 2) * XD, CZ), shape((...]
  transfers between devices with their start and end apart: 7 -> 7, of which waited for: 6 -> 5; matrix products, arithmetic and copies ran while one was open for 1% -> 1% of each run, Pallas kernels for 1% -> 10%
where the time goes in v2:
time: 63.3 us; the launch traced here: 62.9 us
  starting transfers between devices  26.6 us (42%)
  waiting for transfers between devices  17.9 us (28%)
  Pallas kernels  13.9 us (22%)
  local copies, waits for them, and re-layouts  2.76 us (4%)
  between operations  1.51 us (2%)
    ppermute x6, starting transfers between devices, shifted(): lax.ppermute(block, axis, [(i, (i + distance) % n) for i in range(n)])  23.3 us
    ppermute x6, waiting for transfers between devices, shifted(): lax.ppermute(block, axis, [(i, (i + distance) % n) for i in range(n)])  11.9 us
    all_to_all x1, waiting for transfers between devices, local(): parts = lax.all_to_all(parts, 'band', 0, 0)  5.93 us
    pallas_call x1, Pallas kernels, local(): pl.pallas_call(field_kernel, out_shape=(shape(CX * CY, CZ), shape(4, 64,...  5.66 us
    all_to_all x1, starting transfers between devices, local(): parts = lax.all_to_all(parts, 'band', 0, 0)  3.33 us
    pallas_call x1, Pallas kernels, local(): pl.pallas_call(inner_kernel, out_shape=(shape((CY - 2) * XD, CZ), shape((...  2.5 us
    pallas_call x1, Pallas kernels, local(): pl.pallas_call(outer_kernel, out_shape=(shape(YH * XH, CZ), shape(4, XD,...  2.44 us
    unnamed x20, local copies, waits for them, and re-layouts  1.67 us
  transfers between devices with their start and end apart: 7, of which 5 were waited for; matrix products, arithmetic and copies ran while one was open for 1% of the time, Pallas kernels for 10%

profile of v2, /device:TPU:56, one launch (start us, length us, event | category | flops | bytes accessed | tf_op | source)
XLA Modules:
  0.0 62.9 jit_solution(8843308223710184899)
XLA Ops:
  0.6 0.0 slice-start.1
  0.6 0.0 slice-start
  0.7 0.9 %slice-done.1 = f32[15,24,128]{2,1,0:T(8,128)S(1)} async-done(((f32[32,24,128]{2,1,0:T(8,128)}), f32[15,24,128]{2,1,0:T(8,128)S(1)}, s32[]{:S(2)}) %slice-start.1) | async-done | bytes 184344 | tf_op jit(solution)/shard_map/slice | solution.py:312
  1.6 0.1 slice-done
  1.7 0.0 copy-start
  1.7 0.0 copy-start.1
  1.7 0.0 copy-start.5
  1.7 3.4 %collective-permute-start = (f32[32,24,128]{2,1,0:T(8,128)S(1)}, f32[32,24,128]{2,1,0:T(8,128)S(1)}, u32[]{:S(2)}, u32[]{:S(2)}) collective-permute-start(f32[32,24,128]{2,1,0:T(8,128)S(1)} %pad_maximum_fusion), channel_id=1, source_target_pairs={{0,112},{16,0},{32,16},{48,32},{64,48},{80,64},{96,80},{112,96},{1... | collective-permute-start | bytes 1179656 | tf_op jit(solution)/shard_map/ppermute | solution.py:34
  5.1 0.0 copy-done
  5.1 5.7 %collective-permute-start.1 = (f32[2,24,128]{2,1,0:T(8,128)S(1)}, f32[2,24,128]{2,1,0:T(8,128)S(1)}, u32[]{:S(2)}, u32[]{:S(2)}) collective-permute-start(f32[2,24,128]{2,1,0:T(8,128)S(1)} %slice.23), channel_id=1, source_target_pairs={{0,16},{16,32},{32,48},{48,64},{64,80},{80,96},{96,112},{112,0},{1... | collective-permute-start | bytes 73736 | tf_op jit(solution)/shard_map/ppermute | solution.py:34
  11.5 0.8 %collective-permute-done.1.below_ref = f32[2,24,128]{2,1,0:T(8,128)S(1)} collective-permute-done((f32[2,24,128]{2,1,0:T(8,128)S(1)}, f32[2,24,128]{2,1,0:T(8,128)S(1)}, u32[]{:S(2)}, u32[]{:S(2)}) %collective-permute-start.1) | collective-permute-done | bytes 24608 | tf_op jit(solution)/shard_map/ppermute | solution.py:34
  12.3 3.5 %collective-permute-done.above_ref = f32[32,24,128]{2,1,0:T(8,128)S(1)} collective-permute-done((f32[32,24,128]{2,1,0:T(8,128)S(1)}, f32[32,24,128]{2,1,0:T(8,128)S(1)}, u32[]{:S(2)}, u32[]{:S(2)}) %collective-permute-start) | collective-permute-done | bytes 393248 | tf_op jit(solution)/shard_map/ppermute | solution.py:34
  15.8 0.0 copy-done.1
  15.8 0.0 copy-start.8
  15.8 0.4 widen.1
  16.2 0.0 copy-start.7
  16.2 7.6 %collective-permute-start.2 = (f32[1672,128]{1,0:T(8,128)S(1)}, f32[1672,128]{1,0:T(8,128)S(1)}, u32[]{:S(2)}, u32[]{:S(2)}) collective-permute-start(f32[1672,128]{1,0:T(8,128)S(1)} %get-tuple-element.19), channel_id=1, source_target_pairs={{0,15},{1,0},{2,1},{3,2},{4,3},{5,4},{6,5},{7,6},{8,7},{9,8},{10,9... | collective-permute-start | bytes 2568200 | tf_op jit(solution)/shard_map/ppermute | solution.py:34
  23.8 0.0 copy-done.8
  23.8 0.0 copy-done.7
  23.8 0.1 fusion.pick_ref
  23.9 0.1 compare_select_fusion.mask_ref
  24.0 0.0 collective-permute-start.3
  24.0 0.0 copy-done.5
  24.0 0.0 copy-start.6
  24.0 0.0 copy-start.2
  24.1 0.5 copy.13.shape_ref
  24.5 0.3 copy-done.6
  24.8 0.0 copy-start.4
  24.9 0.2 copy-done.2
  25.1 0.6 copy-done.4
  25.7 1.1 %prep.1 = (bf16[4096,128]{1,0:T(8,128)(2,1)S(1)}, f32[64,256]{1,0:T(8,128)S(1)}) custom-call(f32[2,25,4096]{2,1,0:T(8,128)S(1)} %copy.13.shape_ref, f32[64,256]{1,0:T(8,128)S(1)} %copy-done.4, f32[2,256,256]{2,1,0:T(8,128)S(1)} %copy-done.2, f32[64,128]{1,0:T(8,128)S(1)} %fusion.pick_ref), custom_call_target="tpu_custom_call" | custom-call | tf_op jit(solution)/shard_map/prep/pallas_call | solution.py:325
  26.8 2.5 %inner.1 = (f32[1232,128]{1,0:T(8,128)S(1)}, f32[1232,128]{1,0:T(8,128)S(1)}, f32[56,256]{1,0:T(8,128)S(1)}) custom-call(f32[1344,128]{1,0:T(8,128)S(1)} %get-tuple-element.18.ed_ref), custom_call_target="tpu_custom_call" | custom-call | tf_op jit(solution)/shard_map/inner/pallas_call | solution.py:351
  29.3 0.0 collective-permute-done.3.up_ref
  29.3 4.8 %collective-permute-done.2.down_ref = f32[1672,128]{1,0:T(8,128)S(1)} collective-permute-done((f32[1672,128]{1,0:T(8,128)S(1)}, f32[1672,128]{1,0:T(8,128)S(1)}, u32[]{:S(2)}, u32[]{:S(2)}) %collective-permute-start.2) | collective-permute-done | bytes 856096 | tf_op jit(solution)/shard_map/ppermute | solution.py:34
  34.1 0.2 ends.1.ends_ref
  34.3 4.7 %collective-permute-start.4 = (f32[56,256]{1,0:T(8,128)S(1)}, f32[56,256]{1,0:T(8,128)S(1)}, u32[]{:S(2)}, u32[]{:S(2)}) collective-permute-start(f32[56,256]{1,0:T(8,128)S(1)} %ends.1.ends_ref), channel_id=1, source_target_pairs={{0,384},{128,0},{256,128},{384,256},{1,385},{129,1},{257,129},{385... | collective-permute-start | bytes 172040 | tf_op jit(solution)/shard_map/ppermute | solution.py:34
  39.0 1.9 %collective-permute-start.5 = (f32[56,256]{1,0:T(8,128)S(1)}, f32[56,256]{1,0:T(8,128)S(1)}, u32[]{:S(2)}, u32[]{:S(2)}) collective-permute-start(f32[56,256]{1,0:T(8,128)S(1)} %ends.1.ends_ref), channel_id=1, source_target_pairs={{0,128},{128,256},{256,384},{384,0},{1,129},{129,257},{257,385},{3... | collective-permute-start | bytes 172040 | tf_op jit(solution)/shard_map/ppermute | solution.py:34
  40.9 2.4 %outer.1 = (f32[1872,128]{1,0:T(8,128)S(1)}, f32[4,56,256]{2,1,0:T(8,128)S(1)}) custom-call(f32[1344,128]{1,0:T(8,128)S(1)} %get-tuple-element.18.ed_ref, f32[1672,128]{1,0:T(8,128)S(1)} %collective-permute-done.2.down_ref, f32[112,128]{1,0:T(8,128)S(1)} %collective-permute-done.3.up_ref, f32[56,256]{1,0:T(8,128)S(1)} %ends.1.ends_ref, ...), custom_call_target="tpu_custom_call" | custom-call | tf_op jit(solution)/shard_map/outer/pallas_call | solution.py:372
  43.4 0.0 collective-permute-done.4.after_ref
  43.4 2.9 %collective-permute-done.5.before_ref = f32[56,256]{1,0:T(8,128)S(1)} collective-permute-done((f32[56,256]{1,0:T(8,128)S(1)}, f32[56,256]{1,0:T(8,128)S(1)}, u32[]{:S(2)}, u32[]{:S(2)}) %collective-permute-start.5) | collective-permute-done | bytes 57376 | tf_op jit(solution)/shard_map/ppermute | solution.py:34
  46.2 0.0 copy-start.3
  46.2 5.7 %field.1 = (f32[768,128]{1,0:T(8,128)}, f32[4,64,128]{2,1,0:T(8,128)}) custom-call(s32[4,64]{1,0:T(4,128)S(1)} %pad_add_fusion.plan_ref, f32[1872,128]{1,0:T(8,128)S(1)} %get-tuple-element.24.bulk_ref, f32[1152,128]{1,0:T(8,128)S(1)} %get-tuple-element.25.eh_ref, f32[1672,128]{1,0:T(8,128)S(1)} %collective-permute-done.2.down_ref, ...), custom_call_target="tpu_custom_call" | custom-call | tf_op jit(solution)/shard_map/field/pallas_call | solution.py:387
  51.9 3.3 %all-to-all-start = ((f32[4,64,128]{2,1,0:T(8,128)}), f32[4,64,128]{2,1,0:T(8,128)S(1)}, u32[]{:S(2)}, u32[]{:S(2)}) async-start(f32[4,64,128]{2,1,0:T(8,128)} %get-tuple-element.29), calls=%async_computation | async-start | bytes 262144 | tf_op jit(solution)/shard_map/all_to_all | solution.py:401
  55.3 5.9 %all-to-all-done.parts_ref = f32[4,64,128]{2,1,0:T(8,128)S(1)} async-done(((f32[4,64,128]{2,1,0:T(8,128)}), f32[4,64,128]{2,1,0:T(8,128)S(1)}, u32[]{:S(2)}, u32[]{:S(2)}) %all-to-all-start) | async-done | bytes 131104 | tf_op jit(solution)/shard_map/all_to_all | solution.py:401
  61.2 0.1 broadcast_in_dim.2.live_ref
  61.3 0.0 copy-done.3
  61.3 1.6 %apply.1 = (f32[64,256]{1,0:T(8,128)}, f32[1024,128]{1,0:T(8,128)}) custom-call(f32[4,64,128]{2,1,0:T(8,128)S(1)} %all-to-all-done.parts_ref, f32[128,256]{1,0:T(8,128)S(1)} %bitcast.8, f32[64,256]{1,0:T(8,128)S(1)} %get-tuple-element.30.base_ref, f32[64,128]{1,0:T(8,128)S(1)} %broadcast_in_dim.2.live_ref, f32[1024,128]{1,0:T(8,128)S(1)} %bitcast.7), custom_call_target="tpu_custom_call" | custom-call | tf_op jit(solution)/shard_map/apply/pallas_call | solution.py:403
  (9 shorter events, 0.1 us)
Async XLA Ops:
  0.6 0.9 %slice-start.1 = ((f32[32,24,128]{2,1,0:T(8,128)}), f32[15,24,128]{2,1,0:T(8,128)S(1)}, s32[]{:S(2)}) async-start(f32[32,24,128]{2,1,0:T(8,128)} %hart_ref.1), calls=%async_computation.2 | async-start | bytes 368640 | tf_op jit(solution)/shard_map/slice | solution.py:312
  0.6 1.0 %slice-start = ((f32[32,24,128]{2,1,0:T(8,128)}), f32[17,24,128]{2,1,0:T(8,128)S(1)}, s32[]{:S(2)}) async-start(f32[32,24,128]{2,1,0:T(8,128)} %dens_ref.1), calls=%async_computation.1 | async-start | bytes 417792 | tf_op jit(solution)/shard_map/slice | solution.py:312
  1.7 3.4 %copy-start = (f32[32,24,128]{2,1,0:T(8,128)S(1)}, f32[32,24,128]{2,1,0:T(8,128)}, u32[]{:S(2)}) copy-start(f32[32,24,128]{2,1,0:T(8,128)} %dens_ref.1) | copy-start | bytes 1179652
  1.7 14.1 %copy-start.1 = (f32[32,24,128]{2,1,0:T(8,128)S(1)}, f32[32,24,128]{2,1,0:T(8,128)}, u32[]{:S(2)}) copy-start(f32[32,24,128]{2,1,0:T(8,128)} %hart_ref.1) | copy-start | bytes 1179652
  1.7 22.3 %copy-start.5 = (f32[2,25,4096]{2,0,1:T(2,128)S(1)}, f32[2,25,4096]{2,0,1:T(2,128)}, u32[]{:S(2)}) copy-start(f32[2,25,4096]{2,0,1:T(2,128)} %param.15) | copy-start | bytes 2457604
  1.7 14.1 %collective-permute-start = (f32[32,24,128]{2,1,0:T(8,128)S(1)}, f32[32,24,128]{2,1,0:T(8,128)S(1)}, u32[]{:S(2)}, u32[]{:S(2)}) collective-permute-start(f32[32,24,128]{2,1,0:T(8,128)S(1)} %pad_maximum_fusion), channel_id=1, source_target_pairs={{0,112},{16,0},{32,16},{48,32},{64,48},{80,64},{96,80},{112,96},{1... | collective-permute-start | bytes 1179656 | tf_op jit(solution)/shard_map/ppermute | solution.py:34
  5.1 7.2 %collective-permute-start.1 = (f32[2,24,128]{2,1,0:T(8,128)S(1)}, f32[2,24,128]{2,1,0:T(8,128)S(1)}, u32[]{:S(2)}, u32[]{:S(2)}) collective-permute-start(f32[2,24,128]{2,1,0:T(8,128)S(1)} %slice.23), channel_id=1, source_target_pairs={{0,16},{16,32},{32,48},{48,64},{64,80},{80,96},{96,112},{112,0},{1... | collective-permute-start | bytes 73736 | tf_op jit(solution)/shard_map/ppermute | solution.py:34
  15.8 8.0 %copy-start.8 = (s32[3,64]{1,0:T(4,128)S(1)}, s32[3,64]{1,0:T(4,128)}, u32[]{:S(2)}) copy-start(s32[3,64]{1,0:T(4,128)} %param.12) | copy-start | bytes 2308
  16.2 7.6 %copy-start.7 = (s32[64]{0:T(128)S(1)}, s32[64]{0:T(128)}, u32[]{:S(2)}) copy-start(s32[64]{0:T(128)} %param.13) | copy-start | bytes 772
  16.2 17.9 %collective-permute-start.2 = (f32[1672,128]{1,0:T(8,128)S(1)}, f32[1672,128]{1,0:T(8,128)S(1)}, u32[]{:S(2)}, u32[]{:S(2)}) collective-permute-start(f32[1672,128]{1,0:T(8,128)S(1)} %get-tuple-element.19), channel_id=1, source_target_pairs={{0,15},{1,0},{2,1},{3,2},{4,3},{5,4},{6,5},{7,6},{8,7},{9,8},{10,9... | collective-permute-start | bytes 2568200 | tf_op jit(solution)/shard_map/ppermute | solution.py:34
  24.0 5.3 %collective-permute-start.3 = (f32[112,128]{1,0:T(8,128)S(1)}, f32[112,128]{1,0:T(8,128)S(1)}, u32[]{:S(2)}, u32[]{:S(2)}) collective-permute-start(f32[112,128]{1,0:T(8,128)S(1)} %get-tuple-element.20), channel_id=1, source_target_pairs={{0,1},{1,2},{2,3},{3,4},{4,5},{5,6},{6,7},{7,8},{8,9},{9,10},{10,1... | collective-permute-start | bytes 172040 | tf_op jit(solution)/shard_map/ppermute | solution.py:34
  24.0 0.8 %copy-start.6 = (f32[2,25,256]{2,0,1:T(2,128)S(1)}, f32[2,25,256]{2,0,1:T(2,128)}, u32[]{:S(2)}) copy-start(f32[2,25,256]{2,0,1:T(2,128)} %param.16) | copy-start | bytes 153604
  24.0 1.1 %copy-start.2 = (f32[2,256,256]{2,1,0:T(8,128)S(1)}, f32[2,256,256]{2,1,0:T(8,128)}, u32[]{:S(2)}) copy-start(f32[2,256,256]{2,1,0:T(8,128)} %coulomb_ref.1) | copy-start | bytes 1572868
  24.8 0.9 %copy-start.4 = (f32[64,256]{1,0:T(8,128)S(1)}, f32[64,256]{1,0:T(8,128)}, u32[]{:S(2)}) copy-start(f32[64,256]{1,0:T(8,128)} %rho_ref.1) | copy-start | bytes 196612
  34.3 9.1 %collective-permute-start.4 = (f32[56,256]{1,0:T(8,128)S(1)}, f32[56,256]{1,0:T(8,128)S(1)}, u32[]{:S(2)}, u32[]{:S(2)}) collective-permute-start(f32[56,256]{1,0:T(8,128)S(1)} %ends.1.ends_ref), channel_id=1, source_target_pairs={{0,384},{128,0},{256,128},{384,256},{1,385},{129,1},{257,129},{385... | collective-permute-start | bytes 172040 | tf_op jit(solution)/shard_map/ppermute | solution.py:34
  39.0 7.3 %collective-permute-start.5 = (f32[56,256]{1,0:T(8,128)S(1)}, f32[56,256]{1,0:T(8,128)S(1)}, u32[]{:S(2)}, u32[]{:S(2)}) collective-permute-start(f32[56,256]{1,0:T(8,128)S(1)} %ends.1.ends_ref), channel_id=1, source_target_pairs={{0,128},{128,256},{256,384},{384,0},{1,129},{129,257},{257,385},{3... | collective-permute-start | bytes 172040 | tf_op jit(solution)/shard_map/ppermute | solution.py:34
  46.2 15.0 %copy-start.3 = (f32[64,16,128]{2,1,0:T(8,128)S(1)}, f32[64,16,128]{2,1,0:T(8,128)}, u32[]{:S(2)}) copy-start(f32[64,16,128]{2,1,0:T(8,128)} %param.19) | copy-start | bytes 1572868
  51.9 9.3 %all-to-all-start = ((f32[4,64,128]{2,1,0:T(8,128)}), f32[4,64,128]{2,1,0:T(8,128)S(1)}, u32[]{:S(2)}, u32[]{:S(2)}) async-start(f32[4,64,128]{2,1,0:T(8,128)} %get-tuple-element.29), calls=%async_computation | async-start | bytes 262144 | tf_op jit(solution)/shard_map/all_to_all | solution.py:401

commit v3 on v2

v3 whole, which is shorter than its diff:
```python
import math

import jax
import jax.numpy as jnp
from jax import lax
from jax.experimental import pallas as pl
from jax.experimental.pallas import tpu as pltpu
from jax.sharding import PartitionSpec as P

BOX = 16
NI = 16
NL = 25
GRID_H = 0.15
HALF = 0.5 / GRID_H
KAPPA = 0.804
MU = 0.2195149727645171
A0 = -0.75 * (3.0 / math.pi) ** (1.0 / 3.0)
C0 = 4.0 * (3.0 * math.pi**2) ** (2.0 / 3.0)

CX, CY, CZ = 32, 24, 128
LOW = 2
DUP = 17
HUP = 15
XD = 56
XH = 48
YD = CY + LOW + DUP
YH = CY + HUP
F32, BF16 = jnp.float32, jnp.bfloat16
PARAMS = pltpu.CompilerParams(vmem_limit_bytes=16 * 1024 * 1024)


def shifted(block, axis, distance):
    n = lax.axis_size(axis)
    return lax.ppermute(block, axis, [(i, (i + distance) % n) for i in range(n)])


def split(value):
    high = value.astype(BF16)
    low = (value - high.astype(F32)).astype(BF16)
    return high, low


def dot(left, right):
    return jnp.dot(left, right, preferred_element_type=F32)


def dot3(left, right):
    lh, ll = split(left)
    rh, rl = split(right)
    return dot(lh, rh) + (dot(ll, rh) + dot(lh, rl))


def column(row):
    shape = (64, 64)
    diagonal = lax.broadcasted_iota(jnp.int32, shape, 0) == lax.broadcasted_iota(jnp.int32, shape, 1)
    spread = jnp.broadcast_to(row.astype(F32), shape)
    return jnp.sum(jnp.where(diagonal, spread, 0.0), axis=1, keepdims=True)


def base_kernel(after_ref, rho_ref, coulomb_ref, kinds_ref, base_ref):
    rho = rho_ref[...]
    kind = kinds_ref[1, :, :1]
    total = jnp.zeros((64, 256), F32)
    for s in range(2):
        total = total + dot3(jnp.where(kind == s, rho, 0.0), coulomb_ref[s])
    base_ref[...] = 2.0 * total


def plan_kernel(root_ref, count_ref, rows_hbm, species_hbm, plan_ref, kinds_ref, rows_ref, species_ref, sems):
    copies = [
        pltpu.make_async_copy(rows_hbm, rows_ref, sems.at[0]),
        pltpu.make_async_copy(species_hbm, species_ref, sems.at[1]),
    ]
    for copy in copies:
        copy.start()
    first_z = lax.axis_index("band") * CZ
    count = count_ref[0]

    def step(i, found):
        for atom in [4 * i + k for k in range(4)]:
            offset = (root_ref[2, atom] - first_z) & 511
            meets = (atom < count) & ((offset < CZ) | (offset > 512 - BOX))
            plan_ref[found] = atom
            found = found + meets.astype(jnp.int32)
        return found

    plan_ref[65] = lax.fori_loop(0, (count + 3) // 4, step, 0)
    for copy in copies:
        copy.wait()
    offset = (rows_ref[2:3, :] - first_z) & 511
    live = lax.broadcasted_iota(jnp.int32, (1, 64), 1) < count_ref[0]
    meets = live & ((offset < CZ) | (offset > 512 - BOX))
    for i, here in enumerate((meets, live)):
        kinds_ref[i] = jnp.broadcast_to(column(jnp.where(here, species_ref[...], 2)), (64, 128))


def lift_kernel(dens_ref, hart_ref, low_ref, high_ref, hart_low_ref, sems):
    copies = [
        pltpu.make_async_copy(dens_ref.at[pl.ds(0, DUP)], low_ref, sems.at[0]),
        pltpu.make_async_copy(dens_ref.at[pl.ds(CX - LOW, LOW)], high_ref, sems.at[1]),
        pltpu.make_async_copy(hart_ref.at[:, pl.ds(0, 16), :], hart_low_ref, sems.at[2]),
    ]
    for copy in copies:
        copy.start()
    for copy in copies:
        copy.wait()


def widen_kernel(after_ref, dens_ref, above_ref, below_ref, ed_ref, down_ref, up_ref):
    for s in range(XD):
        x = s - LOW
        if x < 0:
            plane = below_ref[s]
        elif x < CX:
            plane = dens_ref[x]
        elif x < CX + DUP:
            plane = above_ref[x - CX]
        else:
            plane = jnp.ones((CY, CZ), F32)
        ed_ref[pl.ds(s, CY, stride=XD), :] = plane
    down_ref[...] = ed_ref[: DUP * XD]
    up_ref[...] = ed_ref[(CY - LOW) * XD :]


def turn_kernel(after1_ref, after2_ref, hart_ref, above_ref, send_ref):
    for x in range(16):
        send_ref[pl.ds(x, CY, stride=16), :] = hart_ref[x]
        send_ref[pl.ds(CY * 16 + x, 16, stride=16), :] = above_ref[x]


def packed(own, tile, lines, group):
    for line, rows in lines:
        if line // 32 == tile:
            turned = pltpu.roll(rows, (4 * (line % 32) + 2) % 128, 1)
            own = jnp.where(group == line % 32, turned, own)
    return own


def line_group():
    return lax.broadcasted_iota(jnp.int32, (XD, 128), 1) // 4


def ends_kernel(own_ref, down_ref, up_ref, ends_ref, send_ref):
    group = line_group()
    lines = [(0, up_ref[:XD]), (1, up_ref[XD:])]
    lines += [(LOW + CY + i, down_ref[i * XD : (i + 1) * XD]) for i in range(DUP)]
    tiles = []
    for tile in range(2):
        cols = pl.ds(tile * 128, 128)
        tiles.append(packed(own_ref[:, cols], tile, lines, group))
        ends_ref[:, cols] = tiles[tile]
    place = lax.broadcasted_iota(jnp.int32, (XD, 128), 1) % 4
    to_below = jnp.where(place >= 2, tiles[0], pltpu.roll(tiles[1], 126, 1))
    to_above = jnp.where(place < 2, tiles[0], pltpu.roll(tiles[1], 2, 1))
    below = (lax.axis_index("band") + 3) & 3
    for b in range(4):
        send_ref[b] = jnp.where(below == b, to_below, to_above)


def slopes(dens, sigma):
    power = jnp.log2(dens)
    root = jnp.exp2(power * (1.0 / 3.0))
    inv = jnp.exp2(power * (-4.0 / 3.0))
    scaled = sigma * (inv * inv)
    below = 1.0 + (MU / (KAPPA * C0)) * scaled
    t = pl.reciprocal(below, approx=True)
    t = t * (2.0 - below * t)
    tt = t * t
    slope_s = (A0 * MU / C0) * (inv * tt)
    slope_n = root * (
        (A0 * 4.0 / 3.0 * (1.0 + KAPPA) - (A0 * 4.0 / 3.0 * KAPPA) * t)
        - (A0 * 8.0 / 3.0 * MU / C0) * (scaled * tt)
    )
    return slope_n, slope_s


def line_flux(center, x_up, x_down, y_up, y_down):
    gx = (x_up - x_down) * HALF
    gy = (y_up - y_down) * HALF
    gz = (pltpu.roll(center, 127, 1) - pltpu.roll(center, 1, 1)) * HALF
    slope_n, slope_s = slopes(center, gx * gx + gy * gy + gz * gz)
    fx, fy, fz = slope_s * gx, slope_s * gy, slope_s * gz
    spread = (pltpu.roll(fx, XD - 1, 0) - pltpu.roll(fx, 1, 0)) + (
        pltpu.roll(fz, 127, 1) - pltpu.roll(fz, 1, 1)
    )
    return slope_n - (2.0 * HALF) * spread, fy


def flux_lines(source, first, count, local_ref, flux_ref, target):
    def step(i, carry):
        base = pl.multiple_of((first + i) * XD, 8)
        goal = pl.ds(pl.multiple_of((target + i) * XD, 8), XD)
        part, flux = line_flux(
            source[pl.ds(base, XD), :],
            source[pl.ds(base + 1, XD), :],
            source[pl.ds(base - 1, XD), :],
            source[pl.ds(pl.multiple_of(base + XD, 8), XD), :],
            source[pl.ds(pl.multiple_of(base - XD, 8), XD), :],
        )
        local_ref[goal, :] = part
        flux_ref[goal, :] = flux
        return carry

    lax.fori_loop(0, count, step, 0, unroll=2)


def packed_flux(dens):
    gx = (pltpu.roll(dens, XD - 1, 0) - pltpu.roll(dens, 1, 0)) * HALF
    gy = (pltpu.roll(dens, 252, 1) - pltpu.roll(dens, 4, 1)) * HALF
    gz = (pltpu.roll(dens, 255, 1) - pltpu.roll(dens, 1, 1)) * HALF
    slope_n, slope_s = slopes(dens, gx * gx + gy * gy + gz * gz)
    return slope_n, slope_s * gx, slope_s * gy, slope_s * gz


def bulk_lines(part, flux, first, count, bulk_ref):
    def step(i, carry):
        base = (first + i) * XD + LOW
        spread = flux[pl.ds(base + XD, XH), :] - flux[pl.ds(base - XD, XH), :]
        goal = pl.ds(pl.multiple_of(i * XH, 8), XH)
        bulk_ref[goal, :] = part[pl.ds(base, XH), :] - (2.0 * HALF) * spread
        return carry

    lax.fori_loop(0, count, step, 0, unroll=2)


def inner_kernel(ed_ref, bulk_ref, tail_ref, ends_ref, part, flux):
    group = line_group()
    lines = [(LOW + i, ed_ref[i * XD : (i + 1) * XD]) for i in range(CY)]
    for tile in range(2):
        ends_ref[:, pl.ds(tile * 128, 128)] = packed(jnp.ones((XD, 128), F32), tile, lines, group)
    flux_lines(ed_ref, 1, 22, part, flux, 0)
    bulk_lines(part, flux, 1, 20, bulk_ref)
    tail_ref[: 2 * XD] = flux[: 2 * XD]
    tail_ref[2 * XD : 4 * XD] = flux[20 * XD :]
    tail_ref[4 * XD : 5 * XD] = part[:XD]
    tail_ref[5 * XD : 6 * XD] = part[21 * XD :]
    tail_ref[6 * XD : 8 * XD] = ed_ref[: 2 * XD]
    tail_ref[8 * XD :] = ed_ref[22 * XD :]


def outer_kernel(down_ref, up_ref, tail_ref, ends_ref, bulk_ref, wrap_ref, near, near_part, near_flux, far, part, flux):
    near[: 2 * XD] = up_ref[...]
    near[2 * XD :] = tail_ref[6 * XD : 8 * XD]
    near_flux[2 * XD :] = tail_ref[: 2 * XD]
    near_part[2 * XD :] = tail_ref[4 * XD : 5 * XD]
    far[: 2 * XD] = tail_ref[8 * XD :]
    far[2 * XD :] = down_ref[...]
    flux[: 2 * XD] = tail_ref[2 * XD : 4 * XD]
    part[XD : 2 * XD] = tail_ref[5 * XD : 6 * XD]
    flux_lines(near, 1, 2, near_part, near_flux, 0)
    flux_lines(far, 1, DUP, part, flux, 2)
    bulk_lines(near_part, near_flux, 1, 2, bulk_ref.at[pl.ds(0, 2 * XH)])
    bulk_lines(part, flux, 1, DUP, bulk_ref.at[pl.ds(2 * XH, DUP * XH)])
    for i, value in enumerate(packed_flux(ends_ref[...])):
        wrap_ref[i] = value


def field_kernel(
    root_ref, plan_ref,
    hart_ref, cells_ref,
    hart_above, hart_right, bulk1_ref, bulk2_ref, ends_ref, beside_ref, wrap_ref, kinds_ref,
    field, part_ref,
    hart, cells, windows, fixes, sems,
):
    copies = [
        pltpu.make_async_copy(hart_ref, hart, sems.at[0]),
        pltpu.make_async_copy(cells_ref, cells, sems.at[1]),
    ]
    for copy in copies:
        copy.start()
    place = lax.broadcasted_iota(jnp.int32, (XD, 256), 1) % 4
    middle = (place == 1) | (place == 2)
    low = place < 2
    own = ends_ref[...]

    def fix(dens):
        dn, dx, dy, dz = [
            jnp.where(middle, value - wrap_ref[i], 0.0) for i, value in enumerate(packed_flux(dens))
        ]
        spread = (
            (pltpu.roll(dx, XD - 1, 0) - pltpu.roll(dx, 1, 0))
            + (pltpu.roll(dy, 252, 1) - pltpu.roll(dy, 4, 1))
            + (pltpu.roll(dz, 255, 1) - pltpu.roll(dz, 1, 1))
        )
        return dn - (2.0 * HALF) * spread

    band = lax.axis_index("band")
    after = beside_ref[(band + 1) & 3]
    before = beside_ref[(band + 3) & 3]
    after = jnp.concatenate([after, pltpu.roll(after, 2, 1)], axis=1)
    before = jnp.concatenate([before, pltpu.roll(before, 126, 1)], axis=1)
    top = fix(jnp.where(low, own, after))
    bottom = fix(jnp.where(low, before, own))
    fixes[...] = jnp.where(low, top, bottom)

    lane = lax.broadcasted_iota(jnp.int32, (XH, 128), 1)
    edge = (lane < 2) | (lane >= 126)
    tiles = [fixes[pl.ds(LOW, XH), pl.ds(t * 128, 128)] for t in range(2)]

    copies[0].wait()
    for y in range(YH):
        line = y + LOW
        turned = pltpu.roll(tiles[line // 32], (254 - 4 * (line % 32)) % 128, 1)
        if y < CY:
            own = hart[pl.ds(y, CX, stride=CY), :]
        else:
            own = hart_above[pl.ds(y - CY, CX, stride=16), :]
        source = jnp.concatenate([own, hart_right[pl.ds(y * 16, 16), :]], axis=0)
        if 2 <= y < 22:
            bulk = bulk1_ref[pl.ds((y - 2) * XH, XH), :]
        else:
            bulk = bulk2_ref[pl.ds((y if y < 2 else y - 20) * XH, XH), :]
        field[pl.ds(y * XH, XH), :] = (source + bulk) + jnp.where(edge, turned, 0.0)

    step_z = lax.broadcasted_iota(jnp.int32, (16, 128), 1)
    group = step_z // 16
    step_z = step_z % 16
    count = plan_ref[65]
    first_x, first_y = lax.axis_index("dx") * CX, lax.axis_index("dyz") * CY
    first_z = band * CZ

    def window(atom):
        rx, ry, rz = root_ref[0, atom] - first_x, root_ref[1, atom] - first_y, root_ref[2, atom] - first_z
        shift = 128 - (rz & 127)
        inside = ((step_z + rz) & 511) < 128
        halves = []
        for jh in range(2):
            value = jnp.zeros((16, 128), F32)
            for jl in range(8):
                rows = field[pl.ds((ry + (jh * 8 + jl)) * XH + rx, 16), :]
                turned = pltpu.roll(rows, (shift + jl * 16) & 127, 1)
                value = jnp.where(group == jl, turned, value)
            halves.append(jnp.where(inside, value, 0.0))
        return halves

    def atom_step(i, carry):
        items = [2 * i, jnp.minimum(2 * i + 1, count - 1)]
        atoms = [plan_ref[item] for item in items]
        values = [window(atom) for atom in atoms]
        for atom, halves in zip(atoms, values):
            for jh in range(2):
                windows[pl.ds(atom + jh * 1024, 16, stride=64), :] = halves[jh]
        return carry

    lax.fori_loop(0, (count + 1) // 2, atom_step, 0)

    copies[1].wait()
    pad = jnp.zeros((7, 128), F32)
    total = jnp.zeros((128, 128), F32)
    for i in range(16):
        rows = [windows[pl.ds(jh * 1024 + i * 64, 64), :] for jh in range(2)]
        high, low = split(jnp.concatenate(rows, axis=1))
        both = jnp.concatenate([high, low], axis=0)
        shaped = []
        for c in (2 * i, 2 * i + 1):
            first, second = [cells[pl.ds(2 * c + s, NL, stride=64), :] for s in range(2)]
            shaped.append(jnp.concatenate([first, pad, second, pad], axis=0))
        shaped = jnp.concatenate(split(jnp.concatenate(shaped, axis=1)), axis=0)
        total = total + lax.dot_general(both, shaped, (((1,), (1,)), ((), ())), preferred_element_type=F32)
    total = (total[:64] + total[64:]) * GRID_H**3
    total = total + pltpu.roll(total, 64, 1)
    kind = kinds_ref[0]
    moments = jnp.where(kind == 0, total, 0.0) + jnp.where(kind == 1, pltpu.roll(total, 96, 1), 0.0)
    moments = jnp.where(lax.broadcasted_iota(jnp.int32, (64, 128), 1) < 32, moments, 0.0)
    joined = moments[:16]
    for g in range(1, 4):
        joined = joined + pltpu.roll(moments[g * 16 : g * 16 + 16], 32 * g, 1)
    for b in range(4):
        part_ref[b] = joined


def own_kernel(field_ref, out_ref):
    for y in range(CY):
        out_ref[pl.ds(y, CX, stride=CY), :] = field_ref[pl.ds(y * XH, CX), :]


def apply_kernel(
    parts_ref, coupling_ref, base_ref, kinds_ref, proj_ref, ham_ref, out_ref, spread_ref
):
    kind = kinds_ref[1]
    joined = (parts_ref[0] + parts_ref[1]) + (parts_ref[2] + parts_ref[3])
    rows = [joined] + [pltpu.roll(joined, 128 - 32 * g, 1) for g in range(1, 4)]
    moments = jnp.concatenate(rows, axis=0)
    moments = jnp.where(lax.broadcasted_iota(jnp.int32, (64, 128), 1) < 32, moments, 0.0)
    moments = jnp.where(kind == 0, moments, jnp.where(kind == 1, pltpu.roll(moments, 32, 1), 0.0))
    pad = jnp.zeros((7, 256), F32)
    tensors = jnp.concatenate([coupling_ref[0], pad, coupling_ref[1], pad, jnp.zeros((64, 256), F32)], axis=0)
    ham = jnp.where(kind[:, :1] < 2, dot3(moments, tensors) + base_ref[...], 0.0)
    ham_ref[...] = ham
    lane = lax.broadcasted_iota(jnp.int32, (64, 128), 1)
    row = lax.broadcasted_iota(jnp.int32, (64, 128), 0)
    mine = (lane // 16) == (row % 8)
    halves = [pltpu.roll(ham[:, s : s + 128], 0, 1, stride=16, stride_axis=0) for s in (0, 128)]
    for i in range(16):
        placed = halves[i // 8]
        if i % 8:
            placed = pltpu.roll(placed, 128 - (i % 8) * 16, 1)
        spread_ref[pl.ds(i, 64, stride=16), :] = jnp.where(mine, placed, 0.0)
    for g in range(8):
        rows = pl.ds(g * 128, 128)
        out_ref[rows, :] = dot3(spread_ref[rows, :], proj_ref[rows, :])


def far(value):
    return pltpu.with_memory_space_constraint(value, pltpu.HBM)


def close(value):
    return pltpu.with_memory_space_constraint(value, pltpu.VMEM)


def vmem(count):
    return [pl.BlockSpec(memory_space=pltpu.VMEM)] * count


def anywhere(count):
    return [pl.BlockSpec(memory_space=pl.ANY)] * count


def hbm(count):
    return [pl.BlockSpec(memory_space=pltpu.HBM)] * count


def smem(count):
    return [pl.BlockSpec(memory_space=pltpu.SMEM)] * count


def call(kernel, name, outs, specs, scratch=()):
    return pl.pallas_call(
        kernel,
        out_shape=outs,
        in_specs=specs,
        out_specs=tuple(vmem(len(outs))),
        scratch_shapes=list(scratch),
        compiler_params=PARAMS,
        name=name,
    )


def shape(*dims, dtype=F32):
    return jax.ShapeDtypeStruct(dims, dtype)


def local(
    density, hartree, box_root, species, atom_count, shape_functions, coupling, coulomb, rho_ij, projections
):
    slots = box_root.shape[1]

    dens_low, dens_high, hart_low = call(
        lift_kernel,
        "lift",
        (shape(DUP, CY, CZ), shape(LOW, CY, CZ), shape(CX, 16, CZ)),
        hbm(2),
        [pltpu.SemaphoreType.DMA((3,))],
    )(far(density), far(hartree))
    below = shifted(dens_high, "dx", 1)
    above = shifted(dens_low, "dx", -1)
    hart_above = shifted(hart_low, "dyz", -1)

    plan, kinds = pl.pallas_call(
        plan_kernel,
        out_shape=(shape(66, dtype=jnp.int32), shape(2, 64, 128)),
        in_specs=smem(2) + hbm(2),
        out_specs=(smem(1)[0], vmem(1)[0]),
        scratch_shapes=[
            pltpu.VMEM((3, 64), jnp.int32),
            pltpu.VMEM((1, 64), jnp.int32),
            pltpu.SemaphoreType.DMA((2,)),
        ],
        compiler_params=PARAMS,
        name="plan",
    )(box_root, atom_count, far(box_root), far(species.reshape(1, slots)))
    wide_d, send_down, send_up = call(
        widen_kernel,
        "widen",
        (shape(CY * XD, CZ), shape(DUP * XD, CZ), shape(LOW * XD, CZ)),
        anywhere(1) + vmem(3),
    )(close(kinds), density, above, below)
    from_up = shifted(send_down, "dyz", -1)
    from_down = shifted(send_up, "dyz", 1)

    bulk1, tail, own_ends = call(
        inner_kernel,
        "inner",
        (shape(20 * XH, CZ), shape(10 * XD, CZ), shape(XD, 256)),
        vmem(1),
        [pltpu.VMEM((22 * XD, CZ), F32), pltpu.VMEM((22 * XD, CZ), F32)],
    )(wide_d)
    send_right = call(turn_kernel, "turn", (shape(40 * 16, CZ),), anywhere(2) + vmem(2))(
        close(from_down), close(own_ends), hartree, hart_above
    )[0]
    hart_right = shifted(send_right, "dx", -1)

    ends, send_ends = call(ends_kernel, "ends", (shape(XD, 256), pltpu.VMEM((4, XD, 128), F32)), vmem(3))(
        close(own_ends), close(from_up), close(from_down)
    )

    beside = lax.all_to_all(send_ends, "band", 0, 0)
    cells = shape_functions.transpose(1, 0, 2).reshape(NL, 2, 32, 128).transpose(0, 2, 1, 3).reshape(NL * 64, 128)
    bulk2, wrap = call(
        outer_kernel,
        "outer",
        (shape(19 * XH, CZ), shape(4, XD, 256)),
        vmem(4),
        [pltpu.VMEM((n * XD, CZ), F32) for n in (4, 3, 4, 19, 19, 19)],
    )(close(from_up), close(from_down), close(tail), close(ends))

    field, parts = call(
        field_kernel,
        "field",
        (pltpu.VMEM((YH * XH, CZ), F32), pltpu.VMEM((4, 16, 128), F32)),
        smem(2) + hbm(2) + vmem(8),
        [
            pltpu.VMEM((CX * CY, CZ), F32),
            pltpu.VMEM((NL * 64, 128), F32),
            pltpu.VMEM((2 * 16 * 64, 128), F32),
            pltpu.VMEM((XD, 256), F32),
            pltpu.SemaphoreType.DMA((2,)),
        ],
    )(
        box_root, plan,
        far(hartree.reshape(CX * CY, CZ)), far(cells),
        close(hart_above.reshape(CX * 16, CZ)), close(hart_right), close(bulk1), close(bulk2), close(ends), close(beside), close(wrap), close(kinds),
    )

    summed = lax.all_to_all(parts, "band", 0, 0)
    potential = call(own_kernel, "own", (shape(CX * CY, CZ),), vmem(1))(field)[0]
    base = call(base_kernel, "base", (shape(64, 256),), anywhere(1) + vmem(3))(
        parts, rho_ij, coulomb, kinds
    )[0]
    atom_hamiltonian, applied = call(
        apply_kernel,
        "apply",
        (shape(64, 256), shape(64 * NI, 128)),
        vmem(5),
        [pltpu.VMEM((64 * NI, 128), F32)],
    )(summed, coupling, base, kinds, projections.reshape(slots * NI, CZ))
    return (
        potential.reshape(CX, CY, CZ),
        atom_hamiltonian,
        applied.reshape(slots, NI, CZ),
    )


def solution(mesh):
    in_specs = (
        P("dx", "dyz", "band"),
        P("dx", "dyz", "band"),
        P(None, ("dx", "dyz")),
        P(("dx", "dyz")),
        P(("dx", "dyz")),
        P(),
        P(),
        P(),
        P(("dx", "dyz"), None),
        P(("dx", "dyz"), None, "band"),
    )
    out_specs = (P("dx", "dyz", "band"), P(("dx", "dyz"), None), P(("dx", "dyz"), None, "band"))
    return jax.shard_map(local, mesh=mesh, in_specs=in_specs, out_specs=out_specs, check_vma=False)
```

time: 63.3 us -> 57.5 us (0.908)
  the two profiles are of different devices: /device:TPU:56 before, /device:TPU:2 now
where the time goes in v3:
time: 57.5 us; the launch traced here: 56.9 us
  starting transfers between devices  31.4 us (55%)
  Pallas kernels  16.2 us (28%)
  waiting for transfers between devices  6.74 us (12%)
  between operations  1.46 us (3%)
  local copies, waits for them, and re-layouts  1.04 us (2%)
    ppermute x6, starting transfers between devices, shifted(): lax.ppermute(block, axis, [(i, (i + distance) % n) for i in range(n)])  21.6 us
    all_to_all x1, starting transfers between devices, local(): summed = lax.all_to_all(parts, 'band', 0, 0)  4.99 us
    all_to_all x1, starting transfers between devices, local(): beside = lax.all_to_all(send_ends, 'band', 0, 0)  4.82 us
    pallas_call x1, Pallas kernels, local(): call(field_kernel, 'field', (pltpu.VMEM((YH * XH, CZ), F32), pltpu.VMEM((...  4.02 us
    pallas_call x1, Pallas kernels, local(): call(inner_kernel, 'inner', (shape(20 * XH, CZ), shape(10 * XD, CZ), shap...  2.67 us
    all_to_all x1, waiting for transfers between devices, local(): summed = lax.all_to_all(parts, 'band', 0, 0)  2.52 us
    pallas_call x1, Pallas kernels, local(): call(outer_kernel, 'outer', (shape(19 * XH, CZ), shape(4, XD, 256)), vmem...  2.33 us
    ppermute x6, waiting for transfers between devices, shifted(): lax.ppermute(block, axis, [(i, (i + distance) % n) for i in range(n)])  2.13 us
  transfers between devices with their start and end apart: 8, of which 3 were waited for; matrix products, arithmetic and copies ran while one was open for 0% of the time, Pallas kernels for 16%

profile of v3, /device:TPU:2, one launch (start us, length us, event | category | flops | bytes accessed | tf_op | source)
XLA Modules:
  0.0 56.9 jit_solution(1051146637009366295)
XLA Ops:
  0.6 0.0 copy-start.1
  0.6 1.1 %lift.1 = (f32[17,24,128]{2,1,0:T(8,128)S(1)}, f32[2,24,128]{2,1,0:T(8,128)S(1)}, f32[32,16,128]{2,1,0:T(8,128)S(1)}) custom-call(f32[32,24,128]{2,1,0:T(8,128)} %dens_ref.3, f32[32,24,128]{2,1,0:T(8,128)} %hart_ref.3), custom_call_target="tpu_custom_call" | custom-call | tf_op jit(solution)/shard_map/lift/pallas_call | solution.py:449
  1.8 5.4 %collective-permute-start.1 = (f32[17,24,128]{2,1,0:T(8,128)S(1)}, f32[17,24,128]{2,1,0:T(8,128)S(1)}, u32[]{:S(2)}, u32[]{:S(2)}) collective-permute-start(f32[17,24,128]{2,1,0:T(8,128)S(1)} %get-tuple-element.25), channel_id=1, source_target_pairs={{0,112},{16,0},{32,16},{48,32},{64,48},{80,64},{96,80},{112,96},{1... | collective-permute-start | bytes 626696 | tf_op jit(solution)/shard_map/ppermute | solution.py:34
  7.2 1.9 %collective-permute-start.2 = (f32[2,24,128]{2,1,0:T(8,128)S(1)}, f32[2,24,128]{2,1,0:T(8,128)S(1)}, u32[]{:S(2)}, u32[]{:S(2)}) collective-permute-start(f32[2,24,128]{2,1,0:T(8,128)S(1)} %get-tuple-element.26), channel_id=1, source_target_pairs={{0,16},{16,32},{32,48},{48,64},{64,80},{80,96},{96,112},{112,0},{1... | collective-permute-start | bytes 73736 | tf_op jit(solution)/shard_map/ppermute | solution.py:34
  9.1 8.2 %collective-permute-start = (f32[32,16,128]{2,1,0:T(8,128)S(1)}, f32[32,16,128]{2,1,0:T(8,128)S(1)}, u32[]{:S(2)}, u32[]{:S(2)}) collective-permute-start(f32[32,16,128]{2,1,0:T(8,128)S(1)} %get-tuple-element.23), channel_id=1, source_target_pairs={{0,15},{1,0},{2,1},{3,2},{4,3},{5,4},{6,5},{7,6},{8,7},{9,8},{10,9... | collective-permute-start | bytes 786440 | tf_op jit(solution)/shard_map/ppermute | solution.py:34
  18.0 2.0 %plan.1 = (s32[66]{0:T(128)S(1)}, f32[2,64,128]{2,1,0:T(8,128)S(1)}) custom-call(s32[3,64]{1,0:T(4,128)} %root_ref.3, s32[1]{0:T(128)S(6)} %copy.15.count_ref, s32[3,64]{1,0:T(4,128)} %root_ref.3, s32[1,64]{1,0:T(1,128)} %bitcast.18), custom_call_target="tpu_custom_call" | custom-call | tf_op jit(solution)/shard_map/plan/pallas_call | solution.py:460
  20.0 0.0 collective-permute-done.2.below_ref
  20.0 0.0 collective-permute-done.1.above_ref
  20.0 0.0 copy-done.1
  20.0 0.1 widen.1
  20.1 0.0 copy-start
  20.2 1.2 %collective-permute-start.5 = (f32[952,128]{1,0:T(8,128)S(1)}, f32[952,128]{1,0:T(8,128)S(1)}, u32[]{:S(2)}, u32[]{:S(2)}) collective-permute-start(f32[952,128]{1,0:T(8,128)S(1)} %get-tuple-element.31), channel_id=1, source_target_pairs={{0,15},{1,0},{2,1},{3,2},{4,3},{5,4},{6,5},{7,6},{8,7},{9,8},{10,9... | collective-permute-start | bytes 1462280 | tf_op jit(solution)/shard_map/ppermute | solution.py:34
  21.3 0.0 collective-permute-start.3
  21.3 2.7 %inner.1 = (f32[960,128]{1,0:T(8,128)S(1)}, f32[560,128]{1,0:T(8,128)S(1)}, f32[56,256]{1,0:T(8,128)S(1)}) custom-call(f32[1344,128]{1,0:T(8,128)S(1)} %get-tuple-element.28.ed_ref), custom_call_target="tpu_custom_call" | custom-call | tf_op jit(solution)/shard_map/inner/pallas_call | solution.py:482
  24.0 0.0 collective-permute-done.above_ref
  24.0 2.1 %collective-permute-done.3.after1_ref.up_ref = f32[112,128]{1,0:T(8,128)S(1)} collective-permute-done((f32[112,128]{1,0:T(8,128)S(1)}, f32[112,128]{1,0:T(8,128)S(1)}, u32[]{:S(2)}, u32[]{:S(2)}) %collective-permute-start.3) | collective-permute-done | bytes 57376 | tf_op jit(solution)/shard_map/ppermute | solution.py:34
  26.1 0.0 copy-done
  26.1 0.1 turn.1
  26.3 4.9 %collective-permute-start.4 = (f32[640,128]{1,0:T(8,128)S(1)}, f32[640,128]{1,0:T(8,128)S(1)}, u32[]{:S(2)}, u32[]{:S(2)}) collective-permute-start(f32[640,128]{1,0:T(8,128)S(1)} %turn.1), channel_id=1, source_target_pairs={{0,112},{16,0},{32,16},{48,32},{64,48},{80,64},{96,80},{112,96},{1... | collective-permute-start | bytes 983048 | tf_op jit(solution)/shard_map/ppermute | solution.py:34
  31.2 0.0 collective-permute-done.5.down_ref
  31.2 0.9 %ends.1 = (f32[56,256]{1,0:T(8,128)S(1)}, f32[4,56,128]{2,1,0:T(8,128)}) custom-call(f32[56,256]{1,0:T(8,128)S(1)} %get-tuple-element.29.after2_ref.own_ref, f32[952,128]{1,0:T(8,128)S(1)} %collective-permute-done.5.down_ref, f32[112,128]{1,0:T(8,128)S(1)} %collective-permute-done.3.after1_ref.up_ref), custom_call_target="tpu_custom_call" | custom-call | tf_op jit(solution)/shard_map/ends/pallas_call | solution.py:494
  32.2 4.8 %all-to-all-start = ((f32[4,56,128]{2,1,0:T(8,128)}), f32[4,56,128]{2,1,0:T(8,128)S(1)}, u32[]{:S(2)}, u32[]{:S(2)}) async-start(f32[4,56,128]{2,1,0:T(8,128)} %get-tuple-element.35), calls=%async_computation | async-start | bytes 229376 | tf_op jit(solution)/shard_map/all_to_all | solution.py:498
  37.0 2.3 %outer.1 = (f32[912,128]{1,0:T(8,128)S(1)}, f32[4,56,256]{2,1,0:T(8,128)S(1)}) custom-call(f32[952,128]{1,0:T(8,128)S(1)} %collective-permute-done.5.down_ref, f32[112,128]{1,0:T(8,128)S(1)} %collective-permute-done.3.after1_ref.up_ref, f32[560,128]{1,0:T(8,128)S(1)} %get-tuple-element.32.tail_ref, f32[56,256]{1,0:T(8,128)S(1)} %get-tuple-element.33.ends_ref), custom_call_target="tpu_custom_call" | custom-call | tf_op jit(solution)/shard_map/outer/pallas_call | solution.py:500
  39.3 0.0 collective-permute-done.4.hart_right
  39.3 2.1 %all-to-all-done.beside_ref = f32[4,56,128]{2,1,0:T(8,128)S(1)} async-done(((f32[4,56,128]{2,1,0:T(8,128)}), f32[4,56,128]{2,1,0:T(8,128)S(1)}, u32[]{:S(2)}, u32[]{:S(2)}) %all-to-all-start) | async-done | bytes 114720 | tf_op jit(solution)/shard_map/all_to_all | solution.py:498
  41.4 0.0 copy-start.5
  41.4 0.7 %copy-done.5 = s32[3,64]{1,0:T(4,128)S(1)} copy-done((s32[3,64]{1,0:T(4,128)S(1)}, s32[3,64]{1,0:T(4,128)}, u32[]{:S(2)}) %copy-start.5) | copy-done | bytes 792
  42.1 4.0 %field.1 = (f32[1872,128]{1,0:T(8,128)S(1)}, f32[4,16,128]{2,1,0:T(8,128)}) custom-call(s32[3,64]{1,0:T(4,128)S(1)} %copy-done.5, s32[66]{0:T(128)S(1)} %get-tuple-element.22.plan_ref, f32[768,128]{1,0:T(8,128)} %bitcast.13, f32[1600,128]{1,0:T(8,128)} %bitcast.16, f32[512,128]{1,0:T(8,128)S(1)} %bitcast.14, ...), custom_call_target="tpu_custom_call" | custom-call | tf_op jit(solution)/shard_map/field/pallas_call | solution.py:508
  46.1 0.0 copy-start.6
  46.2 5.0 %all-to-all-start.1 = ((f32[4,16,128]{2,1,0:T(8,128)}), f32[4,16,128]{2,1,0:T(8,128)S(1)}, u32[]{:S(2)}, u32[]{:S(2)}) async-start(f32[4,16,128]{2,1,0:T(8,128)} %get-tuple-element.38.after_ref), calls=%async_computation.1 | async-start | bytes 65536 | tf_op jit(solution)/shard_map/all_to_all | solution.py:526
  51.1 0.0 copy-done.6
  51.2 0.0 copy-start.2
  51.2 0.0 copy-start.4
  51.2 0.8 %own.1 = f32[768,128]{1,0:T(8,128)} custom-call(f32[1872,128]{1,0:T(8,128)S(1)} %get-tuple-element.37.field_ref), custom_call_target="tpu_custom_call" | custom-call | tf_op jit(solution)/shard_map/own/pallas_call | solution.py:527
  52.0 0.3 copy-done.2
  52.3 0.0 copy-done.4
  52.3 0.0 copy-start.3
  52.3 0.3 base.1.base_ref
  52.6 2.5 %all-to-all-done.1.parts_ref = f32[4,16,128]{2,1,0:T(8,128)S(1)} async-done(((f32[4,16,128]{2,1,0:T(8,128)}), f32[4,16,128]{2,1,0:T(8,128)S(1)}, u32[]{:S(2)}, u32[]{:S(2)}) %all-to-all-start.1) | async-done | bytes 32800 | tf_op jit(solution)/shard_map/all_to_all | solution.py:526
  55.1 0.0 copy-done.3
  55.1 1.8 %apply.1 = (f32[64,256]{1,0:T(8,128)}, f32[1024,128]{1,0:T(8,128)}) custom-call(f32[4,16,128]{2,1,0:T(8,128)S(1)} %all-to-all-done.1.parts_ref, f32[2,25,256]{2,1,0:T(8,128)S(1)} %copy.14.coupling_ref, f32[64,256]{1,0:T(8,128)S(1)} %base.1.base_ref, f32[2,64,128]{2,1,0:T(8,128)S(1)} %get-tuple-element.24.after_ref.kinds_ref, f32[1024,128]{1,0:T(8,128)S(1)} %bitcast.15), custom_call_target="tpu_custom_call" | custom-call | tf_op jit(solution)/shard_map/apply/pallas_call | solution.py:531
  (1 shorter events, 0.0 us)
Async XLA Ops:
  0.6 19.4 %copy-start.1 = (f32[32,24,128]{2,1,0:T(8,128)S(1)}, f32[32,24,128]{2,1,0:T(8,128)}, u32[]{:S(2)}) copy-start(f32[32,24,128]{2,1,0:T(8,128)} %dens_ref.3) | copy-start | bytes 1179652
  1.8 18.2 %collective-permute-start.1 = (f32[17,24,128]{2,1,0:T(8,128)S(1)}, f32[17,24,128]{2,1,0:T(8,128)S(1)}, u32[]{:S(2)}, u32[]{:S(2)}) collective-permute-start(f32[17,24,128]{2,1,0:T(8,128)S(1)} %get-tuple-element.25), channel_id=1, source_target_pairs={{0,112},{16,0},{32,16},{48,32},{64,48},{80,64},{96,80},{112,96},{1... | collective-permute-start | bytes 626696 | tf_op jit(solution)/shard_map/ppermute | solution.py:34
  7.2 12.8 %collective-permute-start.2 = (f32[2,24,128]{2,1,0:T(8,128)S(1)}, f32[2,24,128]{2,1,0:T(8,128)S(1)}, u32[]{:S(2)}, u32[]{:S(2)}) collective-permute-start(f32[2,24,128]{2,1,0:T(8,128)S(1)} %get-tuple-element.26), channel_id=1, source_target_pairs={{0,16},{16,32},{32,48},{48,64},{64,80},{80,96},{96,112},{112,0},{1... | collective-permute-start | bytes 73736 | tf_op jit(solution)/shard_map/ppermute | solution.py:34
  9.1 14.9 %collective-permute-start = (f32[32,16,128]{2,1,0:T(8,128)S(1)}, f32[32,16,128]{2,1,0:T(8,128)S(1)}, u32[]{:S(2)}, u32[]{:S(2)}) collective-permute-start(f32[32,16,128]{2,1,0:T(8,128)S(1)} %get-tuple-element.23), channel_id=1, source_target_pairs={{0,15},{1,0},{2,1},{3,2},{4,3},{5,4},{6,5},{7,6},{8,7},{9,8},{10,9... | collective-permute-start | bytes 786440 | tf_op jit(solution)/shard_map/ppermute | solution.py:34
  20.1 6.0 %copy-start = (f32[32,24,128]{2,1,0:T(8,128)S(1)}, f32[32,24,128]{2,1,0:T(8,128)}, u32[]{:S(2)}) copy-start(f32[32,24,128]{2,1,0:T(8,128)} %hart_ref.3) | copy-start | bytes 1179652
  20.2 11.1 %collective-permute-start.5 = (f32[952,128]{1,0:T(8,128)S(1)}, f32[952,128]{1,0:T(8,128)S(1)}, u32[]{:S(2)}, u32[]{:S(2)}) collective-permute-start(f32[952,128]{1,0:T(8,128)S(1)} %get-tuple-element.31), channel_id=1, source_target_pairs={{0,15},{1,0},{2,1},{3,2},{4,3},{5,4},{6,5},{7,6},{8,7},{9,8},{10,9... | collective-permute-start | bytes 1462280 | tf_op jit(solution)/shard_map/ppermute | solution.py:34
  21.3 4.8 %collective-permute-start.3 = (f32[112,128]{1,0:T(8,128)S(1)}, f32[112,128]{1,0:T(8,128)S(1)}, u32[]{:S(2)}, u32[]{:S(2)}) collective-permute-start(f32[112,128]{1,0:T(8,128)S(1)} %get-tuple-element.27), channel_id=1, source_target_pairs={{0,1},{1,2},{2,3},{3,4},{4,5},{5,6},{6,7},{7,8},{8,9},{9,10},{10,1... | collective-permute-start | bytes 172040 | tf_op jit(solution)/shard_map/ppermute | solution.py:34
  26.3 13.0 %collective-permute-start.4 = (f32[640,128]{1,0:T(8,128)S(1)}, f32[640,128]{1,0:T(8,128)S(1)}, u32[]{:S(2)}, u32[]{:S(2)}) collective-permute-start(f32[640,128]{1,0:T(8,128)S(1)} %turn.1), channel_id=1, source_target_pairs={{0,112},{16,0},{32,16},{48,32},{64,48},{80,64},{96,80},{112,96},{1... | collective-permute-start | bytes 983048 | tf_op jit(solution)/shard_map/ppermute | solution.py:34
  32.2 9.3 %all-to-all-start = ((f32[4,56,128]{2,1,0:T(8,128)}), f32[4,56,128]{2,1,0:T(8,128)S(1)}, u32[]{:S(2)}, u32[]{:S(2)}) async-start(f32[4,56,128]{2,1,0:T(8,128)} %get-tuple-element.35), calls=%async_computation | async-start | bytes 229376 | tf_op jit(solution)/shard_map/all_to_all | solution.py:498
  41.4 0.7 %copy-start.5 = (s32[3,64]{1,0:T(4,128)S(1)}, s32[3,64]{1,0:T(4,128)}, u32[]{:S(2)}) copy-start(s32[3,64]{1,0:T(4,128)} %root_ref.3) | copy-start | bytes 2308
  46.1 5.0 %copy-start.6 = (f32[2,25,256]{2,0,1:T(2,128)S(1)}, f32[2,25,256]{2,0,1:T(2,128)}, u32[]{:S(2)}) copy-start(f32[2,25,256]{2,0,1:T(2,128)} %param.16) | copy-start | bytes 153604
  46.2 9.0 %all-to-all-start.1 = ((f32[4,16,128]{2,1,0:T(8,128)}), f32[4,16,128]{2,1,0:T(8,128)S(1)}, u32[]{:S(2)}, u32[]{:S(2)}) async-start(f32[4,16,128]{2,1,0:T(8,128)} %get-tuple-element.38.after_ref), calls=%async_computation.1 | async-start | bytes 65536 | tf_op jit(solution)/shard_map/all_to_all | solution.py:526
  51.2 1.2 %copy-start.2 = (f32[2,256,256]{2,1,0:T(8,128)S(1)}, f32[2,256,256]{2,1,0:T(8,128)}, u32[]{:S(2)}) copy-start(f32[2,256,256]{2,1,0:T(8,128)} %coulomb_ref.1) | copy-start | bytes 1572868
  51.2 1.2 %copy-start.4 = (f32[64,256]{1,0:T(8,128)S(1)}, f32[64,256]{1,0:T(8,128)}, u32[]{:S(2)}) copy-start(f32[64,256]{1,0:T(8,128)} %rho_ref.1) | copy-start | bytes 196612
  52.3 2.8 %copy-start.3 = (f32[64,16,128]{2,1,0:T(8,128)S(1)}, f32[64,16,128]{2,1,0:T(8,128)}, u32[]{:S(2)}) copy-start(f32[64,16,128]{2,1,0:T(8,128)} %param.19) | copy-start | bytes 1572868

commit v4 on v3

--- a/solution.py
+++ b/solution.py
@@ -57,75 +57,59 @@
     return jnp.sum(jnp.where(diagonal, spread, 0.0), axis=1, keepdims=True)
 
 
-def base_kernel(after_ref, rho_ref, coulomb_ref, kinds_ref, base_ref):
+def base_kernel(after_ref, rho_ref, coulomb_ref, coupling_ref, kinds_ref, proj_ref, base_ref, tensor_ref, halves_ref):
     rho = rho_ref[...]
     kind = kinds_ref[1, :, :1]
     total = jnp.zeros((64, 256), F32)
     for s in range(2):
         total = total + dot3(jnp.where(kind == s, rho, 0.0), coulomb_ref[s])
     base_ref[...] = 2.0 * total
-
-
-def plan_kernel(root_ref, count_ref, rows_hbm, species_hbm, plan_ref, kinds_ref, rows_ref, species_ref, sems):
+    pad = jnp.zeros((7, 256), F32)
+    rows = [coupling_ref[0], pad, coupling_ref[1], pad, jnp.zeros((64, 256), F32)]
+    tensor_ref[0], tensor_ref[1] = split(jnp.concatenate(rows, axis=0))
+    halves_ref[0], halves_ref[1] = split(proj_ref[...])
+
+
+def lift_kernel(dens_ref, hart_ref, low_ref, high_ref, lines_ref, rim_ref, dens, hart, sems):
     copies = [
-        pltpu.make_async_copy(rows_hbm, rows_ref, sems.at[0]),
-        pltpu.make_async_copy(species_hbm, species_ref, sems.at[1]),
+        pltpu.make_async_copy(dens_ref.at[pl.ds(0, DUP * CY)], low_ref, sems.at[0]),
+        pltpu.make_async_copy(dens_ref.at[pl.ds((CX - LOW) * CY, LOW * CY)], high_ref, sems.at[1]),
+        pltpu.make_async_copy(dens_ref, dens, sems.at[2]),
+        pltpu.make_async_copy(hart_ref, hart, sems.at[3]),
     ]
     for copy in copies:
         copy.start()
-    first_z = lax.axis_index("band") * CZ
-    count = count_ref[0]
-
-    def step(i, found):
-        for atom in [4 * i + k for k in range(4)]:
-            offset = (root_ref[2, atom] - first_z) & 511
-            meets = (atom < count) & ((offset < CZ) | (offset > 512 - BOX))
-            plan_ref[found] = atom
-            found = found + meets.astype(jnp.int32)
-        return found
-
-    plan_ref[65] = lax.fori_loop(0, (count + 3) // 4, step, 0)
-    for copy in copies:
+    copies[2].wait()
+    for y in range(DUP):
+        lines_ref[y * CX : (y + 1) * CX] = dens[pl.ds(y, CX, stride=CY), :]
+    copies[3].wait()
+    for y in range(HUP):
+        lines_ref[(DUP + y) * CX : (DUP + y + 1) * CX] = hart[pl.ds(y, CX, stride=CY), :]
+    for x in range(16):
+        rim_ref[pl.ds(x, CY, stride=16), :] = hart[x * CY : (x + 1) * CY]
+    for copy in copies[:2]:
         copy.wait()
-    offset = (rows_ref[2:3, :] - first_z) & 511
-    live = lax.broadcasted_iota(jnp.int32, (1, 64), 1) < count_ref[0]
-    meets = live & ((offset < CZ) | (offset > 512 - BOX))
-    for i, here in enumerate((meets, live)):
-        kinds_ref[i] = jnp.broadcast_to(column(jnp.where(here, species_ref[...], 2)), (64, 128))
-
-
-def lift_kernel(dens_ref, hart_ref, low_ref, high_ref, hart_low_ref, sems):
-    copies = [
-        pltpu.make_async_copy(dens_ref.at[pl.ds(0, DUP)], low_ref, sems.at[0]),
-        pltpu.make_async_copy(dens_ref.at[pl.ds(CX - LOW, LOW)], high_ref, sems.at[1]),
-        pltpu.make_async_copy(hart_ref.at[:, pl.ds(0, 16), :], hart_low_ref, sems.at[2]),
-    ]
-    for copy in copies:
-        copy.start()
-    for copy in copies:
-        copy.wait()
-
-
-def widen_kernel(after_ref, dens_ref, above_ref, below_ref, ed_ref, down_ref, up_ref):
+
+
+def widen_kernel(dens_ref, above_ref, below_ref, ed_ref, side_ref, up_ref):
+    def plane(ref, x):
+        return ref[pl.ds(x * CY, CY), :]
+
+    ones = jnp.ones((CY, CZ), F32)
+    halo = {-2: plane(below_ref, 0), -1: plane(below_ref, 1)}
+    for x in range(DUP):
+        halo[CX + x] = plane(above_ref, x)
     for s in range(XD):
         x = s - LOW
-        if x < 0:
-            plane = below_ref[s]
-        elif x < CX:
-            plane = dens_ref[x]
-        elif x < CX + DUP:
-            plane = above_ref[x - CX]
-        else:
-            plane = jnp.ones((CY, CZ), F32)
-        ed_ref[pl.ds(s, CY, stride=XD), :] = plane
-    down_ref[...] = ed_ref[: DUP * XD]
+        ed_ref[pl.ds(s, CY, stride=XD), :] = plane(dens_ref, x) if 0 <= x < CX else halo.get(x, ones)
+    for k in range(24):
+        value = halo[CX + k] if k < DUP else halo.get(k - DUP - LOW, ones)
+        side_ref[pl.ds(k, DUP, stride=24), :] = value[:DUP]
     up_ref[...] = ed_ref[(CY - LOW) * XD :]
 
 
-def turn_kernel(after1_ref, after2_ref, hart_ref, above_ref, send_ref):
-    for x in range(16):
-        send_ref[pl.ds(x, CY, stride=16), :] = hart_ref[x]
-        send_ref[pl.ds(CY * 16 + x, 16, stride=16), :] = above_ref[x]
+def corner_kernel(after_ref, rim_ref, corner_ref):
+    corner_ref[...] = rim_ref[: HUP * 16]
 
 
 def packed(own, tile, lines, group):
@@ -140,21 +124,28 @@
     return lax.broadcasted_iota(jnp.int32, (XD, 128), 1) // 4
 
 
-def ends_kernel(own_ref, down_ref, up_ref, ends_ref, send_ref):
+def ends_kernel(own_ref, lines_ref, side_ref, up_ref, ends_ref, out_ref, down_ref, send_ref, sem):
     group = line_group()
+    for i in range(DUP):
+        base, side = i * XD, i * 24
+        down_ref[base : base + LOW] = side_ref[side + DUP : side + DUP + LOW]
+        down_ref[base + LOW : base + LOW + CX] = lines_ref[i * CX : (i + 1) * CX]
+        down_ref[base + LOW + CX : base + LOW + CX + DUP] = side_ref[side : side + DUP]
+        down_ref[base + LOW + CX + DUP : base + XD] = jnp.ones((XD - LOW - CX - DUP, CZ), F32)
     lines = [(0, up_ref[:XD]), (1, up_ref[XD:])]
     lines += [(LOW + CY + i, down_ref[i * XD : (i + 1) * XD]) for i in range(DUP)]
-    tiles = []
-    for tile in range(2):
-        cols = pl.ds(tile * 128, 128)
-        tiles.append(packed(own_ref[:, cols], tile, lines, group))
-        ends_ref[:, cols] = tiles[tile]
+    tiles = [packed(own_ref[:, pl.ds(t * 128, 128)], t, lines, group) for t in range(2)]
     place = lax.broadcasted_iota(jnp.int32, (XD, 128), 1) % 4
     to_below = jnp.where(place >= 2, tiles[0], pltpu.roll(tiles[1], 126, 1))
     to_above = jnp.where(place < 2, tiles[0], pltpu.roll(tiles[1], 2, 1))
     below = (lax.axis_index("band") + 3) & 3
     for b in range(4):
         send_ref[b] = jnp.where(below == b, to_below, to_above)
+    copy = pltpu.make_async_copy(send_ref, out_ref, sem)
+    copy.start()
+    for t in range(2):
+        ends_ref[:, pl.ds(t * 128, 128)] = tiles[t]
+    copy.wait()
 
 
 def slopes(dens, sigma):
@@ -238,7 +229,39 @@
     tail_ref[8 * XD :] = ed_ref[22 * XD :]
 
 
-def outer_kernel(down_ref, up_ref, tail_ref, ends_ref, bulk_ref, wrap_ref, near, near_part, near_flux, far, part, flux):
+def list_atoms(root_ref, rows_ref, species_ref, count, plan_ref, kinds_ref):
+    first_x, first_y = lax.axis_index("dx") * CX, lax.axis_index("dyz") * CY
+    first_z = lax.axis_index("band") * CZ
+
+    def step(i, found):
+        for atom in [4 * i + k for k in range(4)]:
+            offset = (root_ref[2, atom] - first_z) & 511
+            meets = (atom < count) & ((offset < CZ) | (offset > 512 - BOX))
+            x, y = root_ref[0, atom] - first_x, root_ref[1, atom] - first_y
+            plan_ref[found] = x | (y << 5) | (offset << 10) | (atom << 19)
+            found = found + meets.astype(jnp.int32)
+        return found
+
+    plan_ref[65] = lax.fori_loop(0, (count + 3) // 4, step, 0)
+    offset = (rows_ref[2:3, :] - first_z) & 511
+    live = lax.broadcasted_iota(jnp.int32, (1, 64), 1) < count
+    meets = live & ((offset < CZ) | (offset > 512 - BOX))
+    for i, here in enumerate((meets, live)):
+        kinds_ref[i] = jnp.broadcast_to(column(jnp.where(here, species_ref[...], 2)), (64, 128))
+
+
+def outer_kernel(
+    count_ref, down_ref, up_ref, tail_ref, ends_ref, root_hbm, species_hbm,
+    bulk_ref, wrap_ref, plan_ref, kinds_ref,
+    near, near_part, near_flux, far, part, flux, roots, root_rows, species, sems,
+):
+    copies = [
+        pltpu.make_async_copy(root_hbm, roots, sems.at[0]),
+        pltpu.make_async_copy(root_hbm, root_rows, sems.at[1]),
+        pltpu.make_async_copy(species_hbm, species, sems.at[2]),
+    ]
+    for copy in copies:
+        copy.start()
     near[: 2 * XD] = up_ref[...]
     near[2 * XD :] = tail_ref[6 * XD : 8 * XD]
     near_flux[2 * XD :] = tail_ref[: 2 * XD]
@@ -253,12 +276,15 @@
     bulk_lines(part, flux, 1, DUP, bulk_ref.at[pl.ds(2 * XH, DUP * XH)])
     for i, value in enumerate(packed_flux(ends_ref[...])):
         wrap_ref[i] = value
+    for copy in copies:
+        copy.wait()
+    list_atoms(roots, root_rows, species, count_ref[0], plan_ref, kinds_ref)
 
 
 def field_kernel(
-    root_ref, plan_ref,
+    plan_ref,
     hart_ref, cells_ref,
-    hart_above, hart_right, bulk1_ref, bulk2_ref, ends_ref, beside_ref, wrap_ref, kinds_ref,
+    rim_ref, lines_ref, corner_ref, bulk1_ref, bulk2_ref, ends_ref, beside_ref, wrap_ref, kinds_ref,
     field, part_ref,
     hart, cells, windows, fixes, sems,
 ):
@@ -303,9 +329,11 @@
         turned = pltpu.roll(tiles[line // 32], (254 - 4 * (line % 32)) % 128, 1)
         if y < CY:
             own = hart[pl.ds(y, CX, stride=CY), :]
+            rim = rim_ref[pl.ds(y * 16, 16), :]
         else:
-            own = hart_above[pl.ds(y - CY, CX, stride=16), :]
-        source = jnp.concatenate([own, hart_right[pl.ds(y * 16, 16), :]], axis=0)
+            own = lines_ref[pl.ds((DUP + y - CY) * CX, CX), :]
+            rim = corner_ref[pl.ds((y - CY) * 16, 16), :]
+        source = jnp.concatenate([own, rim], axis=0)
         if 2 <= y < 22:
             bulk = bulk1_ref[pl.ds((y - 2) * XH, XH), :]
         else:
@@ -316,11 +344,9 @@
     group = step_z // 16
     step_z = step_z % 16
     count = plan_ref[65]
-    first_x, first_y = lax.axis_index("dx") * CX, lax.axis_index("dyz") * CY
-    first_z = band * CZ
-
-    def window(atom):
-        rx, ry, rz = root_ref[0, atom] - first_x, root_ref[1, atom] - first_y, root_ref[2, atom] - first_z
+
+    def window(entry):
+        rx, ry, rz = entry & 31, (entry >> 5) & 31, (entry >> 10) & 511
         shift = 128 - (rz & 127)
         inside = ((step_z + rz) & 511) < 128
         halves = []
@@ -335,8 +361,9 @@
 
     def atom_step(i, carry):
         items = [2 * i, jnp.minimum(2 * i + 1, count - 1)]
-        atoms = [plan_ref[item] for item in items]
-        values = [window(atom) for atom in atoms]
+        entries = [plan_ref[item] for item in items]
+        values = [window(entry) for entry in entries]
+        atoms = [entry >> 19 for entry in entries]
         for atom, halves in zip(atoms, values):
             for jh in range(2):
                 windows[pl.ds(atom + jh * 1024, 16, stride=64), :] = halves[jh]
@@ -375,7 +402,7 @@
 
 
 def apply_kernel(
-    parts_ref, coupling_ref, base_ref, kinds_ref, proj_ref, ham_ref, out_ref, spread_ref
+    parts_ref, tensor_ref, base_ref, kinds_ref, halves_ref, ham_out, out_ref, spread_ref, ham_ref, rows_ref, sems
 ):
     kind = kinds_ref[1]
     joined = (parts_ref[0] + parts_ref[1]) + (parts_ref[2] + parts_ref[3])
@@ -383,10 +410,12 @@
     moments = jnp.concatenate(rows, axis=0)
     moments = jnp.where(lax.broadcasted_iota(jnp.int32, (64, 128), 1) < 32, moments, 0.0)
     moments = jnp.where(kind == 0, moments, jnp.where(kind == 1, pltpu.roll(moments, 32, 1), 0.0))
-    pad = jnp.zeros((7, 256), F32)
-    tensors = jnp.concatenate([coupling_ref[0], pad, coupling_ref[1], pad, jnp.zeros((64, 256), F32)], axis=0)
-    ham = jnp.where(kind[:, :1] < 2, dot3(moments, tensors) + base_ref[...], 0.0)
+    high, low = split(moments)
+    ham = dot(high, tensor_ref[0]) + (dot(low, tensor_ref[0]) + dot(high, tensor_ref[1]))
+    ham = jnp.where(kind[:, :1] < 2, ham + base_ref[...], 0.0)
     ham_ref[...] = ham
+    copies = [pltpu.make_async_copy(ham_ref, ham_out, sems.at[4])]
+    copies[0].start()
     lane = lax.broadcasted_iota(jnp.int32, (64, 128), 1)
     row = lax.broadcasted_iota(jnp.int32, (64, 128), 0)
     mine = (lane // 16) == (row % 8)
@@ -398,7 +427,15 @@
         spread_ref[pl.ds(i, 64, stride=16), :] = jnp.where(mine, placed, 0.0)
     for g in range(8):
         rows = pl.ds(g * 128, 128)
-        out_ref[rows, :] = dot3(spread_ref[rows, :], proj_ref[rows, :])
+        high, low = split(spread_ref[rows, :])
+        first = halves_ref[0, rows, :]
+        rows_ref[rows, :] = dot(high, first) + (dot(low, first) + dot(high, halves_ref[1, rows, :]))
+        if g % 2:
+            part = pl.ds((g - 1) * 128, 256)
+            copies.append(pltpu.make_async_copy(rows_ref.at[part], out_ref.at[part], sems.at[g // 2]))
+            copies[-1].start()
+    for copy in copies:
+        copy.wait()
 
 
 def far(value):
@@ -446,37 +483,26 @@
 ):
     slots = box_root.shape[1]
 
-    dens_low, dens_high, hart_low = call(
+    dens_rows, hart_rows = density.reshape(CX * CY, CZ), hartree.reshape(CX * CY, CZ)
+    low, high, lines, rim = call(
         lift_kernel,
         "lift",
-        (shape(DUP, CY, CZ), shape(LOW, CY, CZ), shape(CX, 16, CZ)),
+        (shape(DUP * CY, CZ), shape(LOW * CY, CZ), shape((DUP + HUP) * CX, CZ), shape(CY * 16, CZ)),
         hbm(2),
-        [pltpu.SemaphoreType.DMA((3,))],
-    )(far(density), far(hartree))
-    below = shifted(dens_high, "dx", 1)
-    above = shifted(dens_low, "dx", -1)
-    hart_above = shifted(hart_low, "dyz", -1)
-
-    plan, kinds = pl.pallas_call(
-        plan_kernel,
-        out_shape=(shape(66, dtype=jnp.int32), shape(2, 64, 128)),
-        in_specs=smem(2) + hbm(2),
-        out_specs=(smem(1)[0], vmem(1)[0]),
-        scratch_shapes=[
-            pltpu.VMEM((3, 64), jnp.int32),
-            pltpu.VMEM((1, 64), jnp.int32),
-            pltpu.SemaphoreType.DMA((2,)),
-        ],
-        compiler_params=PARAMS,
-        name="plan",
-    )(box_root, atom_count, far(box_root), far(species.reshape(1, slots)))
-    wide_d, send_down, send_up = call(
+        [pltpu.VMEM((CX * CY, CZ), F32), pltpu.VMEM((CX * CY, CZ), F32), pltpu.SemaphoreType.DMA((4,))],
+    )(far(dens_rows), far(hart_rows))
+    above = shifted(low, "dx", -1)
+    below = shifted(high, "dx", 1)
+    rim = shifted(rim, "dx", -1)
+    lines_above = shifted(lines, "dyz", -1)
+
+    wide_d, side, send_up = call(
         widen_kernel,
         "widen",
-        (shape(CY * XD, CZ), shape(DUP * XD, CZ), shape(LOW * XD, CZ)),
-        anywhere(1) + vmem(3),
-    )(close(kinds), density, above, below)
-    from_up = shifted(send_down, "dyz", -1)
+        (shape(CY * XD, CZ), shape(DUP * 24, CZ), shape(LOW * XD, CZ)),
+        vmem(3),
+    )(dens_rows, above, below)
+    side_above = shifted(side, "dyz", -1)
     from_down = shifted(send_up, "dyz", 1)
 
     bulk1, tail, own_ends = call(
@@ -486,30 +512,54 @@
         vmem(1),
         [pltpu.VMEM((22 * XD, CZ), F32), pltpu.VMEM((22 * XD, CZ), F32)],
     )(wide_d)
-    send_right = call(turn_kernel, "turn", (shape(40 * 16, CZ),), anywhere(2) + vmem(2))(
-        close(from_down), close(own_ends), hartree, hart_above
+
+    corner = call(corner_kernel, "corner", (shape(HUP * 16, CZ),), anywhere(1) + vmem(1))(
+        close(own_ends), close(rim)
     )[0]
-    hart_right = shifted(send_right, "dx", -1)
-
-    ends, send_ends = call(ends_kernel, "ends", (shape(XD, 256), pltpu.VMEM((4, XD, 128), F32)), vmem(3))(
-        close(own_ends), close(from_up), close(from_down)
-    )
+    corner = shifted(corner, "dyz", -1)
+
+    ends, send_ends, from_up = pl.pallas_call(
+        ends_kernel,
+        out_shape=(shape(XD, 256), pltpu.HBM((4, XD, 128), F32), shape(DUP * XD, CZ)),
+        in_specs=vmem(4),
+        out_specs=tuple(vmem(1) + hbm(1) + vmem(1)),
+        scratch_shapes=[pltpu.VMEM((4, XD, 128), F32), pltpu.SemaphoreType.DMA(())],
+        compiler_params=PARAMS,
+        name="ends",
+    )(close(own_ends), close(lines_above), close(side_above), close(from_down))
 
     beside = lax.all_to_all(send_ends, "band", 0, 0)
     cells = shape_functions.transpose(1, 0, 2).reshape(NL, 2, 32, 128).transpose(0, 2, 1, 3).reshape(NL * 64, 128)
-    bulk2, wrap = call(
+    bulk2, wrap, plan, kinds = pl.pallas_call(
         outer_kernel,
-        "outer",
-        (shape(19 * XH, CZ), shape(4, XD, 256)),
-        vmem(4),
-        [pltpu.VMEM((n * XD, CZ), F32) for n in (4, 3, 4, 19, 19, 19)],
-    )(close(from_up), close(from_down), close(tail), close(ends))
+        out_shape=(
+            shape(19 * XH, CZ),
+            shape(4, XD, 256),
+            shape(66, dtype=jnp.int32),
+            shape(2, 64, 128),
+        ),
+        in_specs=smem(1) + vmem(4) + hbm(2),
+        out_specs=tuple(vmem(2) + smem(1) + vmem(1)),
+        scratch_shapes=[pltpu.VMEM((n * XD, CZ), F32) for n in (4, 3, 4, 19, 19, 19)]
+        + [
+            pltpu.SMEM((3, 64), jnp.int32),
+            pltpu.VMEM((3, 64), jnp.int32),
+            pltpu.VMEM((1, 64), jnp.int32),
+            pltpu.SemaphoreType.DMA((3,)),
+        ],
+        compiler_params=PARAMS,
+        name="outer",
+    )(
+        atom_count,
+        close(from_up), close(from_down), close(tail), close(ends),
+        far(box_root), far(species.reshape(1, slots)),
+    )
 
     field, parts = call(
         field_kernel,
         "field",
         (pltpu.VMEM((YH * XH, CZ), F32), pltpu.VMEM((4, 16, 128), F32)),
-        smem(2) + hbm(2) + vmem(8),
+        smem(1) + hbm(2) + vmem(9),
         [
             pltpu.VMEM((CX * CY, CZ), F32),
             pltpu.VMEM((NL * 64, 128), F32),
@@ -518,23 +568,33 @@
             pltpu.SemaphoreType.DMA((2,)),
         ],
     )(
-        box_root, plan,
-        far(hartree.reshape(CX * CY, CZ)), far(cells),
-        close(hart_above.reshape(CX * 16, CZ)), close(hart_right), close(bulk1), close(bulk2), close(ends), close(beside), close(wrap), close(kinds),
+        plan,
+        far(hart_rows), far(cells),
+        close(rim), close(lines_above), close(corner), close(bulk1), close(bulk2), close(ends), close(beside), close(wrap), close(kinds),
     )
 
     summed = lax.all_to_all(parts, "band", 0, 0)
     potential = call(own_kernel, "own", (shape(CX * CY, CZ),), vmem(1))(field)[0]
-    base = call(base_kernel, "base", (shape(64, 256),), anywhere(1) + vmem(3))(
-        parts, rho_ij, coulomb, kinds
-    )[0]
-    atom_hamiltonian, applied = call(
+    base, tensors, halves = call(
+        base_kernel,
+        "base",
+        (shape(64, 256), shape(2, 128, 256, dtype=BF16), shape(2, 64 * NI, 128, dtype=BF16)),
+        anywhere(1) + vmem(5),
+    )(parts, rho_ij, coulomb, coupling, close(kinds), projections.reshape(slots * NI, CZ))
+    atom_hamiltonian, applied = pl.pallas_call(
         apply_kernel,
-        "apply",
-        (shape(64, 256), shape(64 * NI, 128)),
-        vmem(5),
-        [pltpu.VMEM((64 * NI, 128), F32)],
-    )(summed, coupling, base, kinds, projections.reshape(slots * NI, CZ))
+        out_shape=(pltpu.HBM((64, 256), F32), pltpu.HBM((64 * NI, 128), F32)),
+        in_specs=vmem(5),
+        out_specs=tuple(hbm(2)),
+        scratch_shapes=[
+            pltpu.VMEM((64 * NI, 128), F32),
+            pltpu.VMEM((64, 256), F32),
+            pltpu.VMEM((64 * NI, 128), F32),
+            pltpu.SemaphoreType.DMA((5,)),
+        ],
+        compiler_params=PARAMS,
+        name="apply",
+    )(close(summed), close(tensors), close(base), close(kinds), close(halves))
     return (
         potential.reshape(CX, CY, CZ),
         atom_hamiltonian,

time: 57.5 us -> 54.7 us (0.951)
  the two profiles are of different devices: /device:TPU:2 before, /device:TPU:56 now
where the time goes in v4:
time: 54.7 us; the launch traced here: 54.2 us
  starting transfers between devices  26.7 us (49%)
  Pallas kernels  16.7 us (31%)
  waiting for transfers between devices  8.8 us (16%)
  between operations  1.44 us (3%)
    ppermute x7, starting transfers between devices, shifted(): lax.ppermute(block, axis, [(i, (i + distance) % n) for i in range(n)])  18.9 us
    pallas_call x1, Pallas kernels, local(): call(field_kernel, 'field', (pltpu.VMEM((YH * XH, CZ), F32), pltpu.VMEM((...  5.21 us
    all_to_all x1, starting transfers between devices, local(): beside = lax.all_to_all(send_ends, 'band', 0, 0)  4.05 us
    all_to_all x1, waiting for transfers between devices, local(): summed = lax.all_to_all(parts, 'band', 0, 0)  3.78 us
    all_to_all x1, starting transfers between devices, local(): summed = lax.all_to_all(parts, 'band', 0, 0)  3.75 us
    pallas_call x1, Pallas kernels, local(): pl.pallas_call(outer_kernel, out_shape=(shape(19 * XH, CZ), shape(4, XD,...  3.56 us
    ppermute x7, waiting for transfers between devices, shifted(): lax.ppermute(block, axis, [(i, (i + distance) % n) for i in range(n)])  3.36 us
    pallas_call x1, Pallas kernels, local(): call(inner_kernel, 'inner', (shape(20 * XH, CZ), shape(10 * XD, CZ), shap...  2.67 us
  transfers between devices with their start and end apart: 9, of which 4 were waited for; matrix products, arithmetic and copies ran while one was open for 0% of the time, Pallas kernels for 16%

profile of v4, /device:TPU:56, one launch (start us, length us, event | category | flops | bytes accessed | tf_op | source)
XLA Modules:
  0.0 54.2 jit_solution(10602765556833852993)
XLA Ops:
  0.6 0.0 copy-start
  0.6 1.4 %lift.1 = (f32[408,128]{1,0:T(8,128)S(1)}, f32[48,128]{1,0:T(8,128)S(1)}, f32[1024,128]{1,0:T(8,128)S(1)}, f32[384,128]{1,0:T(8,128)S(1)}) custom-call(f32[768,128]{1,0:T(8,128)} %bitcast.13, f32[768,128]{1,0:T(8,128)} %bitcast.16), custom_call_target="tpu_custom_call" | custom-call | tf_op jit(solution)/shard_map/lift/pallas_call | solution.py:487
  2.1 8.5 %collective-permute-start.2 = (f32[1024,128]{1,0:T(8,128)S(1)}, f32[1024,128]{1,0:T(8,128)S(1)}, u32[]{:S(2)}, u32[]{:S(2)}) collective-permute-start(f32[1024,128]{1,0:T(8,128)S(1)} %get-tuple-element.31), channel_id=1, source_target_pairs={{0,15},{1,0},{2,1},{3,2},{4,3},{5,4},{6,5},{7,6},{8,7},{9,8},{10,9... | collective-permute-start | bytes 1572872 | tf_op jit(solution)/shard_map/ppermute | solution.py:34
  10.6 3.2 %collective-permute-start = (f32[408,128]{1,0:T(8,128)S(1)}, f32[408,128]{1,0:T(8,128)S(1)}, u32[]{:S(2)}, u32[]{:S(2)}) collective-permute-start(f32[408,128]{1,0:T(8,128)S(1)} %get-tuple-element.27), channel_id=1, source_target_pairs={{0,112},{16,0},{32,16},{48,32},{64,48},{80,64},{96,80},{112,96},{1... | collective-permute-start | bytes 626696 | tf_op jit(solution)/shard_map/ppermute | solution.py:34
  13.8 3.8 %collective-permute-start.1 = (f32[48,128]{1,0:T(8,128)S(1)}, f32[48,128]{1,0:T(8,128)S(1)}, u32[]{:S(2)}, u32[]{:S(2)}) collective-permute-start(f32[48,128]{1,0:T(8,128)S(1)} %get-tuple-element.28), channel_id=1, source_target_pairs={{0,16},{16,32},{32,48},{48,64},{64,80},{80,96},{96,112},{112,0},{1... | collective-permute-start | bytes 73736 | tf_op jit(solution)/shard_map/ppermute | solution.py:34
  17.6 2.0 %collective-permute-start.5 = (f32[384,128]{1,0:T(8,128)S(1)}, f32[384,128]{1,0:T(8,128)S(1)}, u32[]{:S(2)}, u32[]{:S(2)}) collective-permute-start(f32[384,128]{1,0:T(8,128)S(1)} %get-tuple-element.38), channel_id=1, source_target_pairs={{0,112},{16,0},{32,16},{48,32},{64,48},{80,64},{96,80},{112,96},{1... | collective-permute-start | bytes 589832 | tf_op jit(solution)/shard_map/ppermute | solution.py:34
  19.7 0.0 collective-permute-done.1.below_ref
  19.7 1.6 %collective-permute-done.above_ref = f32[408,128]{1,0:T(8,128)S(1)} collective-permute-done((f32[408,128]{1,0:T(8,128)S(1)}, f32[408,128]{1,0:T(8,128)S(1)}, u32[]{:S(2)}, u32[]{:S(2)}) %collective-permute-start) | collective-permute-done | bytes 208928 | tf_op jit(solution)/shard_map/ppermute | solution.py:34
  21.3 0.0 copy-done
  21.3 0.1 widen.1
  21.5 0.0 collective-permute-start.3
  21.5 0.5 collective-permute-start.4
  22.0 2.7 %inner.1 = (f32[960,128]{1,0:T(8,128)S(1)}, f32[560,128]{1,0:T(8,128)S(1)}, f32[56,256]{1,0:T(8,128)S(1)}) custom-call(f32[1344,128]{1,0:T(8,128)S(1)} %get-tuple-element.29.ed_ref), custom_call_target="tpu_custom_call" | custom-call | tf_op jit(solution)/shard_map/inner/pallas_call | solution.py:508
  24.7 1.7 %collective-permute-done.5.rim_ref = f32[384,128]{1,0:T(8,128)S(1)} collective-permute-done((f32[384,128]{1,0:T(8,128)S(1)}, f32[384,128]{1,0:T(8,128)S(1)}, u32[]{:S(2)}, u32[]{:S(2)}) %collective-permute-start.5) | collective-permute-done | bytes 196640 | tf_op jit(solution)/shard_map/ppermute | solution.py:34
  26.4 0.8 %collective-permute-start.6 = (f32[240,128]{1,0:T(8,128)S(1)}, f32[240,128]{1,0:T(8,128)S(1)}, u32[]{:S(2)}, u32[]{:S(2)}) collective-permute-start(f32[240,128]{1,0:T(8,128)S(1)} %corner.1), channel_id=1, source_target_pairs={{0,15},{1,0},{2,1},{3,2},{4,3},{5,4},{6,5},{7,6},{8,7},{9,8},{10,9... | collective-permute-start | bytes 368648 | tf_op jit(solution)/shard_map/ppermute | solution.py:34
  27.2 0.0 collective-permute-done.4.up_ref
  27.2 0.0 collective-permute-done.3.side_ref
  27.2 0.0 collective-permute-done.2.lines_ref
  27.2 1.0 %ends.1 = (f32[56,256]{1,0:T(8,128)S(1)}, f32[4,56,128]{2,1,0:T(8,128)}, f32[952,128]{1,0:T(8,128)S(1)}) custom-call(f32[56,256]{1,0:T(8,128)S(1)} %get-tuple-element.30.own_ref.after_ref, f32[1024,128]{1,0:T(8,128)S(1)} %collective-permute-done.2.lines_ref, f32[408,128]{1,0:T(8,128)S(1)} %collective-permute-done.3.side_ref, ...), custom_call_target="tpu_custom_call" | custom-call | tf_op jit(solution)/shard_map/ends/pallas_call | solution.py:521
  28.2 4.1 %all-to-all-start = ((f32[4,56,128]{2,1,0:T(8,128)}), f32[4,56,128]{2,1,0:T(8,128)S(1)}, u32[]{:S(2)}, u32[]{:S(2)}) async-start(f32[4,56,128]{2,1,0:T(8,128)} %get-tuple-element.41), calls=%async_computation | async-start | bytes 229376 | tf_op jit(solution)/shard_map/all_to_all | solution.py:531
  32.9 3.6 %outer.1 = (f32[912,128]{1,0:T(8,128)S(1)}, f32[4,56,256]{2,1,0:T(8,128)S(1)}, s32[66]{0:T(128)S(1)}, f32[2,64,128]{2,1,0:T(8,128)S(1)}) custom-call(s32[1]{0:T(128)S(6)} %copy.15.count_ref, f32[952,128]{1,0:T(8,128)S(1)} %get-tuple-element.34.down_ref, f32[112,128]{1,0:T(8,128)S(1)} %collective-permute-done.4.up_ref, ...), custom_call_target="tpu_custom_call" | custom-call | tf_op jit(solution)/shard_map/outer/pallas_call | solution.py:533
  36.5 0.0 collective-permute-done.6.corner_ref
  36.5 1.7 %all-to-all-done.beside_ref = f32[4,56,128]{2,1,0:T(8,128)S(1)} async-done(((f32[4,56,128]{2,1,0:T(8,128)}), f32[4,56,128]{2,1,0:T(8,128)S(1)}, u32[]{:S(2)}, u32[]{:S(2)}) %all-to-all-start) | async-done | bytes 114720 | tf_op jit(solution)/shard_map/all_to_all | solution.py:531
  38.1 5.2 %field.1 = (f32[1872,128]{1,0:T(8,128)S(1)}, f32[4,16,128]{2,1,0:T(8,128)}) custom-call(s32[66]{0:T(128)S(1)} %get-tuple-element.37.plan_ref, f32[768,128]{1,0:T(8,128)} %bitcast.17, f32[1600,128]{1,0:T(8,128)} %bitcast.18, f32[384,128]{1,0:T(8,128)S(1)} %collective-permute-done.5.rim_ref, f32[1024,128]{1,0:T(8,128)S(1)} %collective-permute-done.2.lines_ref, ...), custom_call_target="tpu_custom_call" | custom-call | tf_op jit(solution)/shard_map/field/pallas_call | solution.py:558
  43.4 0.0 copy-start.4
  43.4 3.8 %all-to-all-start.1 = ((f32[4,16,128]{2,1,0:T(8,128)}), f32[4,16,128]{2,1,0:T(8,128)S(1)}, u32[]{:S(2)}, u32[]{:S(2)}) async-start(f32[4,16,128]{2,1,0:T(8,128)} %get-tuple-element.45.after_ref), calls=%async_computation.1 | async-start | bytes 65536 | tf_op jit(solution)/shard_map/all_to_all | solution.py:576
  47.1 0.0 copy-done.4
  47.1 0.0 copy-start.1
  47.1 0.0 copy-start.2
  47.2 0.0 copy-start.3
  47.2 0.8 %own.1 = f32[768,128]{1,0:T(8,128)} custom-call(f32[1872,128]{1,0:T(8,128)S(1)} %get-tuple-element.44.field_ref), custom_call_target="tpu_custom_call" | custom-call | tf_op jit(solution)/shard_map/own/pallas_call | solution.py:577
  48.0 0.3 copy-done.1
  48.3 0.2 copy-done.2
  48.5 0.0 copy-done.3
  48.5 0.3 base.1
  48.8 3.8 %all-to-all-done.1.parts_ref = f32[4,16,128]{2,1,0:T(8,128)S(1)} async-done(((f32[4,16,128]{2,1,0:T(8,128)}), f32[4,16,128]{2,1,0:T(8,128)S(1)}, u32[]{:S(2)}, u32[]{:S(2)}) %all-to-all-start.1) | async-done | bytes 32800 | tf_op jit(solution)/shard_map/all_to_all | solution.py:576
  52.6 1.6 %apply.1 = (f32[64,256]{1,0:T(8,128)}, f32[1024,128]{1,0:T(8,128)}) custom-call(f32[4,16,128]{2,1,0:T(8,128)S(1)} %all-to-all-done.1.parts_ref, bf16[2,128,256]{2,1,0:T(8,128)(2,1)S(1)} %get-tuple-element.46.tensor_ref, f32[64,256]{1,0:T(8,128)S(1)} %get-tuple-element.47.base_ref, f32[2,64,128]{2,1,0:T(8,128)S(1)} %get-tuple-element.43.kinds_ref, ...), custom_call_target="tpu_custom_call" | custom-call | tf_op jit(solution)/shard_map/apply/pallas_call | solution.py:584
  (2 shorter events, 0.0 us)
Async XLA Ops:
  0.6 20.7 %copy-start = (f32[32,24,128]{2,1,0:T(8,128)S(1)}, f32[32,24,128]{2,1,0:T(8,128)}, u32[]{:S(2)}) copy-start(f32[32,24,128]{2,1,0:T(8,128)} %param.10) | copy-start | bytes 1179652
  2.1 25.1 %collective-permute-start.2 = (f32[1024,128]{1,0:T(8,128)S(1)}, f32[1024,128]{1,0:T(8,128)S(1)}, u32[]{:S(2)}, u32[]{:S(2)}) collective-permute-start(f32[1024,128]{1,0:T(8,128)S(1)} %get-tuple-element.31), channel_id=1, source_target_pairs={{0,15},{1,0},{2,1},{3,2},{4,3},{5,4},{6,5},{7,6},{8,7},{9,8},{10,9... | collective-permute-start | bytes 1572872 | tf_op jit(solution)/shard_map/ppermute | solution.py:34
  10.6 10.8 %collective-permute-start = (f32[408,128]{1,0:T(8,128)S(1)}, f32[408,128]{1,0:T(8,128)S(1)}, u32[]{:S(2)}, u32[]{:S(2)}) collective-permute-start(f32[408,128]{1,0:T(8,128)S(1)} %get-tuple-element.27), channel_id=1, source_target_pairs={{0,112},{16,0},{32,16},{48,32},{64,48},{80,64},{96,80},{112,96},{1... | collective-permute-start | bytes 626696 | tf_op jit(solution)/shard_map/ppermute | solution.py:34
  13.8 5.9 %collective-permute-start.1 = (f32[48,128]{1,0:T(8,128)S(1)}, f32[48,128]{1,0:T(8,128)S(1)}, u32[]{:S(2)}, u32[]{:S(2)}) collective-permute-start(f32[48,128]{1,0:T(8,128)S(1)} %get-tuple-element.28), channel_id=1, source_target_pairs={{0,16},{16,32},{32,48},{48,64},{64,80},{80,96},{96,112},{112,0},{1... | collective-permute-start | bytes 73736 | tf_op jit(solution)/shard_map/ppermute | solution.py:34
  17.6 8.8 %collective-permute-start.5 = (f32[384,128]{1,0:T(8,128)S(1)}, f32[384,128]{1,0:T(8,128)S(1)}, u32[]{:S(2)}, u32[]{:S(2)}) collective-permute-start(f32[384,128]{1,0:T(8,128)S(1)} %get-tuple-element.38), channel_id=1, source_target_pairs={{0,112},{16,0},{32,16},{48,32},{64,48},{80,64},{96,80},{112,96},{1... | collective-permute-start | bytes 589832 | tf_op jit(solution)/shard_map/ppermute | solution.py:34
  21.5 5.7 %collective-permute-start.3 = (f32[408,128]{1,0:T(8,128)S(1)}, f32[408,128]{1,0:T(8,128)S(1)}, u32[]{:S(2)}, u32[]{:S(2)}) collective-permute-start(f32[408,128]{1,0:T(8,128)S(1)} %get-tuple-element.32), channel_id=1, source_target_pairs={{0,15},{1,0},{2,1},{3,2},{4,3},{5,4},{6,5},{7,6},{8,7},{9,8},{10,9... | collective-permute-start | bytes 626696 | tf_op jit(solution)/shard_map/ppermute | solution.py:34
  21.5 5.7 %collective-permute-start.4 = (f32[112,128]{1,0:T(8,128)S(1)}, f32[112,128]{1,0:T(8,128)S(1)}, u32[]{:S(2)}, u32[]{:S(2)}) collective-permute-start(f32[112,128]{1,0:T(8,128)S(1)} %get-tuple-element.33), channel_id=1, source_target_pairs={{0,1},{1,2},{2,3},{3,4},{4,5},{5,6},{6,7},{7,8},{8,9},{9,10},{10,1... | collective-permute-start | bytes 172040 | tf_op jit(solution)/shard_map/ppermute | solution.py:34
  26.4 10.1 %collective-permute-start.6 = (f32[240,128]{1,0:T(8,128)S(1)}, f32[240,128]{1,0:T(8,128)S(1)}, u32[]{:S(2)}, u32[]{:S(2)}) collective-permute-start(f32[240,128]{1,0:T(8,128)S(1)} %corner.1), channel_id=1, source_target_pairs={{0,15},{1,0},{2,1},{3,2},{4,3},{5,4},{6,5},{7,6},{8,7},{9,8},{10,9... | collective-permute-start | bytes 368648 | tf_op jit(solution)/shard_map/ppermute | solution.py:34
  28.2 9.9 %all-to-all-start = ((f32[4,56,128]{2,1,0:T(8,128)}), f32[4,56,128]{2,1,0:T(8,128)S(1)}, u32[]{:S(2)}, u32[]{:S(2)}) async-start(f32[4,56,128]{2,1,0:T(8,128)} %get-tuple-element.41), calls=%async_computation | async-start | bytes 229376 | tf_op jit(solution)/shard_map/all_to_all | solution.py:531
  43.4 3.8 %copy-start.4 = (f32[2,25,256]{2,0,1:T(2,128)S(1)}, f32[2,25,256]{2,0,1:T(2,128)}, u32[]{:S(2)}) copy-start(f32[2,25,256]{2,0,1:T(2,128)} %param.16) | copy-start | bytes 153604
  43.4 9.2 %all-to-all-start.1 = ((f32[4,16,128]{2,1,0:T(8,128)}), f32[4,16,128]{2,1,0:T(8,128)S(1)}, u32[]{:S(2)}, u32[]{:S(2)}) async-start(f32[4,16,128]{2,1,0:T(8,128)} %get-tuple-element.45.after_ref), calls=%async_computation.1 | async-start | bytes 65536 | tf_op jit(solution)/shard_map/all_to_all | solution.py:576
  47.1 1.1 %copy-start.1 = (f32[2,256,256]{2,1,0:T(8,128)S(1)}, f32[2,256,256]{2,1,0:T(8,128)}, u32[]{:S(2)}) copy-start(f32[2,256,256]{2,1,0:T(8,128)} %coulomb_ref.1) | copy-start | bytes 1572868
  47.1 1.3 %copy-start.2 = (f32[64,16,128]{2,1,0:T(8,128)S(1)}, f32[64,16,128]{2,1,0:T(8,128)}, u32[]{:S(2)}) copy-start(f32[64,16,128]{2,1,0:T(8,128)} %param.19) | copy-start | bytes 1572868
  47.2 1.3 %copy-start.3 = (f32[64,256]{1,0:T(8,128)S(1)}, f32[64,256]{1,0:T(8,128)}, u32[]{:S(2)}) copy-start(f32[64,256]{1,0:T(8,128)} %rho_ref.1) | copy-start | bytes 196612

commit v5 on v4

--- a/solution.py
+++ b/solution.py
@@ -124,14 +124,18 @@
     return lax.broadcasted_iota(jnp.int32, (XD, 128), 1) // 4
 
 
+def join_lines(target, first, lines_ref, side_ref):
+    for i in range(DUP):
+        base, side = first + i * XD, i * 24
+        target[base : base + LOW] = side_ref[side + DUP : side + DUP + LOW]
+        target[base + LOW : base + LOW + CX] = lines_ref[i * CX : (i + 1) * CX]
+        target[base + LOW + CX : base + LOW + CX + DUP] = side_ref[side : side + DUP]
+        target[base + LOW + CX + DUP : base + XD] = jnp.ones((XD - LOW - CX - DUP, CZ), F32)
+
+
 def ends_kernel(own_ref, lines_ref, side_ref, up_ref, ends_ref, out_ref, down_ref, send_ref, sem):
     group = line_group()
-    for i in range(DUP):
-        base, side = i * XD, i * 24
-        down_ref[base : base + LOW] = side_ref[side + DUP : side + DUP + LOW]
-        down_ref[base + LOW : base + LOW + CX] = lines_ref[i * CX : (i + 1) * CX]
-        down_ref[base + LOW + CX : base + LOW + CX + DUP] = side_ref[side : side + DUP]
-        down_ref[base + LOW + CX + DUP : base + XD] = jnp.ones((XD - LOW - CX - DUP, CZ), F32)
+    join_lines(down_ref, 0, lines_ref, side_ref)
     lines = [(0, up_ref[:XD]), (1, up_ref[XD:])]
     lines += [(LOW + CY + i, down_ref[i * XD : (i + 1) * XD]) for i in range(DUP)]
     tiles = [packed(own_ref[:, pl.ds(t * 128, 128)], t, lines, group) for t in range(2)]
@@ -214,13 +218,19 @@
     lax.fori_loop(0, count, step, 0, unroll=2)
 
 
-def inner_kernel(ed_ref, bulk_ref, tail_ref, ends_ref, part, flux):
+def inner_kernel(ed_ref, hart_hbm, bulk_ref, tail_ref, ends_ref, part, flux, hart, sem):
+    copy = pltpu.make_async_copy(hart_hbm, hart, sem)
+    copy.start()
     group = line_group()
     lines = [(LOW + i, ed_ref[i * XD : (i + 1) * XD]) for i in range(CY)]
     for tile in range(2):
         ends_ref[:, pl.ds(tile * 128, 128)] = packed(jnp.ones((XD, 128), F32), tile, lines, group)
     flux_lines(ed_ref, 1, 22, part, flux, 0)
     bulk_lines(part, flux, 1, 20, bulk_ref)
+    copy.wait()
+    for i in range(20):
+        here = slice(i * XH, i * XH + CX)
+        bulk_ref[here] = bulk_ref[here] + hart[pl.ds(i + 2, CX, stride=CY), :]
     tail_ref[: 2 * XD] = flux[: 2 * XD]
     tail_ref[2 * XD : 4 * XD] = flux[20 * XD :]
     tail_ref[4 * XD : 5 * XD] = part[:XD]
@@ -251,14 +261,15 @@
 
 
 def outer_kernel(
-    count_ref, down_ref, up_ref, tail_ref, ends_ref, root_hbm, species_hbm,
+    count_ref, side_ref, up_ref, tail_ref, ends_ref, lines_ref, root_hbm, species_hbm, hart_hbm,
     bulk_ref, wrap_ref, plan_ref, kinds_ref,
-    near, near_part, near_flux, far, part, flux, roots, root_rows, species, sems,
+    near, near_part, near_flux, far, part, flux, roots, root_rows, species, hart, sems,
 ):
     copies = [
         pltpu.make_async_copy(root_hbm, roots, sems.at[0]),
         pltpu.make_async_copy(root_hbm, root_rows, sems.at[1]),
         pltpu.make_async_copy(species_hbm, species, sems.at[2]),
+        pltpu.make_async_copy(hart_hbm, hart, sems.at[3]),
     ]
     for copy in copies:
         copy.start()
@@ -267,7 +278,7 @@
     near_flux[2 * XD :] = tail_ref[: 2 * XD]
     near_part[2 * XD :] = tail_ref[4 * XD : 5 * XD]
     far[: 2 * XD] = tail_ref[8 * XD :]
-    far[2 * XD :] = down_ref[...]
+    join_lines(far, 2 * XD, lines_ref, side_ref)
     flux[: 2 * XD] = tail_ref[2 * XD : 4 * XD]
     part[XD : 2 * XD] = tail_ref[5 * XD : 6 * XD]
     flux_lines(near, 1, 2, near_part, near_flux, 0)
@@ -278,22 +289,26 @@
         wrap_ref[i] = value
     for copy in copies:
         copy.wait()
+    for i in range(2 + DUP):
+        y = i if i < 2 else i + 20
+        here = slice(i * XH, i * XH + CX)
+        if y < CY:
+            own = hart[pl.ds(y, CX, stride=CY), :]
+        else:
+            own = lines_ref[(DUP + y - CY) * CX : (DUP + y - CY + 1) * CX]
+        bulk_ref[here] = bulk_ref[here] + own
     list_atoms(roots, root_rows, species, count_ref[0], plan_ref, kinds_ref)
 
 
 def field_kernel(
     plan_ref,
-    hart_ref, cells_ref,
-    rim_ref, lines_ref, corner_ref, bulk1_ref, bulk2_ref, ends_ref, beside_ref, wrap_ref, kinds_ref,
+    cells_ref,
+    rim_ref, corner_ref, bulk1_ref, bulk2_ref, ends_ref, beside_ref, wrap_ref, kinds_ref,
     field, part_ref,
-    hart, cells, windows, fixes, sems,
+    cells, windows, fixes, sem,
 ):
-    copies = [
-        pltpu.make_async_copy(hart_ref, hart, sems.at[0]),
-        pltpu.make_async_copy(cells_ref, cells, sems.at[1]),
-    ]
-    for copy in copies:
-        copy.start()
+    copy = pltpu.make_async_copy(cells_ref, cells, sem)
+    copy.start()
     place = lax.broadcasted_iota(jnp.int32, (XD, 256), 1) % 4
     middle = (place == 1) | (place == 2)
     low = place < 2
@@ -323,22 +338,20 @@
     edge = (lane < 2) | (lane >= 126)
     tiles = [fixes[pl.ds(LOW, XH), pl.ds(t * 128, 128)] for t in range(2)]
 
-    copies[0].wait()
     for y in range(YH):
         line = y + LOW
         turned = pltpu.roll(tiles[line // 32], (254 - 4 * (line % 32)) % 128, 1)
-        if y < CY:
-            own = hart[pl.ds(y, CX, stride=CY), :]
-            rim = rim_ref[pl.ds(y * 16, 16), :]
-        else:
-            own = lines_ref[pl.ds((DUP + y - CY) * CX, CX), :]
-            rim = corner_ref[pl.ds((y - CY) * 16, 16), :]
-        source = jnp.concatenate([own, rim], axis=0)
         if 2 <= y < 22:
             bulk = bulk1_ref[pl.ds((y - 2) * XH, XH), :]
         else:
             bulk = bulk2_ref[pl.ds((y if y < 2 else y - 20) * XH, XH), :]
-        field[pl.ds(y * XH, XH), :] = (source + bulk) + jnp.where(edge, turned, 0.0)
+        value = bulk + jnp.where(edge, turned, 0.0)
+        if y < CY:
+            rim = rim_ref[pl.ds(y * 16, 16), :]
+        else:
+            rim = corner_ref[pl.ds((y - CY) * 16, 16), :]
+        field[pl.ds(y * XH, CX), :] = value[:CX]
+        field[pl.ds(y * XH + CX, 16), :] = value[CX:] + rim
 
     step_z = lax.broadcasted_iota(jnp.int32, (16, 128), 1)
     group = step_z // 16
@@ -360,7 +373,7 @@
         return halves
 
     def atom_step(i, carry):
-        items = [2 * i, jnp.minimum(2 * i + 1, count - 1)]
+        items = [4 * i] + [jnp.minimum(4 * i + k, count - 1) for k in range(1, 4)]
         entries = [plan_ref[item] for item in items]
         values = [window(entry) for entry in entries]
         atoms = [entry >> 19 for entry in entries]
@@ -369,9 +382,9 @@
                 windows[pl.ds(atom + jh * 1024, 16, stride=64), :] = halves[jh]
         return carry
 
-    lax.fori_loop(0, (count + 1) // 2, atom_step, 0)
-
-    copies[1].wait()
+    lax.fori_loop(0, (count + 3) // 4, atom_step, 0)
+
+    copy.wait()
     pad = jnp.zeros((7, 128), F32)
     total = jnp.zeros((128, 128), F32)
     for i in range(16):
@@ -509,21 +522,26 @@
         inner_kernel,
         "inner",
         (shape(20 * XH, CZ), shape(10 * XD, CZ), shape(XD, 256)),
-        vmem(1),
-        [pltpu.VMEM((22 * XD, CZ), F32), pltpu.VMEM((22 * XD, CZ), F32)],
-    )(wide_d)
+        vmem(1) + hbm(1),
+        [
+            pltpu.VMEM((22 * XD, CZ), F32),
+            pltpu.VMEM((22 * XD, CZ), F32),
+            pltpu.VMEM((CX * CY, CZ), F32),
+            pltpu.SemaphoreType.DMA(()),
+        ],
+    )(wide_d, far(hart_rows))
 
     corner = call(corner_kernel, "corner", (shape(HUP * 16, CZ),), anywhere(1) + vmem(1))(
         close(own_ends), close(rim)
     )[0]
     corner = shifted(corner, "dyz", -1)
 
-    ends, send_ends, from_up = pl.pallas_call(
+    ends, send_ends = pl.pallas_call(
         ends_kernel,
-        out_shape=(shape(XD, 256), pltpu.HBM((4, XD, 128), F32), shape(DUP * XD, CZ)),
+        out_shape=(shape(XD, 256), pltpu.HBM((4, XD, 128), F32)),
         in_specs=vmem(4),
-        out_specs=tuple(vmem(1) + hbm(1) + vmem(1)),
-        scratch_shapes=[pltpu.VMEM((4, XD, 128), F32), pltpu.SemaphoreType.DMA(())],
+        out_specs=tuple(vmem(1) + hbm(1)),
+        scratch_shapes=[pltpu.VMEM((DUP * XD, CZ), F32), pltpu.VMEM((4, XD, 128), F32), pltpu.SemaphoreType.DMA(())],
         compiler_params=PARAMS,
         name="ends",
     )(close(own_ends), close(lines_above), close(side_above), close(from_down))
@@ -538,39 +556,39 @@
             shape(66, dtype=jnp.int32),
             shape(2, 64, 128),
         ),
-        in_specs=smem(1) + vmem(4) + hbm(2),
+        in_specs=smem(1) + vmem(5) + hbm(3),
         out_specs=tuple(vmem(2) + smem(1) + vmem(1)),
         scratch_shapes=[pltpu.VMEM((n * XD, CZ), F32) for n in (4, 3, 4, 19, 19, 19)]
         + [
             pltpu.SMEM((3, 64), jnp.int32),
             pltpu.VMEM((3, 64), jnp.int32),
             pltpu.VMEM((1, 64), jnp.int32),
-            pltpu.SemaphoreType.DMA((3,)),
+            pltpu.VMEM((CX * CY, CZ), F32),
+            pltpu.SemaphoreType.DMA((4,)),
         ],
         compiler_params=PARAMS,
         name="outer",
     )(
         atom_count,
-        close(from_up), close(from_down), close(tail), close(ends),
-        far(box_root), far(species.reshape(1, slots)),
+        close(side_above), close(from_down), close(tail), close(ends), close(lines_above),
+        far(box_root), far(species.reshape(1, slots)), far(hart_rows),
     )
 
     field, parts = call(
         field_kernel,
         "field",
         (pltpu.VMEM((YH * XH, CZ), F32), pltpu.VMEM((4, 16, 128), F32)),
-        smem(1) + hbm(2) + vmem(9),
+        smem(1) + hbm(1) + vmem(8),
         [
-            pltpu.VMEM((CX * CY, CZ), F32),
             pltpu.VMEM((NL * 64, 128), F32),
             pltpu.VMEM((2 * 16 * 64, 128), F32),
             pltpu.VMEM((XD, 256), F32),
-            pltpu.SemaphoreType.DMA((2,)),
+            pltpu.SemaphoreType.DMA(()),
         ],
     )(
         plan,
-        far(hart_rows), far(cells),
-        close(rim), close(lines_above), close(corner), close(bulk1), close(bulk2), close(ends), close(beside), close(wrap), close(kinds),
+        far(cells),
+        close(rim), close(corner), close(bulk1), close(bulk2), close(ends), close(beside), close(wrap), close(kinds),
     )
 
     summed = lax.all_to_all(parts, "band", 0, 0)

time: 54.7 us -> 54.5 us (level)
  the two profiles are of different devices: /device:TPU:56 before, /device:TPU:2 now
where the time goes in v5:
time: 54.5 us; the launch traced here: 54.2 us
  starting transfers between devices  33.8 us (62%)
  Pallas kernels  15.9 us (29%)
  waiting for transfers between devices  2.5 us (5%)
  between operations  1.47 us (3%)
    ppermute x7, starting transfers between devices, shifted(): lax.ppermute(block, axis, [(i, (i + distance) % n) for i in range(n)])  23.9 us
    all_to_all x1, starting transfers between devices, local(): summed = lax.all_to_all(parts, 'band', 0, 0)  5.06 us
    all_to_all x1, starting transfers between devices, local(): beside = lax.all_to_all(send_ends, 'band', 0, 0)  4.84 us
    pallas_call x1, Pallas kernels, local(): call(field_kernel, 'field', (pltpu.VMEM((YH * XH, CZ), F32), pltpu.VMEM((...  4.22 us
    pallas_call x1, Pallas kernels, local(): pl.pallas_call(outer_kernel, out_shape=(shape(19 * XH, CZ), shape(4, XD,...  3.6 us
    pallas_call x1, Pallas kernels, local(): call(inner_kernel, 'inner', (shape(20 * XH, CZ), shape(10 * XD, CZ), shap...  2.76 us
    all_to_all x1, waiting for transfers between devices, local(): summed = lax.all_to_all(parts, 'band', 0, 0)  2.32 us
    pallas_call x1, Pallas kernels, local(): pl.pallas_call(apply_kernel, out_shape=(pltpu.HBM((64, 256), F32), pltpu....  1.62 us
  transfers between devices with their start and end apart: 9, of which 2 were waited for; matrix products, arithmetic and copies ran while one was open for 0% of the time, Pallas kernels for 16%

profile of v5, /device:TPU:2, one launch (start us, length us, event | category | flops | bytes accessed | tf_op | source)
XLA Modules:
  0.0 54.2 jit_solution(17751586657402315177)
XLA Ops:
  0.6 0.0 copy-start
  0.6 1.4 %lift.1 = (f32[408,128]{1,0:T(8,128)S(1)}, f32[48,128]{1,0:T(8,128)S(1)}, f32[1024,128]{1,0:T(8,128)S(1)}, f32[384,128]{1,0:T(8,128)S(1)}) custom-call(f32[768,128]{1,0:T(8,128)} %bitcast.13, f32[768,128]{1,0:T(8,128)} %bitcast.16), custom_call_target="tpu_custom_call" | custom-call | tf_op jit(solution)/shard_map/lift/pallas_call | solution.py:500
  2.1 8.5 %collective-permute-start.4 = (f32[1024,128]{1,0:T(8,128)S(1)}, f32[1024,128]{1,0:T(8,128)S(1)}, u32[]{:S(2)}, u32[]{:S(2)}) collective-permute-start(f32[1024,128]{1,0:T(8,128)S(1)} %get-tuple-element.33), channel_id=1, source_target_pairs={{0,15},{1,0},{2,1},{3,2},{4,3},{5,4},{6,5},{7,6},{8,7},{9,8},{10,9... | collective-permute-start | bytes 1572872 | tf_op jit(solution)/shard_map/ppermute | solution.py:34
  10.6 5.4 %collective-permute-start = (f32[408,128]{1,0:T(8,128)S(1)}, f32[408,128]{1,0:T(8,128)S(1)}, u32[]{:S(2)}, u32[]{:S(2)}) collective-permute-start(f32[408,128]{1,0:T(8,128)S(1)} %get-tuple-element.26), channel_id=1, source_target_pairs={{0,112},{16,0},{32,16},{48,32},{64,48},{80,64},{96,80},{112,96},{1... | collective-permute-start | bytes 626696 | tf_op jit(solution)/shard_map/ppermute | solution.py:34
  16.0 1.9 %collective-permute-start.1 = (f32[48,128]{1,0:T(8,128)S(1)}, f32[48,128]{1,0:T(8,128)S(1)}, u32[]{:S(2)}, u32[]{:S(2)}) collective-permute-start(f32[48,128]{1,0:T(8,128)S(1)} %get-tuple-element.27), channel_id=1, source_target_pairs={{0,16},{16,32},{32,48},{48,64},{64,80},{80,96},{96,112},{112,0},{1... | collective-permute-start | bytes 73736 | tf_op jit(solution)/shard_map/ppermute | solution.py:34
  17.9 5.1 %collective-permute-start.5 = (f32[384,128]{1,0:T(8,128)S(1)}, f32[384,128]{1,0:T(8,128)S(1)}, u32[]{:S(2)}, u32[]{:S(2)}) collective-permute-start(f32[384,128]{1,0:T(8,128)S(1)} %get-tuple-element.36), channel_id=1, source_target_pairs={{0,112},{16,0},{32,16},{48,32},{64,48},{80,64},{96,80},{112,96},{1... | collective-permute-start | bytes 589832 | tf_op jit(solution)/shard_map/ppermute | solution.py:34
  23.0 0.0 collective-permute-done.1.below_ref
  23.0 0.0 collective-permute-done.above_ref
  23.0 0.0 copy-done
  23.1 0.1 widen.1
  23.2 0.0 collective-permute-start.2
  23.2 0.5 collective-permute-start.3
  23.7 2.8 %inner.1 = (f32[960,128]{1,0:T(8,128)S(1)}, f32[560,128]{1,0:T(8,128)S(1)}, f32[56,256]{1,0:T(8,128)S(1)}) custom-call(f32[1344,128]{1,0:T(8,128)S(1)} %get-tuple-element.30.ed_ref, f32[768,128]{1,0:T(8,128)} %bitcast.17), custom_call_target="tpu_custom_call" | custom-call | tf_op jit(solution)/shard_map/inner/pallas_call | solution.py:521
  26.5 0.0 collective-permute-done.5.rim_ref
  26.5 2.5 %collective-permute-start.6 = (f32[240,128]{1,0:T(8,128)S(1)}, f32[240,128]{1,0:T(8,128)S(1)}, u32[]{:S(2)}, u32[]{:S(2)}) collective-permute-start(f32[240,128]{1,0:T(8,128)S(1)} %corner.1), channel_id=1, source_target_pairs={{0,15},{1,0},{2,1},{3,2},{4,3},{5,4},{6,5},{7,6},{8,7},{9,8},{10,9... | collective-permute-start | bytes 368648 | tf_op jit(solution)/shard_map/ppermute | solution.py:34
  29.0 0.0 collective-permute-done.3.up_ref
  29.0 0.0 collective-permute-done.2.side_ref
  29.0 0.0 collective-permute-done.4.lines_ref
  29.0 0.9 %ends.1 = (f32[56,256]{1,0:T(8,128)S(1)}, f32[4,56,128]{2,1,0:T(8,128)}) custom-call(f32[56,256]{1,0:T(8,128)S(1)} %get-tuple-element.32.own_ref.after_ref, f32[1024,128]{1,0:T(8,128)S(1)} %collective-permute-done.4.lines_ref, f32[408,128]{1,0:T(8,128)S(1)} %collective-permute-done.2.side_ref, f32[112,128]{1,0:T(8,128)S(1)} %collective-permute-done.3.up_ref), custom_call_target="tpu_custom_call" | custom-call | tf_op jit(solution)/shard_map/ends/pallas_call | solution.py:539
  30.0 4.8 %all-to-all-start = ((f32[4,56,128]{2,1,0:T(8,128)}), f32[4,56,128]{2,1,0:T(8,128)S(1)}, u32[]{:S(2)}, u32[]{:S(2)}) async-start(f32[4,56,128]{2,1,0:T(8,128)} %get-tuple-element.39), calls=%async_computation | async-start | bytes 229376 | tf_op jit(solution)/shard_map/all_to_all | solution.py:549
  35.5 3.6 %outer.1 = (f32[912,128]{1,0:T(8,128)S(1)}, f32[4,56,256]{2,1,0:T(8,128)S(1)}, s32[66]{0:T(128)S(1)}, f32[2,64,128]{2,1,0:T(8,128)S(1)}) custom-call(s32[1]{0:T(128)S(6)} %copy.15.count_ref, f32[408,128]{1,0:T(8,128)S(1)} %collective-permute-done.2.side_ref, f32[112,128]{1,0:T(8,128)S(1)} %collective-permute-done.3.up_ref, ...), custom_call_target="tpu_custom_call" | custom-call | tf_op jit(solution)/shard_map/outer/pallas_call | solution.py:551
  39.1 0.0 collective-permute-done.6.corner_ref
  39.1 0.2 all-to-all-done.beside_ref
  39.2 4.2 %field.1 = (f32[1872,128]{1,0:T(8,128)S(1)}, f32[4,16,128]{2,1,0:T(8,128)}) custom-call(s32[66]{0:T(128)S(1)} %get-tuple-element.35.plan_ref, f32[1600,128]{1,0:T(8,128)} %bitcast.19, f32[384,128]{1,0:T(8,128)S(1)} %collective-permute-done.5.rim_ref, f32[240,128]{1,0:T(8,128)S(1)} %collective-permute-done.6.corner_ref, ...), custom_call_target="tpu_custom_call" | custom-call | tf_op jit(solution)/shard_map/field/pallas_call | solution.py:577
  43.5 0.0 copy-start.4
  43.5 5.1 %all-to-all-start.1 = ((f32[4,16,128]{2,1,0:T(8,128)}), f32[4,16,128]{2,1,0:T(8,128)S(1)}, u32[]{:S(2)}, u32[]{:S(2)}) async-start(f32[4,16,128]{2,1,0:T(8,128)} %get-tuple-element.43.after_ref), calls=%async_computation.1 | async-start | bytes 65536 | tf_op jit(solution)/shard_map/all_to_all | solution.py:594
  48.5 0.0 copy-done.4
  48.6 0.0 copy-start.1
  48.6 0.0 copy-start.2
  48.6 0.0 copy-start.3
  48.6 0.8 %own.1 = f32[768,128]{1,0:T(8,128)} custom-call(f32[1872,128]{1,0:T(8,128)S(1)} %get-tuple-element.42.field_ref), custom_call_target="tpu_custom_call" | custom-call | tf_op jit(solution)/shard_map/own/pallas_call | solution.py:595
  49.4 0.3 copy-done.1
  49.7 0.2 copy-done.2
  49.9 0.0 copy-done.3
  49.9 0.3 base.1
  50.2 2.3 %all-to-all-done.1.parts_ref = f32[4,16,128]{2,1,0:T(8,128)S(1)} async-done(((f32[4,16,128]{2,1,0:T(8,128)}), f32[4,16,128]{2,1,0:T(8,128)S(1)}, u32[]{:S(2)}, u32[]{:S(2)}) %all-to-all-start.1) | async-done | bytes 32800 | tf_op jit(solution)/shard_map/all_to_all | solution.py:594
  52.5 1.6 %apply.1 = (f32[64,256]{1,0:T(8,128)}, f32[1024,128]{1,0:T(8,128)}) custom-call(f32[4,16,128]{2,1,0:T(8,128)S(1)} %all-to-all-done.1.parts_ref, bf16[2,128,256]{2,1,0:T(8,128)(2,1)S(1)} %get-tuple-element.44.tensor_ref, f32[64,256]{1,0:T(8,128)S(1)} %get-tuple-element.45.base_ref, f32[2,64,128]{2,1,0:T(8,128)S(1)} %get-tuple-element.41.kinds_ref, ...), custom_call_target="tpu_custom_call" | custom-call | tf_op jit(solution)/shard_map/apply/pallas_call | solution.py:602
  (2 shorter events, 0.0 us)
Async XLA Ops:
  0.6 22.4 %copy-start = (f32[32,24,128]{2,1,0:T(8,128)S(1)}, f32[32,24,128]{2,1,0:T(8,128)}, u32[]{:S(2)}) copy-start(f32[32,24,128]{2,1,0:T(8,128)} %param.10) | copy-start | bytes 1179652
  2.1 26.9 %collective-permute-start.4 = (f32[1024,128]{1,0:T(8,128)S(1)}, f32[1024,128]{1,0:T(8,128)S(1)}, u32[]{:S(2)}, u32[]{:S(2)}) collective-permute-start(f32[1024,128]{1,0:T(8,128)S(1)} %get-tuple-element.33), channel_id=1, source_target_pairs={{0,15},{1,0},{2,1},{3,2},{4,3},{5,4},{6,5},{7,6},{8,7},{9,8},{10,9... | collective-permute-start | bytes 1572872 | tf_op jit(solution)/shard_map/ppermute | solution.py:34
  10.6 12.5 %collective-permute-start = (f32[408,128]{1,0:T(8,128)S(1)}, f32[408,128]{1,0:T(8,128)S(1)}, u32[]{:S(2)}, u32[]{:S(2)}) collective-permute-start(f32[408,128]{1,0:T(8,128)S(1)} %get-tuple-element.26), channel_id=1, source_target_pairs={{0,112},{16,0},{32,16},{48,32},{64,48},{80,64},{96,80},{112,96},{1... | collective-permute-start | bytes 626696 | tf_op jit(solution)/shard_map/ppermute | solution.py:34
  16.0 7.1 %collective-permute-start.1 = (f32[48,128]{1,0:T(8,128)S(1)}, f32[48,128]{1,0:T(8,128)S(1)}, u32[]{:S(2)}, u32[]{:S(2)}) collective-permute-start(f32[48,128]{1,0:T(8,128)S(1)} %get-tuple-element.27), channel_id=1, source_target_pairs={{0,16},{16,32},{32,48},{48,64},{64,80},{80,96},{96,112},{112,0},{1... | collective-permute-start | bytes 73736 | tf_op jit(solution)/shard_map/ppermute | solution.py:34
  17.9 8.6 %collective-permute-start.5 = (f32[384,128]{1,0:T(8,128)S(1)}, f32[384,128]{1,0:T(8,128)S(1)}, u32[]{:S(2)}, u32[]{:S(2)}) collective-permute-start(f32[384,128]{1,0:T(8,128)S(1)} %get-tuple-element.36), channel_id=1, source_target_pairs={{0,112},{16,0},{32,16},{48,32},{64,48},{80,64},{96,80},{112,96},{1... | collective-permute-start | bytes 589832 | tf_op jit(solution)/shard_map/ppermute | solution.py:34
  23.2 5.8 %collective-permute-start.2 = (f32[408,128]{1,0:T(8,128)S(1)}, f32[408,128]{1,0:T(8,128)S(1)}, u32[]{:S(2)}, u32[]{:S(2)}) collective-permute-start(f32[408,128]{1,0:T(8,128)S(1)} %get-tuple-element.28), channel_id=1, source_target_pairs={{0,15},{1,0},{2,1},{3,2},{4,3},{5,4},{6,5},{7,6},{8,7},{9,8},{10,9... | collective-permute-start | bytes 626696 | tf_op jit(solution)/shard_map/ppermute | solution.py:34
  23.2 5.8 %collective-permute-start.3 = (f32[112,128]{1,0:T(8,128)S(1)}, f32[112,128]{1,0:T(8,128)S(1)}, u32[]{:S(2)}, u32[]{:S(2)}) collective-permute-start(f32[112,128]{1,0:T(8,128)S(1)} %get-tuple-element.29), channel_id=1, source_target_pairs={{0,1},{1,2},{2,3},{3,4},{4,5},{5,6},{6,7},{7,8},{8,9},{9,10},{10,1... | collective-permute-start | bytes 172040 | tf_op jit(solution)/shard_map/ppermute | solution.py:34
  26.5 12.5 %collective-permute-start.6 = (f32[240,128]{1,0:T(8,128)S(1)}, f32[240,128]{1,0:T(8,128)S(1)}, u32[]{:S(2)}, u32[]{:S(2)}) collective-permute-start(f32[240,128]{1,0:T(8,128)S(1)} %corner.1), channel_id=1, source_target_pairs={{0,15},{1,0},{2,1},{3,2},{4,3},{5,4},{6,5},{7,6},{8,7},{9,8},{10,9... | collective-permute-start | bytes 368648 | tf_op jit(solution)/shard_map/ppermute | solution.py:34
  30.0 9.3 %all-to-all-start = ((f32[4,56,128]{2,1,0:T(8,128)}), f32[4,56,128]{2,1,0:T(8,128)S(1)}, u32[]{:S(2)}, u32[]{:S(2)}) async-start(f32[4,56,128]{2,1,0:T(8,128)} %get-tuple-element.39), calls=%async_computation | async-start | bytes 229376 | tf_op jit(solution)/shard_map/all_to_all | solution.py:549
  43.5 5.1 %copy-start.4 = (f32[2,25,256]{2,0,1:T(2,128)S(1)}, f32[2,25,256]{2,0,1:T(2,128)}, u32[]{:S(2)}) copy-start(f32[2,25,256]{2,0,1:T(2,128)} %param.16) | copy-start | bytes 153604
  43.5 9.1 %all-to-all-start.1 = ((f32[4,16,128]{2,1,0:T(8,128)}), f32[4,16,128]{2,1,0:T(8,128)S(1)}, u32[]{:S(2)}, u32[]{:S(2)}) async-start(f32[4,16,128]{2,1,0:T(8,128)} %get-tuple-element.43.after_ref), calls=%async_computation.1 | async-start | bytes 65536 | tf_op jit(solution)/shard_map/all_to_all | solution.py:594
  48.6 1.1 %copy-start.1 = (f32[2,256,256]{2,1,0:T(8,128)S(1)}, f32[2,256,256]{2,1,0:T(8,128)}, u32[]{:S(2)}) copy-start(f32[2,256,256]{2,1,0:T(8,128)} %coulomb_ref.1) | copy-start | bytes 1572868
  48.6 1.3 %copy-start.2 = (f32[64,16,128]{2,1,0:T(8,128)S(1)}, f32[64,16,128]{2,1,0:T(8,128)}, u32[]{:S(2)}) copy-start(f32[64,16,128]{2,1,0:T(8,128)} %param.19) | copy-start | bytes 1572868
  48.6 1.3 %copy-start.3 = (f32[64,256]{1,0:T(8,128)S(1)}, f32[64,256]{1,0:T(8,128)}, u32[]{:S(2)}) copy-start(f32[64,256]{1,0:T(8,128)} %rho_ref.1) | copy-start | bytes 196612

commit v6 on v5

--- a/solution.py
+++ b/solution.py
@@ -91,7 +91,7 @@
         copy.wait()
 
 
-def widen_kernel(dens_ref, above_ref, below_ref, ed_ref, side_ref, up_ref):
+def widen_kernel(dens_ref, above_ref, below_ref, ed_ref, side_ref, up_ref, sides):
     def plane(ref, x):
         return ref[pl.ds(x * CY, CY), :]
 
@@ -104,7 +104,8 @@
         ed_ref[pl.ds(s, CY, stride=XD), :] = plane(dens_ref, x) if 0 <= x < CX else halo.get(x, ones)
     for k in range(24):
         value = halo[CX + k] if k < DUP else halo.get(k - DUP - LOW, ones)
-        side_ref[pl.ds(k, DUP, stride=24), :] = value[:DUP]
+        sides[pl.ds(k, CY, stride=24), :] = value
+    side_ref[...] = sides[: DUP * 24]
     up_ref[...] = ed_ref[(CY - LOW) * XD :]
 
 
@@ -307,7 +308,7 @@
     field, part_ref,
     cells, windows, fixes, sem,
 ):
-    copy = pltpu.make_async_copy(cells_ref, cells, sem)
+    copy = pltpu.make_async_copy(cells_ref, cells.at[pl.ds(0, NL * 64)], sem)
     copy.start()
     place = lax.broadcasted_iota(jnp.int32, (XD, 256), 1) % 4
     middle = (place == 1) | (place == 2)
@@ -514,6 +515,7 @@
         "widen",
         (shape(CY * XD, CZ), shape(DUP * 24, CZ), shape(LOW * XD, CZ)),
         vmem(3),
+        [pltpu.VMEM((CY * 24, CZ), F32)],
     )(dens_rows, above, below)
     side_above = shifted(side, "dyz", -1)
     from_down = shifted(send_up, "dyz", 1)
@@ -541,7 +543,7 @@
         out_shape=(shape(XD, 256), pltpu.HBM((4, XD, 128), F32)),
         in_specs=vmem(4),
         out_specs=tuple(vmem(1) + hbm(1)),
-        scratch_shapes=[pltpu.VMEM((DUP * XD, CZ), F32), pltpu.VMEM((4, XD, 128), F32), pltpu.SemaphoreType.DMA(())],
+        scratch_shapes=[pltpu.VMEM((DUP * XD + 8, CZ), F32), pltpu.VMEM((4, XD, 128), F32), pltpu.SemaphoreType.DMA(())],
         compiler_params=PARAMS,
         name="ends",
     )(close(own_ends), close(lines_above), close(side_above), close(from_down))
@@ -558,7 +560,7 @@
         ),
         in_specs=smem(1) + vmem(5) + hbm(3),
         out_specs=tuple(vmem(2) + smem(1) + vmem(1)),
-        scratch_shapes=[pltpu.VMEM((n * XD, CZ), F32) for n in (4, 3, 4, 19, 19, 19)]
+        scratch_shapes=[pltpu.VMEM((n * XD, CZ), F32) for n in (4, 3, 4, 20, 20, 20)]
         + [
             pltpu.SMEM((3, 64), jnp.int32),
             pltpu.VMEM((3, 64), jnp.int32),
@@ -580,7 +582,7 @@
         (pltpu.VMEM((YH * XH, CZ), F32), pltpu.VMEM((4, 16, 128), F32)),
         smem(1) + hbm(1) + vmem(8),
         [
-            pltpu.VMEM((NL * 64, 128), F32),
+            pltpu.VMEM((32 * 64, 128), F32),
             pltpu.VMEM((2 * 16 * 64, 128), F32),
             pltpu.VMEM((XD, 256), F32),
             pltpu.SemaphoreType.DMA(()),

time: 54.5 us -> 54.3 us (level)
  transfers between devices with their start and end apart: 9 -> 9, of which waited for: 2 -> 2; matrix products, arithmetic and copies ran while one was open for 0% -> 0% of each run, Pallas kernels for 16% -> 15%
where the time goes in v6:
time: 54.3 us; the launch traced here: 53.8 us
  starting transfers between devices  33.6 us (62%)
  Pallas kernels  15.4 us (28%)
  waiting for transfers between devices  2.86 us (5%)
  between operations  1.47 us (3%)
    ppermute x7, starting transfers between devices, shifted(): lax.ppermute(block, axis, [(i, (i + distance) % n) for i in range(n)])  23.9 us
    all_to_all x1, starting transfers between devices, local(): summed = lax.all_to_all(parts, 'band', 0, 0)  4.84 us
    all_to_all x1, starting transfers between devices, local(): beside = lax.all_to_all(send_ends, 'band', 0, 0)  4.84 us
    pallas_call x1, Pallas kernels, local(): call(field_kernel, 'field', (pltpu.VMEM((YH * XH, CZ), F32), pltpu.VMEM((...  4.12 us
    pallas_call x1, Pallas kernels, local(): pl.pallas_call(outer_kernel, out_shape=(shape(19 * XH, CZ), shape(4, XD,...  3.24 us
    pallas_call x1, Pallas kernels, local(): call(inner_kernel, 'inner', (shape(20 * XH, CZ), shape(10 * XD, CZ), shap...  2.76 us
    all_to_all x1, waiting for transfers between devices, local(): summed = lax.all_to_all(parts, 'band', 0, 0)  2.32 us
    pallas_call x1, Pallas kernels, local(): pl.pallas_call(apply_kernel, out_shape=(pltpu.HBM((64, 256), F32), pltpu....  1.62 us
  transfers between devices with their start and end apart: 9, of which 2 were waited for; matrix products, arithmetic and copies ran while one was open for 0% of the time, Pallas kernels for 15%

profile of v6, /device:TPU:2, one launch (start us, length us, event | category | flops | bytes accessed | tf_op | source)
XLA Modules:
  0.0 53.8 jit_solution(6032123424905551308)
XLA Ops:
  0.6 0.0 copy-start
  0.6 1.4 %lift.1 = (f32[408,128]{1,0:T(8,128)S(1)}, f32[48,128]{1,0:T(8,128)S(1)}, f32[1024,128]{1,0:T(8,128)S(1)}, f32[384,128]{1,0:T(8,128)S(1)}) custom-call(f32[768,128]{1,0:T(8,128)} %bitcast.13, f32[768,128]{1,0:T(8,128)} %bitcast.16), custom_call_target="tpu_custom_call" | custom-call | tf_op jit(solution)/shard_map/lift/pallas_call | solution.py:501
  2.1 8.5 %collective-permute-start.4 = (f32[1024,128]{1,0:T(8,128)S(1)}, f32[1024,128]{1,0:T(8,128)S(1)}, u32[]{:S(2)}, u32[]{:S(2)}) collective-permute-start(f32[1024,128]{1,0:T(8,128)S(1)} %get-tuple-element.33), channel_id=1, source_target_pairs={{0,15},{1,0},{2,1},{3,2},{4,3},{5,4},{6,5},{7,6},{8,7},{9,8},{10,9... | collective-permute-start | bytes 1572872 | tf_op jit(solution)/shard_map/ppermute | solution.py:34
  10.6 5.4 %collective-permute-start = (f32[408,128]{1,0:T(8,128)S(1)}, f32[408,128]{1,0:T(8,128)S(1)}, u32[]{:S(2)}, u32[]{:S(2)}) collective-permute-start(f32[408,128]{1,0:T(8,128)S(1)} %get-tuple-element.26), channel_id=1, source_target_pairs={{0,112},{16,0},{32,16},{48,32},{64,48},{80,64},{96,80},{112,96},{1... | collective-permute-start | bytes 626696 | tf_op jit(solution)/shard_map/ppermute | solution.py:34
  16.0 1.9 %collective-permute-start.1 = (f32[48,128]{1,0:T(8,128)S(1)}, f32[48,128]{1,0:T(8,128)S(1)}, u32[]{:S(2)}, u32[]{:S(2)}) collective-permute-start(f32[48,128]{1,0:T(8,128)S(1)} %get-tuple-element.27), channel_id=1, source_target_pairs={{0,16},{16,32},{32,48},{48,64},{64,80},{80,96},{96,112},{112,0},{1... | collective-permute-start | bytes 73736 | tf_op jit(solution)/shard_map/ppermute | solution.py:34
  17.9 5.1 %collective-permute-start.5 = (f32[384,128]{1,0:T(8,128)S(1)}, f32[384,128]{1,0:T(8,128)S(1)}, u32[]{:S(2)}, u32[]{:S(2)}) collective-permute-start(f32[384,128]{1,0:T(8,128)S(1)} %get-tuple-element.36), channel_id=1, source_target_pairs={{0,112},{16,0},{32,16},{48,32},{64,48},{80,64},{96,80},{112,96},{1... | collective-permute-start | bytes 589832 | tf_op jit(solution)/shard_map/ppermute | solution.py:34
  23.0 0.0 collective-permute-done.1.below_ref
  23.0 0.0 collective-permute-done.above_ref
  23.0 0.0 copy-done
  23.1 0.2 widen.1
  23.2 0.0 collective-permute-start.2
  23.2 0.5 collective-permute-start.3
  23.7 2.8 %inner.1 = (f32[960,128]{1,0:T(8,128)S(1)}, f32[560,128]{1,0:T(8,128)S(1)}, f32[56,256]{1,0:T(8,128)S(1)}) custom-call(f32[1344,128]{1,0:T(8,128)S(1)} %get-tuple-element.30.ed_ref, f32[768,128]{1,0:T(8,128)} %bitcast.17), custom_call_target="tpu_custom_call" | custom-call | tf_op jit(solution)/shard_map/inner/pallas_call | solution.py:523
  26.5 0.0 collective-permute-done.5.rim_ref
  26.5 2.5 %collective-permute-start.6 = (f32[240,128]{1,0:T(8,128)S(1)}, f32[240,128]{1,0:T(8,128)S(1)}, u32[]{:S(2)}, u32[]{:S(2)}) collective-permute-start(f32[240,128]{1,0:T(8,128)S(1)} %corner.1), channel_id=1, source_target_pairs={{0,15},{1,0},{2,1},{3,2},{4,3},{5,4},{6,5},{7,6},{8,7},{9,8},{10,9... | collective-permute-start | bytes 368648 | tf_op jit(solution)/shard_map/ppermute | solution.py:34
  29.0 0.0 collective-permute-done.3.up_ref
  29.0 0.0 collective-permute-done.2.side_ref
  29.0 0.0 collective-permute-done.4.lines_ref
  29.0 0.9 %ends.1 = (f32[56,256]{1,0:T(8,128)S(1)}, f32[4,56,128]{2,1,0:T(8,128)}) custom-call(f32[56,256]{1,0:T(8,128)S(1)} %get-tuple-element.32.own_ref.after_ref, f32[1024,128]{1,0:T(8,128)S(1)} %collective-permute-done.4.lines_ref, f32[408,128]{1,0:T(8,128)S(1)} %collective-permute-done.2.side_ref, f32[112,128]{1,0:T(8,128)S(1)} %collective-permute-done.3.up_ref), custom_call_target="tpu_custom_call" | custom-call | tf_op jit(solution)/shard_map/ends/pallas_call | solution.py:541
  30.0 4.8 %all-to-all-start = ((f32[4,56,128]{2,1,0:T(8,128)}), f32[4,56,128]{2,1,0:T(8,128)S(1)}, u32[]{:S(2)}, u32[]{:S(2)}) async-start(f32[4,56,128]{2,1,0:T(8,128)} %get-tuple-element.39), calls=%async_computation | async-start | bytes 229376 | tf_op jit(solution)/shard_map/all_to_all | solution.py:551
  35.5 3.2 %outer.1 = (f32[912,128]{1,0:T(8,128)S(1)}, f32[4,56,256]{2,1,0:T(8,128)S(1)}, s32[66]{0:T(128)S(1)}, f32[2,64,128]{2,1,0:T(8,128)S(1)}) custom-call(s32[1]{0:T(128)S(6)} %copy.15.count_ref, f32[408,128]{1,0:T(8,128)S(1)} %collective-permute-done.2.side_ref, f32[112,128]{1,0:T(8,128)S(1)} %collective-permute-done.3.up_ref, ...), custom_call_target="tpu_custom_call" | custom-call | tf_op jit(solution)/shard_map/outer/pallas_call | solution.py:553
  38.7 0.0 collective-permute-done.6.corner_ref
  38.7 0.5 all-to-all-done.beside_ref
  39.2 4.1 %field.1 = (f32[1872,128]{1,0:T(8,128)S(1)}, f32[4,16,128]{2,1,0:T(8,128)}) custom-call(s32[66]{0:T(128)S(1)} %get-tuple-element.35.plan_ref, f32[1600,128]{1,0:T(8,128)} %bitcast.19, f32[384,128]{1,0:T(8,128)S(1)} %collective-permute-done.5.rim_ref, f32[240,128]{1,0:T(8,128)S(1)} %collective-permute-done.6.corner_ref, ...), custom_call_target="tpu_custom_call" | custom-call | tf_op jit(solution)/shard_map/field/pallas_call | solution.py:579
  43.4 0.0 copy-start.4
  43.4 4.8 %all-to-all-start.1 = ((f32[4,16,128]{2,1,0:T(8,128)}), f32[4,16,128]{2,1,0:T(8,128)S(1)}, u32[]{:S(2)}, u32[]{:S(2)}) async-start(f32[4,16,128]{2,1,0:T(8,128)} %get-tuple-element.43.after_ref), calls=%async_computation.1 | async-start | bytes 65536 | tf_op jit(solution)/shard_map/all_to_all | solution.py:596
  48.2 0.0 copy-done.4
  48.2 0.0 copy-start.1
  48.2 0.0 copy-start.2
  48.3 0.0 copy-start.3
  48.3 0.8 %own.1 = f32[768,128]{1,0:T(8,128)} custom-call(f32[1872,128]{1,0:T(8,128)S(1)} %get-tuple-element.42.field_ref), custom_call_target="tpu_custom_call" | custom-call | tf_op jit(solution)/shard_map/own/pallas_call | solution.py:597
  49.1 0.3 copy-done.1
  49.4 0.2 copy-done.2
  49.6 0.0 copy-done.3
  49.6 0.3 base.1
  49.9 2.3 %all-to-all-done.1.parts_ref = f32[4,16,128]{2,1,0:T(8,128)S(1)} async-done(((f32[4,16,128]{2,1,0:T(8,128)}), f32[4,16,128]{2,1,0:T(8,128)S(1)}, u32[]{:S(2)}, u32[]{:S(2)}) %all-to-all-start.1) | async-done | bytes 32800 | tf_op jit(solution)/shard_map/all_to_all | solution.py:596
  52.2 1.6 %apply.1 = (f32[64,256]{1,0:T(8,128)}, f32[1024,128]{1,0:T(8,128)}) custom-call(f32[4,16,128]{2,1,0:T(8,128)S(1)} %all-to-all-done.1.parts_ref, bf16[2,128,256]{2,1,0:T(8,128)(2,1)S(1)} %get-tuple-element.44.tensor_ref, f32[64,256]{1,0:T(8,128)S(1)} %get-tuple-element.45.base_ref, f32[2,64,128]{2,1,0:T(8,128)S(1)} %get-tuple-element.41.kinds_ref, ...), custom_call_target="tpu_custom_call" | custom-call | tf_op jit(solution)/shard_map/apply/pallas_call | solution.py:604
  (2 shorter events, 0.0 us)
Async XLA Ops:
  0.6 22.4 %copy-start = (f32[32,24,128]{2,1,0:T(8,128)S(1)}, f32[32,24,128]{2,1,0:T(8,128)}, u32[]{:S(2)}) copy-start(f32[32,24,128]{2,1,0:T(8,128)} %param.10) | copy-start | bytes 1179652
  2.1 26.9 %collective-permute-start.4 = (f32[1024,128]{1,0:T(8,128)S(1)}, f32[1024,128]{1,0:T(8,128)S(1)}, u32[]{:S(2)}, u32[]{:S(2)}) collective-permute-start(f32[1024,128]{1,0:T(8,128)S(1)} %get-tuple-element.33), channel_id=1, source_target_pairs={{0,15},{1,0},{2,1},{3,2},{4,3},{5,4},{6,5},{7,6},{8,7},{9,8},{10,9... | collective-permute-start | bytes 1572872 | tf_op jit(solution)/shard_map/ppermute | solution.py:34
  10.6 12.5 %collective-permute-start = (f32[408,128]{1,0:T(8,128)S(1)}, f32[408,128]{1,0:T(8,128)S(1)}, u32[]{:S(2)}, u32[]{:S(2)}) collective-permute-start(f32[408,128]{1,0:T(8,128)S(1)} %get-tuple-element.26), channel_id=1, source_target_pairs={{0,112},{16,0},{32,16},{48,32},{64,48},{80,64},{96,80},{112,96},{1... | collective-permute-start | bytes 626696 | tf_op jit(solution)/shard_map/ppermute | solution.py:34
  16.0 7.1 %collective-permute-start.1 = (f32[48,128]{1,0:T(8,128)S(1)}, f32[48,128]{1,0:T(8,128)S(1)}, u32[]{:S(2)}, u32[]{:S(2)}) collective-permute-start(f32[48,128]{1,0:T(8,128)S(1)} %get-tuple-element.27), channel_id=1, source_target_pairs={{0,16},{16,32},{32,48},{48,64},{64,80},{80,96},{96,112},{112,0},{1... | collective-permute-start | bytes 73736 | tf_op jit(solution)/shard_map/ppermute | solution.py:34
  17.9 8.6 %collective-permute-start.5 = (f32[384,128]{1,0:T(8,128)S(1)}, f32[384,128]{1,0:T(8,128)S(1)}, u32[]{:S(2)}, u32[]{:S(2)}) collective-permute-start(f32[384,128]{1,0:T(8,128)S(1)} %get-tuple-element.36), channel_id=1, source_target_pairs={{0,112},{16,0},{32,16},{48,32},{64,48},{80,64},{96,80},{112,96},{1... | collective-permute-start | bytes 589832 | tf_op jit(solution)/shard_map/ppermute | solution.py:34
  23.2 5.8 %collective-permute-start.2 = (f32[408,128]{1,0:T(8,128)S(1)}, f32[408,128]{1,0:T(8,128)S(1)}, u32[]{:S(2)}, u32[]{:S(2)}) collective-permute-start(f32[408,128]{1,0:T(8,128)S(1)} %get-tuple-element.28), channel_id=1, source_target_pairs={{0,15},{1,0},{2,1},{3,2},{4,3},{5,4},{6,5},{7,6},{8,7},{9,8},{10,9... | collective-permute-start | bytes 626696 | tf_op jit(solution)/shard_map/ppermute | solution.py:34
  23.2 5.8 %collective-permute-start.3 = (f32[112,128]{1,0:T(8,128)S(1)}, f32[112,128]{1,0:T(8,128)S(1)}, u32[]{:S(2)}, u32[]{:S(2)}) collective-permute-start(f32[112,128]{1,0:T(8,128)S(1)} %get-tuple-element.29), channel_id=1, source_target_pairs={{0,1},{1,2},{2,3},{3,4},{4,5},{5,6},{6,7},{7,8},{8,9},{9,10},{10,1... | collective-permute-start | bytes 172040 | tf_op jit(solution)/shard_map/ppermute | solution.py:34
  26.5 12.2 %collective-permute-start.6 = (f32[240,128]{1,0:T(8,128)S(1)}, f32[240,128]{1,0:T(8,128)S(1)}, u32[]{:S(2)}, u32[]{:S(2)}) collective-permute-start(f32[240,128]{1,0:T(8,128)S(1)} %corner.1), channel_id=1, source_target_pairs={{0,15},{1,0},{2,1},{3,2},{4,3},{5,4},{6,5},{7,6},{8,7},{9,8},{10,9... | collective-permute-start | bytes 368648 | tf_op jit(solution)/shard_map/ppermute | solution.py:34
  30.0 9.3 %all-to-all-start = ((f32[4,56,128]{2,1,0:T(8,128)}), f32[4,56,128]{2,1,0:T(8,128)S(1)}, u32[]{:S(2)}, u32[]{:S(2)}) async-start(f32[4,56,128]{2,1,0:T(8,128)} %get-tuple-element.39), calls=%async_computation | async-start | bytes 229376 | tf_op jit(solution)/shard_map/all_to_all | solution.py:551
  43.4 4.9 %copy-start.4 = (f32[2,25,256]{2,0,1:T(2,128)S(1)}, f32[2,25,256]{2,0,1:T(2,128)}, u32[]{:S(2)}) copy-start(f32[2,25,256]{2,0,1:T(2,128)} %param.16) | copy-start | bytes 153604
  43.4 8.8 %all-to-all-start.1 = ((f32[4,16,128]{2,1,0:T(8,128)}), f32[4,16,128]{2,1,0:T(8,128)S(1)}, u32[]{:S(2)}, u32[]{:S(2)}) async-start(f32[4,16,128]{2,1,0:T(8,128)} %get-tuple-element.43.after_ref), calls=%async_computation.1 | async-start | bytes 65536 | tf_op jit(solution)/shard_map/all_to_all | solution.py:596
  48.2 1.1 %copy-start.1 = (f32[2,256,256]{2,1,0:T(8,128)S(1)}, f32[2,256,256]{2,1,0:T(8,128)}, u32[]{:S(2)}) copy-start(f32[2,256,256]{2,1,0:T(8,128)} %coulomb_ref.1) | copy-start | bytes 1572868
  48.2 1.3 %copy-start.2 = (f32[64,16,128]{2,1,0:T(8,128)S(1)}, f32[64,16,128]{2,1,0:T(8,128)}, u32[]{:S(2)}) copy-start(f32[64,16,128]{2,1,0:T(8,128)} %param.19) | copy-start | bytes 1572868
  48.3 1.3 %copy-start.3 = (f32[64,256]{1,0:T(8,128)S(1)}, f32[64,256]{1,0:T(8,128)}, u32[]{:S(2)}) copy-start(f32[64,256]{1,0:T(8,128)} %rho_ref.1) | copy-start | bytes 196612
